TPU v7x, 512 devices: a whole 4x4x16 slice. The times are simulated.
512 devices in a mesh: row: 32 (over z_lo, x, core), col: 16 (over y, z_hi).
Axes of the slice: x: 4, y: 4, z: 16 (z_hi: 4, z_lo: 4; z = z_hi * 4 + z_lo), core: 2. Of those that a mesh axis runs over, the one named last changes fastest.
Arguments:
- features: bfloat16 [131072, 128], P(('row', 'col')), may hold values from -6 to 6
- weight: bfloat16 [128, 128], replicated, may hold values from -0.5 to 0.5
- bias: float32 [128], replicated, may hold values from -3 to 3
- node_scale: float32 [131072], P(('row', 'col')), may hold values from 0.04 to 0.2
- cotangent: bfloat16 [131072, 128], P(('row', 'col')), may hold values from -6 to 6
- tile_row: int32 [32, 16, 8], P('row', 'col'), may hold values from 0 to 15
- tile_col: int32 [32, 16, 8], P('row', 'col'), may hold values from 0 to 31
- tile_count: int32 [32, 16], P('row', 'col'), may hold values from 1 to 8, as said below
- tile_values: bfloat16 [32, 16, 8, 256, 256], P('row', 'col'), may hold values from 0 to 1
Outputs:
- activated: bfloat16 [131072, 128], P(('row', 'col'))
- feature_grad: bfloat16 [131072, 128], P(('row', 'col'))
- weight_grad: float32 [128, 128], replicated
- bias_grad: float32 [128], replicated
Inputs may be any that keep to these rules, and one draw needn't show every extreme that they name: `tile_count`: slots from this count on are ignored; in every draw some device has exactly 8 live slots.
All inputs are finite; a program needn't handle non-finite values.
Results may differ from a plain program's by a relative error of at most 0.015.
Values may be sent and summed in bfloat16 or wider, within the bound.
No kernel may reach another device: no remote copies, remote signals or barrier semaphores. Data moves between devices by JAX's collectives and lax.ppermute only.
A program may use at most 64 MiB of HBM per device.

v0:
```python
import jax
import jax.numpy as jnp
from jax import lax
from jax.sharding import PartitionSpec as P

BLOCK = 256


def aggregate(blocks, rows_idx, cols_idx, weights, tiles, nbr, nbc):
    n_col = lax.axis_size("col")
    n_row = lax.axis_size("row")
    width = blocks.shape[1]
    x_rows = lax.all_gather(blocks, "col", axis=0, tiled=True).reshape(-1, BLOCK, width)
    x_cols = lax.all_gather(blocks, "row", axis=0, tiled=True).reshape(-1, BLOCK, width)
    row_terms = jnp.einsum(
        "tab,tbf->taf", tiles, x_cols[cols_idx], preferred_element_type=jnp.float32
    )
    col_terms = jnp.einsum(
        "tab,taf->tbf", tiles, x_rows[rows_idx], preferred_element_type=jnp.float32
    )
    row_part = jax.ops.segment_sum(row_terms * weights[:, None, None], rows_idx, num_segments=nbr)
    col_part = jax.ops.segment_sum(col_terms * weights[:, None, None], cols_idx, num_segments=nbc)
    row_in = lax.all_to_all(
        row_part.astype(jnp.bfloat16), "col", split_axis=0, concat_axis=0, tiled=True
    )
    total = jnp.sum(row_in.astype(jnp.float32), axis=0)
    col_in = lax.all_to_all(
        col_part.astype(jnp.bfloat16), "row", split_axis=0, concat_axis=0, tiled=True
    )
    total = total + jnp.sum(col_in.astype(jnp.float32), axis=0)
    return total


def shards(
    features, weight, bias, node_scale, cotangent, tile_row, tile_col, tile_count, tile_values
):
    n_col = lax.axis_size("col")
    n_row = lax.axis_size("row")
    row_pos = lax.axis_index("row")
    col_pos = lax.axis_index("col")
    per_dev = features.shape[0] // BLOCK
    nbr = n_col * per_dev
    nbc = n_row * per_dev
    rows_idx = tile_row[0, 0]
    cols_idx = tile_col[0, 0]
    count = tile_count[0, 0]
    tiles = tile_values[0, 0]
    slots = jnp.arange(rows_idx.shape[0], dtype=jnp.int32)
    glob_i = row_pos * nbr + rows_idx
    glob_j = (cols_idx // per_dev * n_col + col_pos) * per_dev + cols_idx % per_dev
    weights = jnp.where(slots < count, jnp.where(glob_i == glob_j, 0.5, 1.0), 0.0).astype(
        jnp.float32
    )
    scale = node_scale[:, None]
    projected = (scale * jnp.dot(features, weight, preferred_element_type=jnp.float32)).astype(
        jnp.bfloat16
    )
    summed = aggregate(projected, rows_idx, cols_idx, weights, tiles, nbr, nbc)
    preact = scale * (summed + projected.astype(jnp.float32)) + bias[None, :]
    activated = jax.nn.silu(preact).astype(jnp.bfloat16)
    sig = jax.nn.sigmoid(preact)
    delta = cotangent.astype(jnp.float32) * sig * (1.0 + preact * (1.0 - sig))
    scaled_delta = (scale * delta).astype(jnp.bfloat16)
    back = aggregate(scaled_delta, rows_idx, cols_idx, weights, tiles, nbr, nbc)
    proj_grad = (scale * (back + scaled_delta.astype(jnp.float32))).astype(jnp.bfloat16)
    feature_grad = jnp.dot(proj_grad, weight.T, preferred_element_type=jnp.float32).astype(
        jnp.bfloat16
    )
    local_weight = jnp.dot(features.T, proj_grad, preferred_element_type=jnp.float32)
    local_bias = jnp.sum(delta, axis=0)
    weight_grad, bias_grad = lax.psum((local_weight, local_bias), ("row", "col"))
    return (activated, feature_grad, weight_grad, bias_grad)


def solution(mesh):
    placed = (
        P(("row", "col"), None),
        P(),
        P(),
        P(("row", "col")),
        P(("row", "col"), None),
        P("row", "col", None),
        P("row", "col", None),
        P("row", "col"),
        P("row", "col", None, None, None),
    )
    return jax.shard_map(
        shards,
        mesh=mesh,
        in_specs=placed,
        out_specs=(P(("row", "col"), None), P(("row", "col"), None), P(), P()),
        check_vma=False,
    )
```

profile of v0, /device:TPU:1, one launch (start us, length us, event | category | flops | bytes accessed | tf_op | source)
XLA Modules:
  0.0 1041.3 jit_solution(17749433293031500199)
XLA Ops:
  8.1 1.7 fusion.4
  11.8 70.8 %all-gather.5.cloned.1.call-done = bf16[8192,128]{1,0:T(8,128)(2,1)} async-done(((bf16[256,128]{1,0:T(8,128)(2,1)}), bf16[8192,128]{1,0:T(8,128)(2,1)}) %all-gather.5.cloned.1.call-update) | async-done | bytes 2097168 | tf_op jit(solution)/shard_map/all_gather | solution.py:14
  82.6 2.2 gather_fusion
  86.9 2.5 scatter_fusion
  90.5 13.0 %all-to-all-start = ((bf16[16,256,128]{2,1,0:T(8,128)(2,1)}), bf16[16,256,128]{2,1,0:T(8,128)(2,1)S(1)}, u32[]{:S(2)}, u32[]{:S(2)}) async-start(bf16[16,256,128]{2,1,0:T(8,128)(2,1)} %convert_element_type.49), calls=%async_computation | async-start | bytes 2097152 | tf_op jit(solution)/shard_map/all_to_all | solution.py:23
  104.1 99.6 %all-gather.7.cloned.1.call-done = bf16[4096,128]{1,0:T(8,128)(2,1)} async-done(((bf16[256,128]{1,0:T(8,128)(2,1)}), bf16[4096,128]{1,0:T(8,128)(2,1)}) %all-gather.7.cloned.1.call-update) | async-done | bytes 1048592 | tf_op jit(solution)/shard_map/all_gather | solution.py:13
  203.7 1.9 gather_fusion.1
  205.6 1.3 fusion.2
  206.9 1.5 copy.21
  208.4 2.4 broadcast.140.clone
  210.9 3.2 scatter_fusion.1
  214.1 3.8 convert_element_type.51
  218.9 5.7 all-to-all-start.1
  224.7 1.4 convert_reduce_fusion.3
  226.1 46.7 %all-to-all-done.1 = bf16[32,256,128]{2,1,0:T(8,128)(2,1)S(1)} async-done(((bf16[32,256,128]{2,1,0:T(8,128)(2,1)}), bf16[32,256,128]{2,1,0:T(8,128)(2,1)S(1)}, u32[]{:S(2)}, u32[]{:S(2)}) %all-to-all-start.1) | async-done | bytes 2097184 | tf_op jit(solution)/shard_map/all_to_all | solution.py:27
  273.1 1.9 fusion.12
  275.8 60.8 %all-gather.9.cloned.1.call-done = bf16[8192,128]{1,0:T(8,128)(2,1)} async-done(((bf16[256,128]{1,0:T(8,128)(2,1)}), bf16[8192,128]{1,0:T(8,128)(2,1)}) %all-gather.9.cloned.1.call-update) | async-done | bytes 2097168 | tf_op jit(solution)/shard_map/all_gather | solution.py:14
  336.6 2.2 gather_fusion.2
  340.8 2.5 scatter_fusion.2
  344.5 13.0 %all-to-all-start.2 = ((bf16[16,256,128]{2,1,0:T(8,128)(2,1)}), bf16[16,256,128]{2,1,0:T(8,128)(2,1)S(1)}, u32[]{:S(2)}, u32[]{:S(2)}) async-start(bf16[16,256,128]{2,1,0:T(8,128)(2,1)} %convert_element_type.57), calls=%async_computation.2 | async-start | bytes 2097152 | tf_op jit(solution)/shard_map/all_to_all | solution.py:23
  358.0 99.6 %all-gather.11.cloned.1.call-done = bf16[4096,128]{1,0:T(8,128)(2,1)} async-done(((bf16[256,128]{1,0:T(8,128)(2,1)}), bf16[4096,128]{1,0:T(8,128)(2,1)}) %all-gather.11.cloned.1.call-update) | async-done | bytes 1048592 | tf_op jit(solution)/shard_map/all_gather | solution.py:13
  457.6 1.9 gather_fusion.3
  459.5 1.3 fusion
  460.8 1.5 copy.25
  462.4 2.4 broadcast.140
  464.8 3.2 scatter_fusion.3
  468.1 3.8 convert_element_type.59
  472.9 5.7 all-to-all-start.3
  478.7 117.8 %psum.15 = f32[128]{0:T(128)} all-reduce(f32[128]{0:T(128)S(1)} %copy-done.12), channel_id=1, replica_groups=mesh['row'=32,'col'=16] {'row','col'}, use_global_device_ids=true, to_apply=%region_10.11 | all-reduce | flops 128 | bytes 1024 | tf_op jit(solution)/shard_map/psum | solution.py:71
  596.4 1.4 convert_reduce_fusion.2
  599.9 432.2 %all-reduce.2.cloned.1.call-done = f32[128,128]{0,1:T(8,128)} async-done(((f32[128,128]{0,1:T(8,128)}), f32[128,128]{0,1:T(8,128)}) %all-reduce.2.cloned.1.call-update) | async-done | bytes 65552 | tf_op jit(solution)/shard_map/psum | solution.py:71
  1032.1 1.6 copy.26
  (58 shorter events, 14.0 us)
Async XLA Ops:
  8.0 76.8 %copy-start = (bf16[1,1,8,256,256]{4,3,2,1,0:T(8,128)(2,1)S(1)}, bf16[1,1,8,256,256]{4,3,2,1,0:T(8,128)(2,1)}, u32[]{:S(2)}) copy-start(bf16[1,1,8,256,256]{4,3,2,1,0:T(8,128)(2,1)} %param.17) | copy-start | bytes 3145732
  8.0 74.6 %all-gather.5.cloned.1.call-start = ((), (), s32[]{:S(2)}) async-start(), calls=%async_computation.4 | async-start | bytes 2162688 | tf_op jit(solution)/shard_map/all_gather | solution.py:14
  85.3 1.5 copy-start.8
  90.5 127.4 %all-to-all-start = ((bf16[16,256,128]{2,1,0:T(8,128)(2,1)}), bf16[16,256,128]{2,1,0:T(8,128)(2,1)S(1)}, u32[]{:S(2)}, u32[]{:S(2)}) async-start(bf16[16,256,128]{2,1,0:T(8,128)(2,1)} %convert_element_type.49), calls=%async_computation | async-start | bytes 2097152 | tf_op jit(solution)/shard_map/all_to_all | solution.py:23
  103.5 100.2 %all-gather.7.cloned.1.call-start = ((), (), s32[]{:S(2)}) async-start(), calls=%async_computation.5 | async-start | bytes 1114112 | tf_op jit(solution)/shard_map/all_gather | solution.py:13
  208.4 2.4 copy-start.10
  218.0 1.0 copy-start.2
  218.9 53.8 %all-to-all-start.1 = ((bf16[32,256,128]{2,1,0:T(8,128)(2,1)}), bf16[32,256,128]{2,1,0:T(8,128)(2,1)S(1)}, u32[]{:S(2)}, u32[]{:S(2)}) async-start(bf16[32,256,128]{2,1,0:T(8,128)(2,1)} %convert_element_type.51), calls=%async_computation.1 | async-start | bytes 4194304 | tf_op jit(solution)/shard_map/all_to_all | solution.py:27
  224.6 48.4 %copy-start.3 = (bf16[256,128]{1,0:T(8,128)(2,1)S(1)}, bf16[256,128]{1,0:T(8,128)(2,1)}, u32[]{:S(2)}) copy-start(bf16[256,128]{1,0:T(8,128)(2,1)} %fusion.4) | copy-start | bytes 196612
  224.6 48.4 %copy-start.6 = (bf16[256,128]{1,0:T(8,128)(2,1)S(1)}, bf16[256,128]{1,0:T(8,128)(2,1)}, u32[]{:S(2)}) copy-start(bf16[256,128]{1,0:T(8,128)(2,1)} %param.13) | copy-start | bytes 196612
  224.6 48.4 %copy-start.7 = (f32[256]{0:T(256)S(1)}, f32[256]{0:T(256)}, u32[]{:S(2)}) copy-start(f32[256]{0:T(256)} %param.12) | copy-start | bytes 3076
  224.7 111.9 %all-gather.9.cloned.1.call-start = ((), (), s32[]{:S(2)}) async-start(), calls=%async_computation.6 | async-start | bytes 2162688 | tf_op jit(solution)/shard_map/all_gather | solution.py:14
  339.3 1.5 copy-start.9
  344.5 127.4 %all-to-all-start.2 = ((bf16[16,256,128]{2,1,0:T(8,128)(2,1)}), bf16[16,256,128]{2,1,0:T(8,128)(2,1)S(1)}, u32[]{:S(2)}, u32[]{:S(2)}) async-start(bf16[16,256,128]{2,1,0:T(8,128)(2,1)} %convert_element_type.57), calls=%async_computation.2 | async-start | bytes 2097152 | tf_op jit(solution)/shard_map/all_to_all | solution.py:23
  357.4 100.2 %all-gather.11.cloned.1.call-start = ((), (), s32[]{:S(2)}) async-start(), calls=%async_computation.7 | async-start | bytes 1114112 | tf_op jit(solution)/shard_map/all_gather | solution.py:13
  462.4 2.4 copy-start.11
  471.9 6.7 copy-start.12
  471.9 1.0 copy-start.1
  472.9 124.9 %all-to-all-start.3 = ((bf16[32,256,128]{2,1,0:T(8,128)(2,1)}), bf16[32,256,128]{2,1,0:T(8,128)(2,1)S(1)}, u32[]{:S(2)}, u32[]{:S(2)}) async-start(bf16[32,256,128]{2,1,0:T(8,128)(2,1)} %convert_element_type.59), calls=%async_computation.3 | async-start | bytes 4194304 | tf_op jit(solution)/shard_map/all_to_all | solution.py:27
  478.6 119.7 %copy-start.4 = (bf16[256,128]{1,0:T(8,128)(2,1)S(1)}, bf16[256,128]{1,0:T(8,128)(2,1)}, u32[]{:S(2)}) copy-start(bf16[256,128]{1,0:T(8,128)(2,1)} %param.9) | copy-start | bytes 196612
  478.6 120.5 %copy-start.5 = (bf16[128,128]{1,0:T(8,128)(2,1)S(1)}, bf16[128,128]{1,0:T(8,128)(2,1)}, u32[]{:S(2)}) copy-start(bf16[128,128]{1,0:T(8,128)(2,1)} %param.10) | copy-start | bytes 98308
  478.6 553.5 %all-reduce.2.cloned.1.call-start = ((), (), s32[]{:S(2)}) async-start(), calls=%async_computation.8 | async-start | bytes 131072 | tf_op jit(solution)/shard_map/psum | solution.py:71
Sparse Core Ops, SparseCore 0:
  11.6 70.9 all-gather.4
  275.9 60.6 all-gather.8
Sparse Core Ops, SparseCore 1:
  107.6 96.1 all-gather.6
  361.5 96.1 all-gather.10
  599.2 432.9 all-reduce.1
where the time goes:
time: 1040 us
  waiting for transfers between devices  811 us (78%)
  blocking collectives  118 us (11%)
  starting transfers between devices  37.5 us (4%)
  other arithmetic  28.9 us (3%)
  local copies, waits for them, and re-layouts  22.7 us (2%)
  between operations  16.6 us (2%)
    psum x1, waiting for transfers between devices, shards(): lax.psum((local_weight, local_bias), ('row', 'col'))  432 us
    all_gather x2, waiting for transfers between devices, aggregate(): lax.all_gather(blocks, 'col', axis=0, tiled=True).reshape(-1, BLOCK, width)  199 us
    all_gather x2, waiting for transfers between devices, aggregate(): lax.all_gather(blocks, 'row', axis=0, tiled=True).reshape(-1, BLOCK, width)  132 us
    psum x1, blocking collectives, shards(): lax.psum((local_weight, local_bias), ('row', 'col'))  118 us
    all_to_all x2, waiting for transfers between devices, aggregate(): lax.all_to_all(col_part.astype(jnp.bfloat16), 'row', split_axis=0, concat...  46.7 us
    all_to_all x2, starting transfers between devices, aggregate(): lax.all_to_all(row_part.astype(jnp.bfloat16), 'col', split_axis=0, concat...  25.9 us
  transfers between devices with their start and end apart: 9, of which 6 were waited for; matrix products, arithmetic and copies ran while one was open for 3% of the time, Pallas kernels for 0%

commit v1 on v0

v1 whole, which is shorter than its diff:
```python
import jax
import jax.numpy as jnp
from jax import lax
from jax.experimental import pallas as pl
from jax.experimental.pallas import tpu as pltpu
from jax.sharding import PartitionSpec as P

BLOCK = 256
RING = 4
AXES = ("row", "col")


def rank(zl, x, core, y, zh):
    return ((zl * RING + x) * 2 + core) * RING * RING + y * RING + zh


def pairs(step):
    out = []
    for zl in range(RING):
        for x in range(RING):
            for core in range(2):
                for y in range(RING):
                    for zh in range(RING):
                        out.append((rank(zl, x, core, y, zh), rank(*step(zl, x, core, y, zh))))
    return out


def swap_cores(v):
    return lax.ppermute(v, AXES, pairs(lambda zl, x, core, y, zh: (zl, x, 1 - core, y, zh)))


def far_shift(v, k, row_core):
    def step(zl, x, core, y, zh):
        if core == row_core:
            return (zl + k) % RING, x, core, y, zh
        return zl, x, core, y, (zh + k) % RING

    return lax.ppermute(v, AXES, pairs(step))


def near_shift(v, k, row_core):
    def step(zl, x, core, y, zh):
        if core == row_core:
            return zl, (x + k) % RING, core, y, zh
        return zl, x, core, (y + k) % RING, zh

    return lax.ppermute(v, AXES, pairs(step))


def gather(both):
    far = jnp.concatenate([both] + [far_shift(both, k, 0) for k in range(1, RING)], axis=0)
    return jnp.concatenate([far] + [near_shift(far, k, 0) for k in range(1, RING)], axis=0)


def add_up(parts):
    total = parts[0].astype(jnp.float32)
    for part in parts[1:]:
        total = total + part.astype(jnp.float32)
    return total


def scatter_sum(parts):
    n = parts.shape[0] // RING
    near = [parts[k * n : (k + 1) * n] for k in range(RING)]
    near = add_up([near[0]] + [near_shift(near[k], k, 1) for k in range(1, RING)])
    near = near.astype(jnp.bfloat16)
    m = n // RING
    far = [near[k * m : (k + 1) * m] for k in range(RING)]
    return add_up([far[0]] + [far_shift(far[k], k, 1) for k in range(1, RING)])


def tile_kernel(src_ref, dst_ref, weight_ref, gathered_ref, own_ref, other_ref, out_ref, acc_ref):
    acc_ref[...] = jnp.zeros_like(acc_ref)
    slots = own_ref.shape[0]
    for half, tiles_ref in enumerate((own_ref, other_ref)):
        for t in range(slots):
            s = half * slots + t
            term = jnp.dot(
                tiles_ref[t], gathered_ref[src_ref[s]], preferred_element_type=jnp.float32
            )
            acc_ref[dst_ref[s]] += weight_ref[s] * term
    out_ref[...] = acc_ref[...].astype(out_ref.dtype)


def apply_tiles(src, dst, weights, gathered, own, other):
    smem = pl.BlockSpec(memory_space=pltpu.SMEM)
    vmem = pl.BlockSpec(memory_space=pltpu.VMEM)
    return pl.pallas_call(
        tile_kernel,
        out_shape=jax.ShapeDtypeStruct(gathered.shape, jnp.bfloat16),
        in_specs=[smem, smem, smem, vmem, vmem, vmem],
        out_specs=vmem,
        scratch_shapes=[pltpu.VMEM(gathered.shape, jnp.float32)],
        compiler_params=pltpu.CompilerParams(vmem_limit_bytes=32 * 1024 * 1024),
    )(src, dst, weights, gathered, own, other)


def shards(
    features, weight, bias, node_scale, cotangent, tile_row, tile_col, tile_count, tile_values
):
    row_pos = lax.axis_index("row")
    col_pos = lax.axis_index("col")
    core = row_pos % 2
    x = row_pos // 2 % RING
    zl = row_pos // (2 * RING)
    y = col_pos // RING
    zh = col_pos % RING
    n_col = lax.axis_size("col")
    first = core == 0

    rows_idx = tile_row[0, 0]
    cols_idx = tile_col[0, 0]
    tiles = tile_values[0, 0]
    slots = jnp.arange(rows_idx.shape[0], dtype=jnp.int32)
    same = row_pos * n_col + rows_idx == cols_idx * n_col + col_pos
    live = jnp.where(slots < tile_count[0, 0], jnp.where(same, 0.5, 1.0), 0.0)

    scale = node_scale[:, None]
    scaled = (scale * features.astype(jnp.float32)).astype(jnp.bfloat16)

    meta = jnp.stack([rows_idx.astype(jnp.float32), cols_idx.astype(jnp.float32), live])
    meta = jnp.pad(meta, ((0, 13), (0, 120))).astype(jnp.bfloat16)
    sent = swap_cores(jnp.concatenate([scaled, meta], axis=0))
    scaled_other = sent[:BLOCK]
    meta_other = sent[BLOCK : BLOCK + 3, :8]
    turned = jnp.swapaxes(tiles, 1, 2)
    own = jnp.where(first, tiles, turned)
    other = swap_cores(jnp.where(first, turned, tiles))

    rows_all = jnp.concatenate([rows_idx, meta_other[0].astype(jnp.int32)])
    cols_all = jnp.concatenate([cols_idx, meta_other[1].astype(jnp.int32)])
    weights = jnp.concatenate([live, meta_other[2].astype(jnp.float32)])
    foreign = jnp.concatenate([jnp.zeros_like(slots), jnp.ones_like(slots)])
    dx = cols_all // 2 % RING - x
    dzl = cols_all // (2 * RING) - zl
    dcore = (cols_all % 2 != core).astype(jnp.int32)
    dy = rows_all // RING - y
    dzh = rows_all % RING - zh
    from_row = (jnp.mod(-dx, RING) * RING + jnp.mod(-dzl, RING)) * 2 + dcore
    from_col = (jnp.mod(-dy, RING) * RING + jnp.mod(-dzh, RING)) * 2 + foreign
    to_row = (jnp.mod(dx, RING) * RING + jnp.mod(dzl, RING)) * 2 + dcore
    to_col = (jnp.mod(dy, RING) * RING + jnp.mod(dzh, RING)) * 2 + foreign
    src = jnp.where(first, from_row, from_col)
    dst = jnp.where(first, to_col, to_row)

    def aggregate(mine, theirs):
        gathered = gather(jnp.stack([mine, theirs]))
        sums = scatter_sum(apply_tiles(src, dst, weights, gathered, own, other))
        back = swap_cores(sums[1].astype(jnp.bfloat16))
        return sums[0] + back.astype(jnp.float32) + mine.astype(jnp.float32)

    spread = aggregate(scaled, scaled_other).astype(jnp.bfloat16)
    preact = scale * jnp.dot(spread, weight, preferred_element_type=jnp.float32) + bias[None, :]
    sig = jax.nn.sigmoid(preact)
    activated = jax.nn.silu(preact).astype(jnp.bfloat16)
    delta = cotangent.astype(jnp.float32) * sig * (1.0 + preact * (1.0 - sig))
    scaled_delta = (scale * delta).astype(jnp.bfloat16)

    local_weight = jnp.dot(spread.T, scaled_delta, preferred_element_type=jnp.float32)
    local_bias = jnp.sum(delta, axis=0, keepdims=True)
    grads = jnp.concatenate([local_weight, jnp.pad(local_bias, ((0, 7), (0, 0)))], axis=0)
    grads = lax.psum(lax.psum(grads, "row"), "col")

    proj_grad = scale * aggregate(scaled_delta, swap_cores(scaled_delta))
    feature_grad = jnp.dot(
        proj_grad.astype(jnp.bfloat16), weight.T, preferred_element_type=jnp.float32
    ).astype(jnp.bfloat16)
    n = weight.shape[0]
    return (activated, feature_grad, grads[:n], grads[n])


def solution(mesh):
    placed = (
        P(AXES, None),
        P(),
        P(),
        P(AXES),
        P(AXES, None),
        P("row", "col", None),
        P("row", "col", None),
        P("row", "col"),
        P("row", "col", None, None, None),
    )
    return jax.shard_map(
        shards,
        mesh=mesh,
        in_specs=placed,
        out_specs=(P(AXES, None), P(AXES, None), P(), P()),
        check_vma=False,
    )
```

time: 1040 us -> 670 us (0.64); the launches traced: 1040 us -> 659 us
  waiting for transfers between devices: 811 us -> 497 us
  blocking collectives: 118 us -> 0 us
  starting transfers between devices: 37.5 us -> 123 us
  other arithmetic: 28.9 us -> 5.84 us
    all_gather x4 -> x0, waiting for transfers between devices: 331 us -> none  [the longest x2 199 us: aggregate(): lax.all_gather(blocks, 'col', axis=0, tiled=True).reshape(-1, BLOCK, width)]
    ppermute x0 -> x29, starting transfers between devices: none -> 123 us  [the longest x12 58.8 us: far_shift(): return lax.ppermute(v, AXES, pairs(step))]
    psum x1 -> x0, blocking collectives: 118 us -> none  [shards(): lax.psum((local_weight, local_bias), ('row', 'col'))]
    ppermute x0 -> x29, waiting for transfers between devices: none -> 64.2 us  [the longest x12 40.8 us: near_shift(): return lax.ppermute(v, AXES, pairs(step))]
    all_to_all x4 -> x0, waiting for transfers between devices: 46.7 us -> none  [the longest x2 46.7 us: aggregate(): lax.all_to_all(col_part.astype(jnp.bfloat16), 'row', split_axis=0, concat...]
    all_to_all x4 -> x0, starting transfers between devices: 37.3 us -> none  [the longest x2 25.9 us: aggregate(): lax.all_to_all(row_part.astype(jnp.bfloat16), 'col', split_axis=0, concat...]
    scatter-add x4 -> x0, other arithmetic: 11.4 us -> none  [the longest x2 6.49 us: aggregate(): jax.ops.segment_sum(col_terms * weights[:, None, None], cols_idx, num_seg...]
    psum x1 -> x2, waiting for transfers between devices: 432 us -> 433 us  [shards(): grads = lax.psum(lax.psum(grads, 'row'), 'col')]
  transfers between devices with their start and end apart: 9 -> 31, of which waited for: 6 -> 20; matrix products, arithmetic and copies ran while one was open for 3% -> 2% of each run, Pallas kernels for 0% -> 0%
where the time goes in v1:
time: 670 us; the launch traced here: 659 us
  waiting for transfers between devices  497 us (74%)
  starting transfers between devices  123 us (18%)
  between operations  15.4 us (2%)
  local copies, waits for them, and re-layouts  12.5 us (2%)
    psum x2, waiting for transfers between devices, shards(): grads = lax.psum(lax.psum(grads, 'row'), 'col')  433 us
    ppermute x12, starting transfers between devices, far_shift(): return lax.ppermute(v, AXES, pairs(step))  58.8 us
    ppermute x12, starting transfers between devices, near_shift(): return lax.ppermute(v, AXES, pairs(step))  45.9 us
    ppermute x12, waiting for transfers between devices, near_shift(): return lax.ppermute(v, AXES, pairs(step))  40.8 us
    ppermute x12, waiting for transfers between devices, far_shift(): return lax.ppermute(v, AXES, pairs(step))  21.1 us
    ppermute x5, starting transfers between devices, swap_cores(): lax.ppermute(v, AXES, pairs(lambda zl, x, core, y, zh: (zl, x, 1 - core,...  18.7 us
  transfers between devices with their start and end apart: 31, of which 20 were waited for; matrix products, arithmetic and copies ran while one was open for 2% of the time, Pallas kernels for 0%

profile of v1, /device:TPU:1, one launch (start us, length us, event | category | flops | bytes accessed | tf_op | source)
XLA Modules:
  0.0 659.2 jit_solution(17352848485285676019)
XLA Ops:
  10.9 8.8 %collective-permute-start = (bf16[272,128]{1,0:T(8,128)(2,1)S(1)}, bf16[272,128]{1,0:T(8,128)(2,1)S(1)}, u32[]{:S(2)}, u32[]{:S(2)}) collective-permute-start(bf16[272,128]{1,0:T(8,128)(2,1)S(1)} %pad_maximum_fusion.2), channel_id=1, source_target_pairs={{0,16},{1,17},{2,18},{3,19},{4,20},{5,21},{6,22},{7,23},{8,24},{9,... | collective-permute-start | bytes 208904 | tf_op jit(solution)/shard_map/ppermute | solution.py:29
  25.0 3.4 collective-permute-start.1
  28.5 10.6 %collective-permute-start.2 = (bf16[2,256,128]{2,1,0:T(8,128)(2,1)S(1)}, bf16[2,256,128]{2,1,0:T(8,128)(2,1)S(1)}, u32[]{:S(2)}, u32[]{:S(2)}) collective-permute-start(bf16[2,256,128]{2,1,0:T(8,128)(2,1)S(1)} %pad_maximum_fusion), channel_id=1, source_target_pairs={{0,256},{1,257},{2,258},{3,259},{4,260},{5,261},{6,262},{7,263},{8... | collective-permute-start | bytes 393224 | tf_op jit(solution)/shard_map/ppermute | solution.py:38
  39.1 5.2 collective-permute-start.3
  45.7 4.6 collective-permute-done.2
  53.8 3.2 collective-permute-start.4
  57.0 4.5 collective-permute-start.5
  61.6 3.0 collective-permute-start.6
  66.0 6.0 collective-permute-done.5
  72.8 4.8 collective-permute-done.6
  81.8 4.5 collective-permute-start.10
  92.0 6.0 collective-permute-done.10
  98.1 5.3 collective-permute-done.8
  105.6 4.9 collective-permute-start.12
  110.5 3.4 collective-permute-start.11
  114.6 7.2 %collective-permute-done.11 = bf16[2,256,128]{2,1,0:T(8,128)(2,1)S(1)} collective-permute-done((bf16[2,256,128]{2,1,0:T(8,128)(2,1)S(1)}, bf16[2,256,128]{2,1,0:T(8,128)(2,1)S(1)}, u32[]{:S(2)}, u32[]{:S(2)}) %collective-permute-start.11) | collective-permute-done | bytes 131104 | tf_op jit(solution)/shard_map/ppermute | solution.py:38
  129.3 3.1 collective-permute-start.16
  132.4 5.9 collective-permute-start.17
  138.3 5.9 collective-permute-start.18
  144.2 6.2 collective-permute-done.17
  151.0 10.1 %collective-permute-start.19 = (bf16[8,256,128]{2,1,0:T(8,128)(2,1)S(1)}, bf16[8,256,128]{2,1,0:T(8,128)(2,1)S(1)}, u32[]{:S(2)}, u32[]{:S(2)}) collective-permute-start(bf16[8,256,128]{2,1,0:T(8,128)(2,1)S(1)} %get-tuple-element.29), channel_id=1, source_target_pairs={{0,32},{1,33},{2,34},{3,35},{4,36},{5,37},{6,38},{7,39},{8,40},{9,... | collective-permute-start | bytes 1572872 | tf_op jit(solution)/shard_map/ppermute | solution.py:47
  163.8 4.0 collective-permute-start.21
  167.9 6.2 collective-permute-done.20
  179.6 4.3 collective-permute-start.23
  187.7 3.4 collective-permute-done.23
  191.1 5.5 collective-permute-done.22
  197.0 5.8 collective-permute-start.27
  202.8 5.4 collective-permute-start.26
  208.1 3.4 collective-permute-start.25
  212.2 250.5 %all-reduce.5.cloned.1.call-done = f32[136,128]{1,0:T(8,128)} async-done(((f32[136,128]{1,0:T(8,128)}), f32[136,128]{1,0:T(8,128)}) %all-reduce.5.cloned.1.call-update) | async-done | bytes 69648 | tf_op jit(solution)/shard_map/psum | solution.py:162
  462.9 4.0 collective-permute-start.28
  466.9 182.0 %all-reduce.7.cloned.1.call-done = f32[136,128]{1,0:T(8,128)} async-done(((f32[136,128]{1,0:T(8,128)}), f32[136,128]{1,0:T(8,128)}) %all-reduce.7.cloned.1.call-update) | async-done | bytes 69648 | tf_op jit(solution)/shard_map/psum | solution.py:162
  (101 shorter events, 52.8 us)
Async XLA Ops:
  7.2 117.9 %copy-start = (bf16[128,128]{1,0:T(8,128)(2,1)S(1)}, bf16[128,128]{1,0:T(8,128)(2,1)}, u32[]{:S(2)}) copy-start(bf16[128,128]{1,0:T(8,128)(2,1)} %param.10) | copy-start | bytes 98308
  7.2 455.5 %all-reduce.5.cloned.1.call-start = ((), (), s32[]{:S(2)}) async-start(), calls=%async_computation | async-start | bytes 139264 | tf_op jit(solution)/shard_map/psum | solution.py:162
  10.9 14.1 %collective-permute-start = (bf16[272,128]{1,0:T(8,128)(2,1)S(1)}, bf16[272,128]{1,0:T(8,128)(2,1)S(1)}, u32[]{:S(2)}, u32[]{:S(2)}) collective-permute-start(bf16[272,128]{1,0:T(8,128)(2,1)S(1)} %pad_maximum_fusion.2), channel_id=1, source_target_pairs={{0,16},{1,17},{2,18},{3,19},{4,20},{5,21},{6,22},{7,23},{8,24},{9,... | collective-permute-start | bytes 208904 | tf_op jit(solution)/shard_map/ppermute | solution.py:29
  22.4 56.1 %collective-permute-start.7 = (bf16[8,256,256]{2,1,0:T(8,128)(2,1)}, bf16[8,256,256]{2,1,0:T(8,128)(2,1)S(1)}, u32[]{:S(2)}, u32[]{:S(2)}) collective-permute-start(bf16[8,256,256]{2,1,0:T(8,128)(2,1)} %get-tuple-element.21), channel_id=1, source_target_pairs={{0,16},{1,17},{2,18},{3,19},{4,20},{5,21},{6,22},{7,23},{8,24},{9,... | collective-permute-start | bytes 3145736 | tf_op jit(solution)/shard_map/ppermute | solution.py:29
  25.0 20.0 %collective-permute-start.1 = (bf16[2,256,128]{2,1,0:T(8,128)(2,1)S(1)}, bf16[2,256,128]{2,1,0:T(8,128)(2,1)S(1)}, u32[]{:S(2)}, u32[]{:S(2)}) collective-permute-start(bf16[2,256,128]{2,1,0:T(8,128)(2,1)S(1)} %pad_maximum_fusion), channel_id=1, source_target_pairs={{0,128},{1,129},{2,130},{3,131},{4,132},{5,133},{6,134},{7,135},{8... | collective-permute-start | bytes 393224 | tf_op jit(solution)/shard_map/ppermute | solution.py:38
  28.5 21.8 %collective-permute-start.2 = (bf16[2,256,128]{2,1,0:T(8,128)(2,1)S(1)}, bf16[2,256,128]{2,1,0:T(8,128)(2,1)S(1)}, u32[]{:S(2)}, u32[]{:S(2)}) collective-permute-start(bf16[2,256,128]{2,1,0:T(8,128)(2,1)S(1)} %pad_maximum_fusion), channel_id=1, source_target_pairs={{0,256},{1,257},{2,258},{3,259},{4,260},{5,261},{6,262},{7,263},{8... | collective-permute-start | bytes 393224 | tf_op jit(solution)/shard_map/ppermute | solution.py:38
  39.1 13.9 %collective-permute-start.3 = (bf16[2,256,128]{2,1,0:T(8,128)(2,1)S(1)}, bf16[2,256,128]{2,1,0:T(8,128)(2,1)S(1)}, u32[]{:S(2)}, u32[]{:S(2)}) collective-permute-start(bf16[2,256,128]{2,1,0:T(8,128)(2,1)S(1)} %pad_maximum_fusion), channel_id=1, source_target_pairs={{0,384},{1,385},{2,386},{3,387},{4,388},{5,389},{6,390},{7,391},{8... | collective-permute-start | bytes 393224 | tf_op jit(solution)/shard_map/ppermute | solution.py:38
  53.8 11.4 %collective-permute-start.4 = (bf16[8,256,128]{2,1,0:T(8,128)(2,1)}, bf16[8,256,128]{2,1,0:T(8,128)(2,1)S(1)}, u32[]{:S(2)}, u32[]{:S(2)}) collective-permute-start(bf16[8,256,128]{2,1,0:T(8,128)(2,1)} %get-tuple-element.36), channel_id=1, source_target_pairs={{0,32},{1,33},{2,34},{3,35},{4,36},{5,37},{6,38},{7,39},{8,40},{9,... | collective-permute-start | bytes 1572872 | tf_op jit(solution)/shard_map/ppermute | solution.py:47
  57.0 15.0 %collective-permute-start.5 = (bf16[8,256,128]{2,1,0:T(8,128)(2,1)}, bf16[8,256,128]{2,1,0:T(8,128)(2,1)S(1)}, u32[]{:S(2)}, u32[]{:S(2)}) collective-permute-start(bf16[8,256,128]{2,1,0:T(8,128)(2,1)} %get-tuple-element.36), channel_id=1, source_target_pairs={{0,64},{1,65},{2,66},{3,67},{4,68},{5,69},{6,70},{7,71},{8,72},{9,... | collective-permute-start | bytes 1572872 | tf_op jit(solution)/shard_map/ppermute | solution.py:47
  61.6 16.0 %collective-permute-start.6 = (bf16[8,256,128]{2,1,0:T(8,128)(2,1)}, bf16[8,256,128]{2,1,0:T(8,128)(2,1)S(1)}, u32[]{:S(2)}, u32[]{:S(2)}) collective-permute-start(bf16[8,256,128]{2,1,0:T(8,128)(2,1)} %get-tuple-element.36), channel_id=1, source_target_pairs={{0,96},{1,97},{2,98},{3,99},{4,100},{5,101},{6,102},{7,103},{8,104... | collective-permute-start | bytes 1572872 | tf_op jit(solution)/shard_map/ppermute | solution.py:47
  81.8 16.2 %collective-permute-start.10 = (bf16[8,256,128]{2,1,0:T(8,128)(2,1)S(1)}, bf16[8,256,128]{2,1,0:T(8,128)(2,1)S(1)}, u32[]{:S(2)}, u32[]{:S(2)}) collective-permute-start(bf16[8,256,128]{2,1,0:T(8,128)(2,1)S(1)} %get-tuple-element.19), channel_id=1, source_target_pairs={{0,12},{1,13},{2,14},{3,15},{4,0},{5,1},{6,2},{7,3},{8,4},{9,5},{1... | collective-permute-start | bytes 1572872 | tf_op jit(solution)/shard_map/ppermute | solution.py:47
  86.3 11.7 %collective-permute-start.9 = (bf16[8,256,128]{2,1,0:T(8,128)(2,1)S(1)}, bf16[8,256,128]{2,1,0:T(8,128)(2,1)S(1)}, u32[]{:S(2)}, u32[]{:S(2)}) collective-permute-start(bf16[8,256,128]{2,1,0:T(8,128)(2,1)S(1)} %get-tuple-element.20), channel_id=1, source_target_pairs={{0,8},{1,9},{2,10},{3,11},{4,12},{5,13},{6,14},{7,15},{8,0},{9,1},... | collective-permute-start | bytes 1572872 | tf_op jit(solution)/shard_map/ppermute | solution.py:47
  89.1 14.3 %collective-permute-start.8 = (bf16[8,256,128]{2,1,0:T(8,128)(2,1)S(1)}, bf16[8,256,128]{2,1,0:T(8,128)(2,1)S(1)}, u32[]{:S(2)}, u32[]{:S(2)}) collective-permute-start(bf16[8,256,128]{2,1,0:T(8,128)(2,1)S(1)} %get-tuple-element.18), channel_id=1, source_target_pairs={{0,4},{1,5},{2,6},{3,7},{4,8},{5,9},{6,10},{7,11},{8,12},{9,13},{1... | collective-permute-start | bytes 1572872 | tf_op jit(solution)/shard_map/ppermute | solution.py:47
  103.7 10.2 %collective-permute-start.13 = (bf16[2,256,128]{2,1,0:T(8,128)(2,1)S(1)}, bf16[2,256,128]{2,1,0:T(8,128)(2,1)S(1)}, u32[]{:S(2)}, u32[]{:S(2)}) collective-permute-start(bf16[2,256,128]{2,1,0:T(8,128)(2,1)S(1)} %get-tuple-element.27), channel_id=1, source_target_pairs={{0,3},{1,0},{2,1},{3,2},{4,7},{5,4},{6,5},{7,6},{8,11},{9,8},{10,9... | collective-permute-start | bytes 393224 | tf_op jit(solution)/shard_map/ppermute | solution.py:38
  105.6 8.9 %collective-permute-start.12 = (bf16[2,256,128]{2,1,0:T(8,128)(2,1)S(1)}, bf16[2,256,128]{2,1,0:T(8,128)(2,1)S(1)}, u32[]{:S(2)}, u32[]{:S(2)}) collective-permute-start(bf16[2,256,128]{2,1,0:T(8,128)(2,1)S(1)} %get-tuple-element.28), channel_id=1, source_target_pairs={{0,2},{1,3},{2,0},{3,1},{4,6},{5,7},{6,4},{7,5},{8,10},{9,11},{10,... | collective-permute-start | bytes 393224 | tf_op jit(solution)/shard_map/ppermute | solution.py:38
  110.5 11.3 %collective-permute-start.11 = (bf16[2,256,128]{2,1,0:T(8,128)(2,1)S(1)}, bf16[2,256,128]{2,1,0:T(8,128)(2,1)S(1)}, u32[]{:S(2)}, u32[]{:S(2)}) collective-permute-start(bf16[2,256,128]{2,1,0:T(8,128)(2,1)S(1)} %get-tuple-element.26), channel_id=1, source_target_pairs={{0,1},{1,2},{2,3},{3,0},{4,5},{5,6},{6,7},{7,4},{8,9},{9,10},{10,1... | collective-permute-start | bytes 393224 | tf_op jit(solution)/shard_map/ppermute | solution.py:38
  121.9 3.1 collective-permute-start.14
  126.1 3.1 collective-permute-start.15
  129.3 14.9 %collective-permute-start.16 = (bf16[2,256,128]{2,1,0:T(8,128)(2,1)S(1)}, bf16[2,256,128]{2,1,0:T(8,128)(2,1)S(1)}, u32[]{:S(2)}, u32[]{:S(2)}) collective-permute-start(bf16[2,256,128]{2,1,0:T(8,128)(2,1)S(1)} %pad_maximum_fusion.1), channel_id=1, source_target_pairs={{0,128},{1,129},{2,130},{3,131},{4,132},{5,133},{6,134},{7,135},{8... | collective-permute-start | bytes 393224 | tf_op jit(solution)/shard_map/ppermute | solution.py:38
  132.4 18.1 %collective-permute-start.17 = (bf16[2,256,128]{2,1,0:T(8,128)(2,1)S(1)}, bf16[2,256,128]{2,1,0:T(8,128)(2,1)S(1)}, u32[]{:S(2)}, u32[]{:S(2)}) collective-permute-start(bf16[2,256,128]{2,1,0:T(8,128)(2,1)S(1)} %pad_maximum_fusion.1), channel_id=1, source_target_pairs={{0,256},{1,257},{2,258},{3,259},{4,260},{5,261},{6,262},{7,263},{8... | collective-permute-start | bytes 393224 | tf_op jit(solution)/shard_map/ppermute | solution.py:38
  138.3 12.6 %collective-permute-start.18 = (bf16[2,256,128]{2,1,0:T(8,128)(2,1)S(1)}, bf16[2,256,128]{2,1,0:T(8,128)(2,1)S(1)}, u32[]{:S(2)}, u32[]{:S(2)}) collective-permute-start(bf16[2,256,128]{2,1,0:T(8,128)(2,1)S(1)} %pad_maximum_fusion.1), channel_id=1, source_target_pairs={{0,384},{1,385},{2,386},{3,387},{4,388},{5,389},{6,390},{7,391},{8... | collective-permute-start | bytes 393224 | tf_op jit(solution)/shard_map/ppermute | solution.py:38
  151.0 16.8 %collective-permute-start.19 = (bf16[8,256,128]{2,1,0:T(8,128)(2,1)S(1)}, bf16[8,256,128]{2,1,0:T(8,128)(2,1)S(1)}, u32[]{:S(2)}, u32[]{:S(2)}) collective-permute-start(bf16[8,256,128]{2,1,0:T(8,128)(2,1)S(1)} %get-tuple-element.29), channel_id=1, source_target_pairs={{0,32},{1,33},{2,34},{3,35},{4,36},{5,37},{6,38},{7,39},{8,40},{9,... | collective-permute-start | bytes 1572872 | tf_op jit(solution)/shard_map/ppermute | solution.py:47
  161.1 12.9 %collective-permute-start.20 = (bf16[8,256,128]{2,1,0:T(8,128)(2,1)S(1)}, bf16[8,256,128]{2,1,0:T(8,128)(2,1)S(1)}, u32[]{:S(2)}, u32[]{:S(2)}) collective-permute-start(bf16[8,256,128]{2,1,0:T(8,128)(2,1)S(1)} %get-tuple-element.29), channel_id=1, source_target_pairs={{0,64},{1,65},{2,66},{3,67},{4,68},{5,69},{6,70},{7,71},{8,72},{9,... | collective-permute-start | bytes 1572872 | tf_op jit(solution)/shard_map/ppermute | solution.py:47
  163.8 11.8 %collective-permute-start.21 = (bf16[8,256,128]{2,1,0:T(8,128)(2,1)S(1)}, bf16[8,256,128]{2,1,0:T(8,128)(2,1)S(1)}, u32[]{:S(2)}, u32[]{:S(2)}) collective-permute-start(bf16[8,256,128]{2,1,0:T(8,128)(2,1)S(1)} %get-tuple-element.29), channel_id=1, source_target_pairs={{0,96},{1,97},{2,98},{3,99},{4,100},{5,101},{6,102},{7,103},{8,104... | collective-permute-start | bytes 1572872 | tf_op jit(solution)/shard_map/ppermute | solution.py:47
  177.5 10.2 %collective-permute-start.24 = (bf16[8,256,128]{2,1,0:T(8,128)(2,1)S(1)}, bf16[8,256,128]{2,1,0:T(8,128)(2,1)S(1)}, u32[]{:S(2)}, u32[]{:S(2)}) collective-permute-start(bf16[8,256,128]{2,1,0:T(8,128)(2,1)S(1)} %get-tuple-element.16), channel_id=1, source_target_pairs={{0,12},{1,13},{2,14},{3,15},{4,0},{5,1},{6,2},{7,3},{8,4},{9,5},{1... | collective-permute-start | bytes 1572872 | tf_op jit(solution)/shard_map/ppermute | solution.py:47
  179.6 11.5 %collective-permute-start.23 = (bf16[8,256,128]{2,1,0:T(8,128)(2,1)S(1)}, bf16[8,256,128]{2,1,0:T(8,128)(2,1)S(1)}, u32[]{:S(2)}, u32[]{:S(2)}) collective-permute-start(bf16[8,256,128]{2,1,0:T(8,128)(2,1)S(1)} %get-tuple-element.17), channel_id=1, source_target_pairs={{0,8},{1,9},{2,10},{3,11},{4,12},{5,13},{6,14},{7,15},{8,0},{9,1},... | collective-permute-start | bytes 1572872 | tf_op jit(solution)/shard_map/ppermute | solution.py:47
  183.9 12.8 %collective-permute-start.22 = (bf16[8,256,128]{2,1,0:T(8,128)(2,1)S(1)}, bf16[8,256,128]{2,1,0:T(8,128)(2,1)S(1)}, u32[]{:S(2)}, u32[]{:S(2)}) collective-permute-start(bf16[8,256,128]{2,1,0:T(8,128)(2,1)S(1)} %get-tuple-element.15), channel_id=1, source_target_pairs={{0,4},{1,5},{2,6},{3,7},{4,8},{5,9},{6,10},{7,11},{8,12},{9,13},{1... | collective-permute-start | bytes 1572872 | tf_op jit(solution)/shard_map/ppermute | solution.py:47
  197.0 265.8 %collective-permute-start.27 = (bf16[2,256,128]{2,1,0:T(8,128)(2,1)S(1)}, bf16[2,256,128]{2,1,0:T(8,128)(2,1)S(1)}, u32[]{:S(2)}, u32[]{:S(2)}) collective-permute-start(bf16[2,256,128]{2,1,0:T(8,128)(2,1)S(1)} %get-tuple-element.24), channel_id=1, source_target_pairs={{0,3},{1,0},{2,1},{3,2},{4,7},{5,4},{6,5},{7,6},{8,11},{9,8},{10,9... | collective-permute-start | bytes 393224 | tf_op jit(solution)/shard_map/ppermute | solution.py:38
  202.8 260.0 %collective-permute-start.26 = (bf16[2,256,128]{2,1,0:T(8,128)(2,1)S(1)}, bf16[2,256,128]{2,1,0:T(8,128)(2,1)S(1)}, u32[]{:S(2)}, u32[]{:S(2)}) collective-permute-start(bf16[2,256,128]{2,1,0:T(8,128)(2,1)S(1)} %get-tuple-element.25), channel_id=1, source_target_pairs={{0,2},{1,3},{2,0},{3,1},{4,6},{5,7},{6,4},{7,5},{8,10},{9,11},{10,... | collective-permute-start | bytes 393224 | tf_op jit(solution)/shard_map/ppermute | solution.py:38
  208.1 254.6 %collective-permute-start.25 = (bf16[2,256,128]{2,1,0:T(8,128)(2,1)S(1)}, bf16[2,256,128]{2,1,0:T(8,128)(2,1)S(1)}, u32[]{:S(2)}, u32[]{:S(2)}) collective-permute-start(bf16[2,256,128]{2,1,0:T(8,128)(2,1)S(1)} %get-tuple-element.23), channel_id=1, source_target_pairs={{0,1},{1,2},{2,3},{3,0},{4,5},{5,6},{6,7},{7,4},{8,9},{9,10},{10,1... | collective-permute-start | bytes 393224 | tf_op jit(solution)/shard_map/ppermute | solution.py:38
  212.2 436.7 %all-reduce.7.cloned.1.call-start = ((), (), s32[]{:S(2)}) async-start(), calls=%async_computation.1 | async-start | bytes 139264 | tf_op jit(solution)/shard_map/psum | solution.py:162
  462.9 188.7 %collective-permute-start.28 = (bf16[256,128]{1,0:T(8,128)(2,1)S(1)}, bf16[256,128]{1,0:T(8,128)(2,1)S(1)}, u32[]{:S(2)}, u32[]{:S(2)}) collective-permute-start(bf16[256,128]{1,0:T(8,128)(2,1)S(1)} %fusion.10), channel_id=1, source_target_pairs={{0,16},{1,17},{2,18},{3,19},{4,20},{5,21},{6,22},{7,23},{8,24},{9,... | collective-permute-start | bytes 196616 | tf_op jit(solution)/shard_map/ppermute | solution.py:29
  (8 other events, 171.3 us)
Sparse Core Ops, SparseCore 0:
  212.3 250.3 all-reduce.4
  465.9 182.9 all-reduce.6

commit v2 on v1

v2 whole, which is shorter than its diff:
```python
import functools
import jax
import jax.numpy as jnp
from jax import lax
from jax.experimental import pallas as pl
from jax.experimental.pallas import tpu as pltpu
from jax.sharding import PartitionSpec as P

BLOCK = 256
RING = 4
HALF = 64
LIFT = 80
AXES = ("row", "col")


def rank(zl, x, core, y, zh):
    return ((zl * RING + x) * 2 + core) * RING * RING + y * RING + zh


def pairs(step):
    out = []
    for zl in range(RING):
        for x in range(RING):
            for core in range(2):
                for y in range(RING):
                    for zh in range(RING):
                        out.append((rank(zl, x, core, y, zh), rank(*step(zl, x, core, y, zh))))
    return out


def swap_cores(v):
    return lax.ppermute(v, AXES, pairs(lambda zl, x, core, y, zh: (zl, x, 1 - core, y, zh)))


def far_shift(v, k, row_core):
    def step(zl, x, core, y, zh):
        if core == row_core:
            return (zl + k) % RING, x, core, y, zh
        return zl, x, core, y, (zh + k) % RING

    return lax.ppermute(v, AXES, pairs(step))


def near_shift(v, k, row_core):
    def step(zl, x, core, y, zh):
        if core == row_core:
            return zl, (x + k) % RING, core, y, zh
        return zl, x, core, (y + k) % RING, zh

    return lax.ppermute(v, AXES, pairs(step))


def call(kernel, outs, *operands, scalars=0, scratch=()):
    smem = pl.BlockSpec(memory_space=pltpu.SMEM)
    vmem = pl.BlockSpec(memory_space=pltpu.VMEM)
    return pl.pallas_call(
        kernel,
        out_shape=[jax.ShapeDtypeStruct(shape, dtype) for shape, dtype in outs],
        in_specs=[smem] * scalars + [vmem] * (len(operands) - scalars),
        out_specs=[vmem] * len(outs),
        scratch_shapes=list(scratch),
        compiler_params=pltpu.CompilerParams(vmem_limit_bytes=40 * 1024 * 1024),
    )(*operands)


def joined(ref, base):
    return ref[base : base + LIFT].astype(jnp.float32) + ref[
        base + LIFT : base + 2 * LIFT
    ].astype(jnp.float32)


def put_split(refs, base, value):
    high = value.astype(jnp.bfloat16)
    low = (value - high.astype(jnp.float32)).astype(jnp.bfloat16)
    for ref in refs:
        ref[base : base + LIFT] = high
        ref[base + LIFT : base + 2 * LIFT] = low


def put_lifted(refs, base_out, parts, base):
    own, after, across, before = [joined(ref, base) for ref in parts]
    put_split(refs, base_out, (own + across) + (after + before))


def join_kernel(lifted, *refs):
    parts, out_ref = refs[:RING], refs[RING]
    n = parts[0].shape[0] - lifted
    for k in range(RING):
        out_ref[k * n : (k + 1) * n] = parts[k][:n]
    if lifted:
        put_lifted([out_ref], RING * n, parts, n)


def tile_kernel(lifted, src_ref, dst_ref, weight_ref, own_ref, other_ref, *refs):
    parts, outs = refs[:RING], refs[RING : 2 * RING]
    gathered_ref, acc_ref = refs[2 * RING :]
    n = parts[0].shape[0] - lifted
    held = n // BLOCK
    for k in range(RING):
        gathered_ref[k * held : (k + 1) * held] = parts[k][:n].reshape(held, BLOCK, -1)
    acc_ref[...] = jnp.zeros_like(acc_ref)
    slots = own_ref.shape[0]
    for half, tiles_ref in enumerate((own_ref, other_ref)):
        for t in range(slots):
            s = half * slots + t
            term = jnp.dot(
                tiles_ref[t], gathered_ref[src_ref[s]], preferred_element_type=jnp.float32
            )
            acc_ref[dst_ref[s]] += weight_ref[s] * term
    for k in range(RING):
        sums = acc_ref[k * held : (k + 1) * held].astype(jnp.bfloat16)
        outs[k][:n] = sums.reshape(n, sums.shape[-1])
    if lifted:
        put_lifted(outs, n, parts, n)


def sum_kernel(lifted, *refs):
    parts, outs = refs[:RING], refs[RING:]
    n = parts[0].shape[0] - lifted
    m = n // RING
    for k in range(RING):
        total = parts[0][k * m : (k + 1) * m].astype(jnp.float32)
        for part in parts[1:]:
            total = total + part[k * m : (k + 1) * m].astype(jnp.float32)
        outs[k][:m] = total.astype(jnp.bfloat16)
    if lifted:
        put_lifted(outs, m, parts, n)


def last_kernel(lifted, *refs):
    parts, (own_ref, out_ref) = refs[:RING], refs[RING:]
    for k in range(2):
        rows = slice(k * BLOCK, (k + 1) * BLOCK)
        total = parts[0][rows].astype(jnp.float32)
        for part in parts[1:]:
            total = total + part[rows].astype(jnp.float32)
        if k == 0:
            own_ref[...] = total
        else:
            out_ref[:BLOCK] = total.astype(jnp.bfloat16)
    if lifted:
        put_lifted([out_ref], BLOCK, parts, 2 * BLOCK)


def middle_kernel(
    core_ref, own_ref, back_ref, scaled_ref, scale_ref, weight_ref, bias_ref, cotangent_ref,
    activated_ref, sent_ref, kept_ref,
):
    scale = scale_ref[...]
    total = own_ref[...] + back_ref[...].astype(jnp.float32) + scaled_ref[...].astype(jnp.float32)
    spread = total.astype(jnp.bfloat16)
    hidden = jnp.dot(spread, weight_ref[...], preferred_element_type=jnp.float32)
    preact = scale * hidden + bias_ref[...]
    sig = jax.nn.sigmoid(preact)
    activated_ref[...] = (preact * sig).astype(jnp.bfloat16)
    delta = cotangent_ref[...].astype(jnp.float32) * sig * (1.0 + preact * (1.0 - sig))
    scaled_delta = (scale * delta).astype(jnp.bfloat16)
    sent_ref[:BLOCK] = scaled_delta
    grads = lax.dot_general(
        spread, scaled_delta, (((0,), (0,)), ((), ())), preferred_element_type=jnp.float32
    )
    pad = LIFT - HALF
    bias_grad = jnp.sum(delta, axis=0, keepdims=True)
    row = lax.broadcasted_iota(jnp.int32, (pad, grads.shape[1]), 0)
    top = jnp.concatenate([grads[:HALF], jnp.where(row == 0, bias_grad, 0.0)], axis=0)
    bottom = jnp.concatenate([grads[HALF:], jnp.zeros((pad, grads.shape[1]), jnp.float32)], axis=0)
    first = core_ref[0] == 0
    put_split([kept_ref], 0, jnp.where(first, top, bottom))
    put_split([sent_ref], BLOCK, jnp.where(first, bottom, top))


def start_kernel(own_ref, kept_ref, other_ref, out_ref):
    out_ref[:BLOCK] = own_ref[:BLOCK]
    out_ref[BLOCK : 2 * BLOCK] = other_ref[:BLOCK]
    put_split([out_ref], 2 * BLOCK, joined(kept_ref, 0) + joined(other_ref, BLOCK))


def end_kernel(
    core_ref, own_ref, sent_ref, back_ref, mine_ref, scale_ref, weight_ref,
    feature_grad_ref, weight_grad_ref, bias_grad_ref,
):
    total = own_ref[...] + back_ref[:BLOCK].astype(jnp.float32)
    total = total + mine_ref[:BLOCK].astype(jnp.float32)
    proj_grad = (scale_ref[...] * total).astype(jnp.bfloat16)
    feature_grad_ref[...] = lax.dot_general(
        proj_grad, weight_ref[...], (((1,), (1,)), ((), ())), preferred_element_type=jnp.float32
    ).astype(jnp.bfloat16)
    first = core_ref[0] == 0
    here, there = joined(sent_ref, BLOCK), joined(back_ref, BLOCK)
    top = jnp.where(first, here, there)
    bottom = jnp.where(first, there, here)
    weight_grad_ref[:HALF] = top[:HALF]
    weight_grad_ref[HALF:] = bottom[:HALF]
    bias_grad_ref[...] = top[HALF : HALF + 1]


def shards(
    features, weight, bias, node_scale, cotangent, tile_row, tile_col, tile_count, tile_values
):
    row_pos = lax.axis_index("row")
    col_pos = lax.axis_index("col")
    core = row_pos % 2
    x = row_pos // 2 % RING
    zl = row_pos // (2 * RING)
    y = col_pos // RING
    zh = col_pos % RING
    n_col = lax.axis_size("col")
    first = core == 0
    width = features.shape[1]

    rows_idx = tile_row[0, 0]
    cols_idx = tile_col[0, 0]
    tiles = tile_values[0, 0]
    slots = jnp.arange(rows_idx.shape[0], dtype=jnp.int32)
    same = row_pos * n_col + rows_idx == cols_idx * n_col + col_pos
    live = jnp.where(slots < tile_count[0, 0], jnp.where(same, 0.5, 1.0), 0.0)

    scale = node_scale[:, None]
    scaled = (scale * features.astype(jnp.float32)).astype(jnp.bfloat16)

    meta = jnp.stack([rows_idx.astype(jnp.float32), cols_idx.astype(jnp.float32), live])
    meta = jnp.pad(meta, ((0, 13), (0, 120))).astype(jnp.bfloat16)
    arrived = swap_cores(jnp.concatenate([scaled, meta], axis=0))
    meta_other = arrived[BLOCK : BLOCK + 3, :8]
    turned = jnp.swapaxes(tiles, 1, 2)
    own = jnp.where(first, tiles, turned)
    other = swap_cores(jnp.where(first, turned, tiles))

    rows_all = jnp.concatenate([rows_idx, meta_other[0].astype(jnp.int32)])
    cols_all = jnp.concatenate([cols_idx, meta_other[1].astype(jnp.int32)])
    weights = jnp.concatenate([live, meta_other[2].astype(jnp.float32)])
    foreign = jnp.concatenate([jnp.zeros_like(slots), jnp.ones_like(slots)])
    dx = cols_all // 2 % RING - x
    dzl = cols_all // (2 * RING) - zl
    dcore = (cols_all % 2 != core).astype(jnp.int32)
    dy = rows_all // RING - y
    dzh = rows_all % RING - zh
    from_row = (jnp.mod(-dx, RING) * RING + jnp.mod(-dzl, RING)) * 2 + dcore
    from_col = (jnp.mod(-dy, RING) * RING + jnp.mod(-dzh, RING)) * 2 + foreign
    to_row = (jnp.mod(dx, RING) * RING + jnp.mod(dzl, RING)) * 2 + dcore
    to_col = (jnp.mod(dy, RING) * RING + jnp.mod(dzh, RING)) * 2 + foreign
    src = jnp.where(first, from_row, from_col)
    dst = jnp.where(first, to_col, to_row)

    def aggregate(both, lifted):
        bf16 = jnp.bfloat16
        n, m = 2 * RING * BLOCK, 2 * BLOCK
        far = [both] + [far_shift(both, k, 0) for k in range(1, RING)]
        (held,) = call(
            functools.partial(join_kernel, lifted), [((n + lifted, width), bf16)], *far
        )
        near = [held] + [near_shift(held, k, 0) for k in range(1, RING)]
        slabs = (2 * RING * RING, BLOCK, width)
        sums = call(
            functools.partial(tile_kernel, lifted),
            [((n + lifted, width), bf16)] * RING,
            src, dst, weights, own, other, *near,
            scalars=3,
            scratch=[pltpu.VMEM(slabs, bf16), pltpu.VMEM(slabs, jnp.float32)],
        )
        near = [sums[0]] + [near_shift(sums[k], k, 1) for k in range(1, RING)]
        sums = call(
            functools.partial(sum_kernel, lifted), [((m + lifted, width), bf16)] * RING, *near
        )
        far = [sums[0]] + [far_shift(sums[k], k, 1) for k in range(1, RING)]
        mine, theirs = call(
            functools.partial(last_kernel, lifted),
            [((BLOCK, width), jnp.float32), ((BLOCK + lifted, width), bf16)],
            *far,
        )
        return mine, theirs, swap_cores(theirs)

    lifted = 2 * LIFT
    core_no = core.reshape(1)
    mine, _, back = aggregate(jnp.concatenate([scaled, arrived[:BLOCK]], axis=0), 0)
    activated, sent, kept = call(
        middle_kernel,
        [
            ((BLOCK, width), jnp.bfloat16),
            ((BLOCK + lifted, width), jnp.bfloat16),
            ((lifted, width), jnp.bfloat16),
        ],
        core_no, mine, back, scaled, scale, weight, bias[None, :], cotangent,
        scalars=1,
    )
    (both,) = call(
        start_kernel,
        [((2 * BLOCK + lifted, width), jnp.bfloat16)],
        sent, kept, swap_cores(sent),
    )
    mine, theirs, back = aggregate(both, lifted)
    feature_grad, weight_grad, bias_grad = call(
        end_kernel,
        [
            ((BLOCK, width), jnp.bfloat16),
            (weight.shape, jnp.float32),
            ((1, width), jnp.float32),
        ],
        core_no, mine, theirs, back, sent, scale, weight,
        scalars=1,
    )
    return activated, feature_grad, weight_grad, bias_grad[0]


def solution(mesh):
    placed = (
        P(AXES, None),
        P(),
        P(),
        P(AXES),
        P(AXES, None),
        P("row", "col", None),
        P("row", "col", None),
        P("row", "col"),
        P("row", "col", None, None, None),
    )
    return jax.shard_map(
        shards,
        mesh=mesh,
        in_specs=placed,
        out_specs=(P(AXES, None), P(AXES, None), P(), P()),
        check_vma=False,
    )
```

time: 670 us -> 232 us (0.35); the launches traced: 659 us -> 230 us
  waiting for transfers between devices: 497 us -> 94.8 us
  between operations: 15.4 us -> 1.8 us
  local copies, waits for them, and re-layouts: 12.5 us -> 4.36 us
    psum x2 -> x0, waiting for transfers between devices: 433 us -> none  [shards(): grads = lax.psum(lax.psum(grads, 'row'), 'col')]
    ppermute x12, waiting for transfers between devices: 21.1 us -> 49.7 us  [far_shift(): return lax.ppermute(v, AXES, pairs(step))]
  transfers between devices with their start and end apart: 31 -> 29, of which waited for: 20 -> 22; matrix products, arithmetic and copies ran while one was open for 2% -> 1% of each run, Pallas kernels for 0% -> 0%
where the time goes in v2:
time: 232 us; the launch traced here: 230 us
  starting transfers between devices  121 us (52%)
  waiting for transfers between devices  94.8 us (41%)
  Pallas kernels  6.14 us (3%)
  local copies, waits for them, and re-layouts  4.36 us (2%)
  other arithmetic  2.42 us (1%)
    ppermute x12, starting transfers between devices, far_shift(): return lax.ppermute(v, AXES, pairs(step))  61.6 us
    ppermute x12, waiting for transfers between devices, far_shift(): return lax.ppermute(v, AXES, pairs(step))  49.7 us
    ppermute x12, starting transfers between devices, near_shift(): return lax.ppermute(v, AXES, pairs(step))  42.4 us
    ppermute x12, waiting for transfers between devices, near_shift(): return lax.ppermute(v, AXES, pairs(step))  41.5 us
    ppermute x5, starting transfers between devices, swap_cores(): lax.ppermute(v, AXES, pairs(lambda zl, x, core, y, zh: (zl, x, 1 - core,...  16.6 us
    pallas_call x11, Pallas kernels, call(): pl.pallas_call(kernel, out_shape=[jax.ShapeDtypeStruct(shape, dtype) for...  6.14 us
  transfers between devices with their start and end apart: 29, of which 22 were waited for; matrix products, arithmetic and copies ran while one was open for 1% of the time, Pallas kernels for 0%

profile of v2, /device:TPU:1, one launch (start us, length us, event | category | flops | bytes accessed | tf_op | source)
XLA Modules:
  0.0 230.0 jit_solution(9880494113270610839)
XLA Ops:
  3.6 8.8 %collective-permute-start = (bf16[272,128]{1,0:T(8,128)(2,1)S(1)}, bf16[272,128]{1,0:T(8,128)(2,1)S(1)}, u32[]{:S(2)}, u32[]{:S(2)}) collective-permute-start(bf16[272,128]{1,0:T(8,128)(2,1)S(1)} %pad_maximum_fusion.1), channel_id=1, source_target_pairs={{0,16},{1,17},{2,18},{3,19},{4,20},{5,21},{6,22},{7,23},{8,24},{9,... | collective-permute-start | bytes 208904 | tf_op jit(solution)/shard_map/ppermute | solution.py:32
  17.2 7.1 %collective-permute-start.4 = (bf16[512,128]{1,0:T(8,128)(2,1)S(1)}, bf16[512,128]{1,0:T(8,128)(2,1)S(1)}, u32[]{:S(2)}, u32[]{:S(2)}) collective-permute-start(bf16[512,128]{1,0:T(8,128)(2,1)S(1)} %pad_maximum_fusion.refs_0_), channel_id=1, source_target_pairs={{0,384},{1,385},{2,386},{3,387},{4,388},{5,389},{6,390},{7,391},{8... | collective-permute-start | bytes 393224 | tf_op jit(solution)/shard_map/ppermute | solution.py:41
  24.3 4.9 %collective-permute-start.3 = (bf16[512,128]{1,0:T(8,128)(2,1)S(1)}, bf16[512,128]{1,0:T(8,128)(2,1)S(1)}, u32[]{:S(2)}, u32[]{:S(2)}) collective-permute-start(bf16[512,128]{1,0:T(8,128)(2,1)S(1)} %pad_maximum_fusion.refs_0_), channel_id=1, source_target_pairs={{0,256},{1,257},{2,258},{3,259},{4,260},{5,261},{6,262},{7,263},{8... | collective-permute-start | bytes 393224 | tf_op jit(solution)/shard_map/ppermute | solution.py:41
  29.2 7.3 %collective-permute-start.2 = (bf16[512,128]{1,0:T(8,128)(2,1)S(1)}, bf16[512,128]{1,0:T(8,128)(2,1)S(1)}, u32[]{:S(2)}, u32[]{:S(2)}) collective-permute-start(bf16[512,128]{1,0:T(8,128)(2,1)S(1)} %pad_maximum_fusion.refs_0_), channel_id=1, source_target_pairs={{0,128},{1,129},{2,130},{3,131},{4,132},{5,133},{6,134},{7,135},{8... | collective-permute-start | bytes 393224 | tf_op jit(solution)/shard_map/ppermute | solution.py:41
  36.5 2.9 %collective-permute-done.3.refs_2_ = bf16[512,128]{1,0:T(8,128)(2,1)S(1)} collective-permute-done((bf16[512,128]{1,0:T(8,128)(2,1)S(1)}, bf16[512,128]{1,0:T(8,128)(2,1)S(1)}, u32[]{:S(2)}, u32[]{:S(2)}) %collective-permute-start.3) | collective-permute-done | bytes 131104 | tf_op jit(solution)/shard_map/ppermute | solution.py:41
  39.4 3.2 %collective-permute-done.2.refs_1_ = bf16[512,128]{1,0:T(8,128)(2,1)S(1)} collective-permute-done((bf16[512,128]{1,0:T(8,128)(2,1)S(1)}, bf16[512,128]{1,0:T(8,128)(2,1)S(1)}, u32[]{:S(2)}, u32[]{:S(2)}) %collective-permute-start.2) | collective-permute-done | bytes 131104 | tf_op jit(solution)/shard_map/ppermute | solution.py:41
  42.6 4.6 %collective-permute-start.7 = (bf16[2048,128]{1,0:T(8,128)(2,1)S(1)}, bf16[2048,128]{1,0:T(8,128)(2,1)S(1)}, u32[]{:S(2)}, u32[]{:S(2)}) collective-permute-start(bf16[2048,128]{1,0:T(8,128)(2,1)S(1)} %shard_map.120.refs_0_), channel_id=1, source_target_pairs={{0,96},{1,97},{2,98},{3,99},{4,100},{5,101},{6,102},{7,103},{8,104... | collective-permute-start | bytes 1572872 | tf_op jit(solution)/shard_map/ppermute | solution.py:50
  47.2 2.3 collective-permute-start.6
  49.5 2.6 %collective-permute-start.5 = (bf16[2048,128]{1,0:T(8,128)(2,1)S(1)}, bf16[2048,128]{1,0:T(8,128)(2,1)S(1)}, u32[]{:S(2)}, u32[]{:S(2)}) collective-permute-start(bf16[2048,128]{1,0:T(8,128)(2,1)S(1)} %shard_map.120.refs_0_), channel_id=1, source_target_pairs={{0,32},{1,33},{2,34},{3,35},{4,36},{5,37},{6,38},{7,39},{8,40},{9,... | collective-permute-start | bytes 1572872 | tf_op jit(solution)/shard_map/ppermute | solution.py:50
  53.0 5.9 %collective-permute-done.7.refs_3_ = bf16[2048,128]{1,0:T(8,128)(2,1)S(1)} collective-permute-done((bf16[2048,128]{1,0:T(8,128)(2,1)S(1)}, bf16[2048,128]{1,0:T(8,128)(2,1)S(1)}, u32[]{:S(2)}, u32[]{:S(2)}) %collective-permute-start.7) | collective-permute-done | bytes 524320 | tf_op jit(solution)/shard_map/ppermute | solution.py:50
  58.9 6.7 %collective-permute-done.5.refs_1_ = bf16[2048,128]{1,0:T(8,128)(2,1)S(1)} collective-permute-done((bf16[2048,128]{1,0:T(8,128)(2,1)S(1)}, bf16[2048,128]{1,0:T(8,128)(2,1)S(1)}, u32[]{:S(2)}, u32[]{:S(2)}) %collective-permute-start.5) | collective-permute-done | bytes 524320 | tf_op jit(solution)/shard_map/ppermute | solution.py:50
  67.4 6.1 %collective-permute-start.8 = (bf16[2048,128]{1,0:T(8,128)(2,1)S(1)}, bf16[2048,128]{1,0:T(8,128)(2,1)S(1)}, u32[]{:S(2)}, u32[]{:S(2)}) collective-permute-start(bf16[2048,128]{1,0:T(8,128)(2,1)S(1)} %get-tuple-element.31), channel_id=1, source_target_pairs={{0,4},{1,5},{2,6},{3,7},{4,8},{5,9},{6,10},{7,11},{8,12},{9,13},{1... | collective-permute-start | bytes 1572872 | tf_op jit(solution)/shard_map/ppermute | solution.py:50
  73.5 3.6 %collective-permute-start.9 = (bf16[2048,128]{1,0:T(8,128)(2,1)S(1)}, bf16[2048,128]{1,0:T(8,128)(2,1)S(1)}, u32[]{:S(2)}, u32[]{:S(2)}) collective-permute-start(bf16[2048,128]{1,0:T(8,128)(2,1)S(1)} %get-tuple-element.32), channel_id=1, source_target_pairs={{0,8},{1,9},{2,10},{3,11},{4,12},{5,13},{6,14},{7,15},{8,0},{9,1},... | collective-permute-start | bytes 1572872 | tf_op jit(solution)/shard_map/ppermute | solution.py:50
  77.1 3.9 %collective-permute-start.10 = (bf16[2048,128]{1,0:T(8,128)(2,1)S(1)}, bf16[2048,128]{1,0:T(8,128)(2,1)S(1)}, u32[]{:S(2)}, u32[]{:S(2)}) collective-permute-start(bf16[2048,128]{1,0:T(8,128)(2,1)S(1)} %get-tuple-element.33), channel_id=1, source_target_pairs={{0,12},{1,13},{2,14},{3,15},{4,0},{5,1},{6,2},{7,3},{8,4},{9,5},{1... | collective-permute-start | bytes 1572872 | tf_op jit(solution)/shard_map/ppermute | solution.py:50
  81.0 6.3 %collective-permute-done.9.refs_2_ = bf16[2048,128]{1,0:T(8,128)(2,1)S(1)} collective-permute-done((bf16[2048,128]{1,0:T(8,128)(2,1)S(1)}, bf16[2048,128]{1,0:T(8,128)(2,1)S(1)}, u32[]{:S(2)}, u32[]{:S(2)}) %collective-permute-start.9) | collective-permute-done | bytes 524320 | tf_op jit(solution)/shard_map/ppermute | solution.py:50
  89.1 9.3 %collective-permute-start.11 = (bf16[512,128]{1,0:T(8,128)(2,1)S(1)}, bf16[512,128]{1,0:T(8,128)(2,1)S(1)}, u32[]{:S(2)}, u32[]{:S(2)}) collective-permute-start(bf16[512,128]{1,0:T(8,128)(2,1)S(1)} %get-tuple-element.35), channel_id=1, source_target_pairs={{0,1},{1,2},{2,3},{3,0},{4,5},{5,6},{6,7},{7,4},{8,9},{9,10},{10,1... | collective-permute-start | bytes 393224 | tf_op jit(solution)/shard_map/ppermute | solution.py:41
  98.4 7.2 %collective-permute-start.12 = (bf16[512,128]{1,0:T(8,128)(2,1)S(1)}, bf16[512,128]{1,0:T(8,128)(2,1)S(1)}, u32[]{:S(2)}, u32[]{:S(2)}) collective-permute-start(bf16[512,128]{1,0:T(8,128)(2,1)S(1)} %get-tuple-element.36), channel_id=1, source_target_pairs={{0,2},{1,3},{2,0},{3,1},{4,6},{5,7},{6,4},{7,5},{8,10},{9,11},{10,... | collective-permute-start | bytes 393224 | tf_op jit(solution)/shard_map/ppermute | solution.py:41
  108.7 5.7 %collective-permute-done.12.refs_2_ = bf16[512,128]{1,0:T(8,128)(2,1)S(1)} collective-permute-done((bf16[512,128]{1,0:T(8,128)(2,1)S(1)}, bf16[512,128]{1,0:T(8,128)(2,1)S(1)}, u32[]{:S(2)}, u32[]{:S(2)}) %collective-permute-start.12) | collective-permute-done | bytes 131104 | tf_op jit(solution)/shard_map/ppermute | solution.py:41
  125.1 6.2 %collective-permute-start.17 = (bf16[672,128]{1,0:T(8,128)(2,1)S(1)}, bf16[672,128]{1,0:T(8,128)(2,1)S(1)}, u32[]{:S(2)}, u32[]{:S(2)}) collective-permute-start(bf16[672,128]{1,0:T(8,128)(2,1)S(1)} %shard_map.125.refs_0_), channel_id=1, source_target_pairs={{0,256},{1,257},{2,258},{3,259},{4,260},{5,261},{6,262},{7,263},{8... | collective-permute-start | bytes 516104 | tf_op jit(solution)/shard_map/ppermute | solution.py:41
  131.3 3.7 %collective-permute-start.16 = (bf16[672,128]{1,0:T(8,128)(2,1)S(1)}, bf16[672,128]{1,0:T(8,128)(2,1)S(1)}, u32[]{:S(2)}, u32[]{:S(2)}) collective-permute-start(bf16[672,128]{1,0:T(8,128)(2,1)S(1)} %shard_map.125.refs_0_), channel_id=1, source_target_pairs={{0,128},{1,129},{2,130},{3,131},{4,132},{5,133},{6,134},{7,135},{8... | collective-permute-start | bytes 516104 | tf_op jit(solution)/shard_map/ppermute | solution.py:41
  135.0 3.3 %collective-permute-done.18.refs_3_ = bf16[672,128]{1,0:T(8,128)(2,1)S(1)} collective-permute-done((bf16[672,128]{1,0:T(8,128)(2,1)S(1)}, bf16[672,128]{1,0:T(8,128)(2,1)S(1)}, u32[]{:S(2)}, u32[]{:S(2)}) %collective-permute-start.18) | collective-permute-done | bytes 172064 | tf_op jit(solution)/shard_map/ppermute | solution.py:41
  138.4 8.1 %collective-permute-done.17.refs_2_ = bf16[672,128]{1,0:T(8,128)(2,1)S(1)} collective-permute-done((bf16[672,128]{1,0:T(8,128)(2,1)S(1)}, bf16[672,128]{1,0:T(8,128)(2,1)S(1)}, u32[]{:S(2)}, u32[]{:S(2)}) %collective-permute-start.17) | collective-permute-done | bytes 172064 | tf_op jit(solution)/shard_map/ppermute | solution.py:41
  146.5 7.7 %collective-permute-done.16.refs_1_ = bf16[672,128]{1,0:T(8,128)(2,1)S(1)} collective-permute-done((bf16[672,128]{1,0:T(8,128)(2,1)S(1)}, bf16[672,128]{1,0:T(8,128)(2,1)S(1)}, u32[]{:S(2)}, u32[]{:S(2)}) %collective-permute-start.16) | collective-permute-done | bytes 172064 | tf_op jit(solution)/shard_map/ppermute | solution.py:41
  156.2 5.4 %collective-permute-start.20 = (bf16[2208,128]{1,0:T(8,128)(2,1)S(1)}, bf16[2208,128]{1,0:T(8,128)(2,1)S(1)}, u32[]{:S(2)}, u32[]{:S(2)}) collective-permute-start(bf16[2208,128]{1,0:T(8,128)(2,1)S(1)} %shard_map.126.refs_0_), channel_id=1, source_target_pairs={{0,64},{1,65},{2,66},{3,67},{4,68},{5,69},{6,70},{7,71},{8,72},{9,... | collective-permute-start | bytes 1695752 | tf_op jit(solution)/shard_map/ppermute | solution.py:50
  165.2 3.5 %collective-permute-done.20.refs_2_ = bf16[2208,128]{1,0:T(8,128)(2,1)S(1)} collective-permute-done((bf16[2208,128]{1,0:T(8,128)(2,1)S(1)}, bf16[2208,128]{1,0:T(8,128)(2,1)S(1)}, u32[]{:S(2)}, u32[]{:S(2)}) %collective-permute-start.20) | collective-permute-done | bytes 565280 | tf_op jit(solution)/shard_map/ppermute | solution.py:50
  168.7 6.0 %collective-permute-done.19.refs_1_ = bf16[2208,128]{1,0:T(8,128)(2,1)S(1)} collective-permute-done((bf16[2208,128]{1,0:T(8,128)(2,1)S(1)}, bf16[2208,128]{1,0:T(8,128)(2,1)S(1)}, u32[]{:S(2)}, u32[]{:S(2)}) %collective-permute-start.19) | collective-permute-done | bytes 565280 | tf_op jit(solution)/shard_map/ppermute | solution.py:50
  178.4 5.3 %collective-permute-start.23 = (bf16[2208,128]{1,0:T(8,128)(2,1)S(1)}, bf16[2208,128]{1,0:T(8,128)(2,1)S(1)}, u32[]{:S(2)}, u32[]{:S(2)}) collective-permute-start(bf16[2208,128]{1,0:T(8,128)(2,1)S(1)} %get-tuple-element.45), channel_id=1, source_target_pairs={{0,8},{1,9},{2,10},{3,11},{4,12},{5,13},{6,14},{7,15},{8,0},{9,1},... | collective-permute-start | bytes 1695752 | tf_op jit(solution)/shard_map/ppermute | solution.py:50
  183.7 2.9 %collective-permute-start.24 = (bf16[2208,128]{1,0:T(8,128)(2,1)S(1)}, bf16[2208,128]{1,0:T(8,128)(2,1)S(1)}, u32[]{:S(2)}, u32[]{:S(2)}) collective-permute-start(bf16[2208,128]{1,0:T(8,128)(2,1)S(1)} %get-tuple-element.46), channel_id=1, source_target_pairs={{0,12},{1,13},{2,14},{3,15},{4,0},{5,1},{6,2},{7,3},{8,4},{9,5},{1... | collective-permute-start | bytes 1695752 | tf_op jit(solution)/shard_map/ppermute | solution.py:50
  188.3 6.5 %collective-permute-done.23.refs_2_ = bf16[2208,128]{1,0:T(8,128)(2,1)S(1)} collective-permute-done((bf16[2208,128]{1,0:T(8,128)(2,1)S(1)}, bf16[2208,128]{1,0:T(8,128)(2,1)S(1)}, u32[]{:S(2)}, u32[]{:S(2)}) %collective-permute-start.23) | collective-permute-done | bytes 565280 | tf_op jit(solution)/shard_map/ppermute | solution.py:50
  196.9 6.2 %collective-permute-start.25 = (bf16[672,128]{1,0:T(8,128)(2,1)S(1)}, bf16[672,128]{1,0:T(8,128)(2,1)S(1)}, u32[]{:S(2)}, u32[]{:S(2)}) collective-permute-start(bf16[672,128]{1,0:T(8,128)(2,1)S(1)} %get-tuple-element.48), channel_id=1, source_target_pairs={{0,1},{1,2},{2,3},{3,0},{4,5},{5,6},{6,7},{7,4},{8,9},{9,10},{10,1... | collective-permute-start | bytes 516104 | tf_op jit(solution)/shard_map/ppermute | solution.py:41
  205.0 4.0 %collective-permute-start.27 = (bf16[672,128]{1,0:T(8,128)(2,1)S(1)}, bf16[672,128]{1,0:T(8,128)(2,1)S(1)}, u32[]{:S(2)}, u32[]{:S(2)}) collective-permute-start(bf16[672,128]{1,0:T(8,128)(2,1)S(1)} %get-tuple-element.50), channel_id=1, source_target_pairs={{0,3},{1,0},{2,1},{3,2},{4,7},{5,4},{6,5},{7,6},{8,11},{9,8},{10,9... | collective-permute-start | bytes 516104 | tf_op jit(solution)/shard_map/ppermute | solution.py:41
  209.0 16.8 %collective-permute-done.26.refs_2_ = bf16[672,128]{1,0:T(8,128)(2,1)S(1)} collective-permute-done((bf16[672,128]{1,0:T(8,128)(2,1)S(1)}, bf16[672,128]{1,0:T(8,128)(2,1)S(1)}, u32[]{:S(2)}, u32[]{:S(2)}) %collective-permute-start.26) | collective-permute-done | bytes 172064 | tf_op jit(solution)/shard_map/ppermute | solution.py:41
  (68 shorter events, 44.5 us)
Async XLA Ops:
  3.6 13.5 %collective-permute-start = (bf16[272,128]{1,0:T(8,128)(2,1)S(1)}, bf16[272,128]{1,0:T(8,128)(2,1)S(1)}, u32[]{:S(2)}, u32[]{:S(2)}) collective-permute-start(bf16[272,128]{1,0:T(8,128)(2,1)S(1)} %pad_maximum_fusion.1), channel_id=1, source_target_pairs={{0,16},{1,17},{2,18},{3,19},{4,20},{5,21},{6,22},{7,23},{8,24},{9,... | collective-permute-start | bytes 208904 | tf_op jit(solution)/shard_map/ppermute | solution.py:32
  12.4 1.6 copy-start.3
  15.2 50.4 %collective-permute-start.1 = (bf16[8,256,256]{2,1,0:T(8,128)(2,1)}, bf16[8,256,256]{2,1,0:T(8,128)(2,1)S(1)}, u32[]{:S(2)}, u32[]{:S(2)}) collective-permute-start(bf16[8,256,256]{2,1,0:T(8,128)(2,1)} %get-tuple-element.61), channel_id=1, source_target_pairs={{0,16},{1,17},{2,18},{3,19},{4,20},{5,21},{6,22},{7,23},{8,24},{9,... | collective-permute-start | bytes 3145736 | tf_op jit(solution)/shard_map/ppermute | solution.py:32
  17.2 19.3 %collective-permute-start.4 = (bf16[512,128]{1,0:T(8,128)(2,1)S(1)}, bf16[512,128]{1,0:T(8,128)(2,1)S(1)}, u32[]{:S(2)}, u32[]{:S(2)}) collective-permute-start(bf16[512,128]{1,0:T(8,128)(2,1)S(1)} %pad_maximum_fusion.refs_0_), channel_id=1, source_target_pairs={{0,384},{1,385},{2,386},{3,387},{4,388},{5,389},{6,390},{7,391},{8... | collective-permute-start | bytes 393224 | tf_op jit(solution)/shard_map/ppermute | solution.py:41
  24.3 15.1 %collective-permute-start.3 = (bf16[512,128]{1,0:T(8,128)(2,1)S(1)}, bf16[512,128]{1,0:T(8,128)(2,1)S(1)}, u32[]{:S(2)}, u32[]{:S(2)}) collective-permute-start(bf16[512,128]{1,0:T(8,128)(2,1)S(1)} %pad_maximum_fusion.refs_0_), channel_id=1, source_target_pairs={{0,256},{1,257},{2,258},{3,259},{4,260},{5,261},{6,262},{7,263},{8... | collective-permute-start | bytes 393224 | tf_op jit(solution)/shard_map/ppermute | solution.py:41
  29.2 13.4 %collective-permute-start.2 = (bf16[512,128]{1,0:T(8,128)(2,1)S(1)}, bf16[512,128]{1,0:T(8,128)(2,1)S(1)}, u32[]{:S(2)}, u32[]{:S(2)}) collective-permute-start(bf16[512,128]{1,0:T(8,128)(2,1)S(1)} %pad_maximum_fusion.refs_0_), channel_id=1, source_target_pairs={{0,128},{1,129},{2,130},{3,131},{4,132},{5,133},{6,134},{7,135},{8... | collective-permute-start | bytes 393224 | tf_op jit(solution)/shard_map/ppermute | solution.py:41
  42.6 16.3 %collective-permute-start.7 = (bf16[2048,128]{1,0:T(8,128)(2,1)S(1)}, bf16[2048,128]{1,0:T(8,128)(2,1)S(1)}, u32[]{:S(2)}, u32[]{:S(2)}) collective-permute-start(bf16[2048,128]{1,0:T(8,128)(2,1)S(1)} %shard_map.120.refs_0_), channel_id=1, source_target_pairs={{0,96},{1,97},{2,98},{3,99},{4,100},{5,101},{6,102},{7,103},{8,104... | collective-permute-start | bytes 1572872 | tf_op jit(solution)/shard_map/ppermute | solution.py:50
  47.2 11.7 %collective-permute-start.6 = (bf16[2048,128]{1,0:T(8,128)(2,1)S(1)}, bf16[2048,128]{1,0:T(8,128)(2,1)S(1)}, u32[]{:S(2)}, u32[]{:S(2)}) collective-permute-start(bf16[2048,128]{1,0:T(8,128)(2,1)S(1)} %shard_map.120.refs_0_), channel_id=1, source_target_pairs={{0,64},{1,65},{2,66},{3,67},{4,68},{5,69},{6,70},{7,71},{8,72},{9,... | collective-permute-start | bytes 1572872 | tf_op jit(solution)/shard_map/ppermute | solution.py:50
  49.5 16.1 %collective-permute-start.5 = (bf16[2048,128]{1,0:T(8,128)(2,1)S(1)}, bf16[2048,128]{1,0:T(8,128)(2,1)S(1)}, u32[]{:S(2)}, u32[]{:S(2)}) collective-permute-start(bf16[2048,128]{1,0:T(8,128)(2,1)S(1)} %shard_map.120.refs_0_), channel_id=1, source_target_pairs={{0,32},{1,33},{2,34},{3,35},{4,36},{5,37},{6,38},{7,39},{8,40},{9,... | collective-permute-start | bytes 1572872 | tf_op jit(solution)/shard_map/ppermute | solution.py:50
  67.4 13.6 %collective-permute-start.8 = (bf16[2048,128]{1,0:T(8,128)(2,1)S(1)}, bf16[2048,128]{1,0:T(8,128)(2,1)S(1)}, u32[]{:S(2)}, u32[]{:S(2)}) collective-permute-start(bf16[2048,128]{1,0:T(8,128)(2,1)S(1)} %get-tuple-element.31), channel_id=1, source_target_pairs={{0,4},{1,5},{2,6},{3,7},{4,8},{5,9},{6,10},{7,11},{8,12},{9,13},{1... | collective-permute-start | bytes 1572872 | tf_op jit(solution)/shard_map/ppermute | solution.py:50
  73.5 13.8 %collective-permute-start.9 = (bf16[2048,128]{1,0:T(8,128)(2,1)S(1)}, bf16[2048,128]{1,0:T(8,128)(2,1)S(1)}, u32[]{:S(2)}, u32[]{:S(2)}) collective-permute-start(bf16[2048,128]{1,0:T(8,128)(2,1)S(1)} %get-tuple-element.32), channel_id=1, source_target_pairs={{0,8},{1,9},{2,10},{3,11},{4,12},{5,13},{6,14},{7,15},{8,0},{9,1},... | collective-permute-start | bytes 1572872 | tf_op jit(solution)/shard_map/ppermute | solution.py:50
  77.1 11.8 %collective-permute-start.10 = (bf16[2048,128]{1,0:T(8,128)(2,1)S(1)}, bf16[2048,128]{1,0:T(8,128)(2,1)S(1)}, u32[]{:S(2)}, u32[]{:S(2)}) collective-permute-start(bf16[2048,128]{1,0:T(8,128)(2,1)S(1)} %get-tuple-element.33), channel_id=1, source_target_pairs={{0,12},{1,13},{2,14},{3,15},{4,0},{5,1},{6,2},{7,3},{8,4},{9,5},{1... | collective-permute-start | bytes 1572872 | tf_op jit(solution)/shard_map/ppermute | solution.py:50
  89.1 19.6 %collective-permute-start.11 = (bf16[512,128]{1,0:T(8,128)(2,1)S(1)}, bf16[512,128]{1,0:T(8,128)(2,1)S(1)}, u32[]{:S(2)}, u32[]{:S(2)}) collective-permute-start(bf16[512,128]{1,0:T(8,128)(2,1)S(1)} %get-tuple-element.35), channel_id=1, source_target_pairs={{0,1},{1,2},{2,3},{3,0},{4,5},{5,6},{6,7},{7,4},{8,9},{9,10},{10,1... | collective-permute-start | bytes 393224 | tf_op jit(solution)/shard_map/ppermute | solution.py:41
  98.4 16.0 %collective-permute-start.12 = (bf16[512,128]{1,0:T(8,128)(2,1)S(1)}, bf16[512,128]{1,0:T(8,128)(2,1)S(1)}, u32[]{:S(2)}, u32[]{:S(2)}) collective-permute-start(bf16[512,128]{1,0:T(8,128)(2,1)S(1)} %get-tuple-element.36), channel_id=1, source_target_pairs={{0,2},{1,3},{2,0},{3,1},{4,6},{5,7},{6,4},{7,5},{8,10},{9,11},{10,... | collective-permute-start | bytes 393224 | tf_op jit(solution)/shard_map/ppermute | solution.py:41
  105.6 9.6 %collective-permute-start.13 = (bf16[512,128]{1,0:T(8,128)(2,1)S(1)}, bf16[512,128]{1,0:T(8,128)(2,1)S(1)}, u32[]{:S(2)}, u32[]{:S(2)}) collective-permute-start(bf16[512,128]{1,0:T(8,128)(2,1)S(1)} %get-tuple-element.37), channel_id=1, source_target_pairs={{0,3},{1,0},{2,1},{3,2},{4,7},{5,4},{6,5},{7,6},{8,11},{9,8},{10,9... | collective-permute-start | bytes 393224 | tf_op jit(solution)/shard_map/ppermute | solution.py:41
  115.3 3.1 %collective-permute-start.14 = (bf16[256,128]{1,0:T(8,128)(2,1)S(1)}, bf16[256,128]{1,0:T(8,128)(2,1)S(1)}, u32[]{:S(2)}, u32[]{:S(2)}) collective-permute-start(bf16[256,128]{1,0:T(8,128)(2,1)S(1)} %get-tuple-element.39), channel_id=1, source_target_pairs={{0,16},{1,17},{2,18},{3,19},{4,20},{5,21},{6,22},{7,23},{8,24},{9,... | collective-permute-start | bytes 196616 | tf_op jit(solution)/shard_map/ppermute | solution.py:32
  117.2 1.2 copy-start
  117.2 1.2 copy-start.1
  119.9 3.2 %collective-permute-start.15 = (bf16[416,128]{1,0:T(8,128)(2,1)S(1)}, bf16[416,128]{1,0:T(8,128)(2,1)S(1)}, u32[]{:S(2)}, u32[]{:S(2)}) collective-permute-start(bf16[416,128]{1,0:T(8,128)(2,1)S(1)} %get-tuple-element.41.own_ref.mine_ref), channel_id=1, source_target_pairs={{0,16},{1,17},{2,18},{3,19},{4,20},{5,21},{6,22},{7,23},{8,24},{9,... | collective-permute-start | bytes 319496 | tf_op jit(solution)/shard_map/ppermute | solution.py:32
  123.1 15.2 %collective-permute-start.18 = (bf16[672,128]{1,0:T(8,128)(2,1)S(1)}, bf16[672,128]{1,0:T(8,128)(2,1)S(1)}, u32[]{:S(2)}, u32[]{:S(2)}) collective-permute-start(bf16[672,128]{1,0:T(8,128)(2,1)S(1)} %shard_map.125.refs_0_), channel_id=1, source_target_pairs={{0,384},{1,385},{2,386},{3,387},{4,388},{5,389},{6,390},{7,391},{8... | collective-permute-start | bytes 516104 | tf_op jit(solution)/shard_map/ppermute | solution.py:41
  125.1 21.4 %collective-permute-start.17 = (bf16[672,128]{1,0:T(8,128)(2,1)S(1)}, bf16[672,128]{1,0:T(8,128)(2,1)S(1)}, u32[]{:S(2)}, u32[]{:S(2)}) collective-permute-start(bf16[672,128]{1,0:T(8,128)(2,1)S(1)} %shard_map.125.refs_0_), channel_id=1, source_target_pairs={{0,256},{1,257},{2,258},{3,259},{4,260},{5,261},{6,262},{7,263},{8... | collective-permute-start | bytes 516104 | tf_op jit(solution)/shard_map/ppermute | solution.py:41
  131.3 22.9 %collective-permute-start.16 = (bf16[672,128]{1,0:T(8,128)(2,1)S(1)}, bf16[672,128]{1,0:T(8,128)(2,1)S(1)}, u32[]{:S(2)}, u32[]{:S(2)}) collective-permute-start(bf16[672,128]{1,0:T(8,128)(2,1)S(1)} %shard_map.125.refs_0_), channel_id=1, source_target_pairs={{0,128},{1,129},{2,130},{3,131},{4,132},{5,133},{6,134},{7,135},{8... | collective-permute-start | bytes 516104 | tf_op jit(solution)/shard_map/ppermute | solution.py:41
  154.3 10.9 %collective-permute-start.21 = (bf16[2208,128]{1,0:T(8,128)(2,1)S(1)}, bf16[2208,128]{1,0:T(8,128)(2,1)S(1)}, u32[]{:S(2)}, u32[]{:S(2)}) collective-permute-start(bf16[2208,128]{1,0:T(8,128)(2,1)S(1)} %shard_map.126.refs_0_), channel_id=1, source_target_pairs={{0,96},{1,97},{2,98},{3,99},{4,100},{5,101},{6,102},{7,103},{8,104... | collective-permute-start | bytes 1695752 | tf_op jit(solution)/shard_map/ppermute | solution.py:50
  156.2 12.5 %collective-permute-start.20 = (bf16[2208,128]{1,0:T(8,128)(2,1)S(1)}, bf16[2208,128]{1,0:T(8,128)(2,1)S(1)}, u32[]{:S(2)}, u32[]{:S(2)}) collective-permute-start(bf16[2208,128]{1,0:T(8,128)(2,1)S(1)} %shard_map.126.refs_0_), channel_id=1, source_target_pairs={{0,64},{1,65},{2,66},{3,67},{4,68},{5,69},{6,70},{7,71},{8,72},{9,... | collective-permute-start | bytes 1695752 | tf_op jit(solution)/shard_map/ppermute | solution.py:50
  161.6 13.1 %collective-permute-start.19 = (bf16[2208,128]{1,0:T(8,128)(2,1)S(1)}, bf16[2208,128]{1,0:T(8,128)(2,1)S(1)}, u32[]{:S(2)}, u32[]{:S(2)}) collective-permute-start(bf16[2208,128]{1,0:T(8,128)(2,1)S(1)} %shard_map.126.refs_0_), channel_id=1, source_target_pairs={{0,32},{1,33},{2,34},{3,35},{4,36},{5,37},{6,38},{7,39},{8,40},{9,... | collective-permute-start | bytes 1695752 | tf_op jit(solution)/shard_map/ppermute | solution.py:50
  176.5 11.9 %collective-permute-start.22 = (bf16[2208,128]{1,0:T(8,128)(2,1)S(1)}, bf16[2208,128]{1,0:T(8,128)(2,1)S(1)}, u32[]{:S(2)}, u32[]{:S(2)}) collective-permute-start(bf16[2208,128]{1,0:T(8,128)(2,1)S(1)} %get-tuple-element.44), channel_id=1, source_target_pairs={{0,4},{1,5},{2,6},{3,7},{4,8},{5,9},{6,10},{7,11},{8,12},{9,13},{1... | collective-permute-start | bytes 1695752 | tf_op jit(solution)/shard_map/ppermute | solution.py:50
  178.4 16.4 %collective-permute-start.23 = (bf16[2208,128]{1,0:T(8,128)(2,1)S(1)}, bf16[2208,128]{1,0:T(8,128)(2,1)S(1)}, u32[]{:S(2)}, u32[]{:S(2)}) collective-permute-start(bf16[2208,128]{1,0:T(8,128)(2,1)S(1)} %get-tuple-element.45), channel_id=1, source_target_pairs={{0,8},{1,9},{2,10},{3,11},{4,12},{5,13},{6,14},{7,15},{8,0},{9,1},... | collective-permute-start | bytes 1695752 | tf_op jit(solution)/shard_map/ppermute | solution.py:50
  183.7 12.9 %collective-permute-start.24 = (bf16[2208,128]{1,0:T(8,128)(2,1)S(1)}, bf16[2208,128]{1,0:T(8,128)(2,1)S(1)}, u32[]{:S(2)}, u32[]{:S(2)}) collective-permute-start(bf16[2208,128]{1,0:T(8,128)(2,1)S(1)} %get-tuple-element.46), channel_id=1, source_target_pairs={{0,12},{1,13},{2,14},{3,15},{4,0},{5,1},{6,2},{7,3},{8,4},{9,5},{1... | collective-permute-start | bytes 1695752 | tf_op jit(solution)/shard_map/ppermute | solution.py:50
  196.9 12.1 %collective-permute-start.25 = (bf16[672,128]{1,0:T(8,128)(2,1)S(1)}, bf16[672,128]{1,0:T(8,128)(2,1)S(1)}, u32[]{:S(2)}, u32[]{:S(2)}) collective-permute-start(bf16[672,128]{1,0:T(8,128)(2,1)S(1)} %get-tuple-element.48), channel_id=1, source_target_pairs={{0,1},{1,2},{2,3},{3,0},{4,5},{5,6},{6,7},{7,4},{8,9},{9,10},{10,1... | collective-permute-start | bytes 516104 | tf_op jit(solution)/shard_map/ppermute | solution.py:41
  203.1 22.7 %collective-permute-start.26 = (bf16[672,128]{1,0:T(8,128)(2,1)S(1)}, bf16[672,128]{1,0:T(8,128)(2,1)S(1)}, u32[]{:S(2)}, u32[]{:S(2)}) collective-permute-start(bf16[672,128]{1,0:T(8,128)(2,1)S(1)} %get-tuple-element.49), channel_id=1, source_target_pairs={{0,2},{1,3},{2,0},{3,1},{4,6},{5,7},{6,4},{7,5},{8,10},{9,11},{10,... | collective-permute-start | bytes 516104 | tf_op jit(solution)/shard_map/ppermute | solution.py:41
  205.0 20.8 %collective-permute-start.27 = (bf16[672,128]{1,0:T(8,128)(2,1)S(1)}, bf16[672,128]{1,0:T(8,128)(2,1)S(1)}, u32[]{:S(2)}, u32[]{:S(2)}) collective-permute-start(bf16[672,128]{1,0:T(8,128)(2,1)S(1)} %get-tuple-element.50), channel_id=1, source_target_pairs={{0,3},{1,0},{2,1},{3,2},{4,7},{5,4},{6,5},{7,6},{8,11},{9,8},{10,9... | collective-permute-start | bytes 516104 | tf_op jit(solution)/shard_map/ppermute | solution.py:41
  225.9 3.2 %collective-permute-start.28 = (bf16[416,128]{1,0:T(8,128)(2,1)S(1)}, bf16[416,128]{1,0:T(8,128)(2,1)S(1)}, u32[]{:S(2)}, u32[]{:S(2)}) collective-permute-start(bf16[416,128]{1,0:T(8,128)(2,1)S(1)} %get-tuple-element.52.sent_ref), channel_id=1, source_target_pairs={{0,16},{1,17},{2,18},{3,19},{4,20},{5,21},{6,22},{7,23},{8,24},{9,... | collective-permute-start | bytes 319496 | tf_op jit(solution)/shard_map/ppermute | solution.py:32
  (5 other events, 3.3 us)

commit v3 on v2

v3 whole, which is shorter than its diff:
```python
import functools
import jax
import jax.numpy as jnp
from jax import lax
from jax.experimental import pallas as pl
from jax.experimental.pallas import tpu as pltpu
from jax.sharding import PartitionSpec as P

BLOCK = 256
RING = 4
HALF = 64
LIFT = 80
AXES = ("row", "col")


def rank(zl, x, core, y, zh):
    return ((zl * RING + x) * 2 + core) * RING * RING + y * RING + zh


def pairs(step):
    out = []
    for zl in range(RING):
        for x in range(RING):
            for core in range(2):
                for y in range(RING):
                    for zh in range(RING):
                        out.append((rank(zl, x, core, y, zh), rank(*step(zl, x, core, y, zh))))
    return out


def swap_cores(v):
    return lax.ppermute(v, AXES, pairs(lambda zl, x, core, y, zh: (zl, x, 1 - core, y, zh)))


def far_shift(v, k, row_core):
    def step(zl, x, core, y, zh):
        if core == row_core:
            return (zl + k) % RING, x, core, y, zh
        return zl, x, core, y, (zh + k) % RING

    return lax.ppermute(v, AXES, pairs(step))


def near_shift(v, k, row_core):
    def step(zl, x, core, y, zh):
        if core == row_core:
            return zl, (x + k) % RING, core, y, zh
        return zl, x, core, (y + k) % RING, zh

    return lax.ppermute(v, AXES, pairs(step))


def call(kernel, outs, *operands, scalars=0, scratch=()):
    smem = pl.BlockSpec(memory_space=pltpu.SMEM)
    vmem = pl.BlockSpec(memory_space=pltpu.VMEM)
    return pl.pallas_call(
        kernel,
        out_shape=[jax.ShapeDtypeStruct(shape, dtype) for shape, dtype in outs],
        in_specs=[smem] * scalars + [vmem] * (len(operands) - scalars),
        out_specs=[vmem] * len(outs),
        scratch_shapes=list(scratch),
        compiler_params=pltpu.CompilerParams(vmem_limit_bytes=40 * 1024 * 1024),
    )(*operands)


def joined(ref, base, pieces):
    value = ref[base : base + LIFT].astype(jnp.float32)
    if pieces == 2:
        value = value + ref[base + LIFT : base + 2 * LIFT].astype(jnp.float32)
    return value


def put_split(refs, base, pieces, value):
    high = value.astype(jnp.bfloat16)
    low = (value - high.astype(jnp.float32)).astype(jnp.bfloat16)
    for ref in refs:
        ref[base : base + LIFT] = high
        if pieces == 2:
            ref[base + LIFT : base + 2 * LIFT] = low


def put_lifted(refs, base_out, pieces_out, parts, base, pieces):
    own, after, across, before = [joined(ref, base, pieces) for ref in parts]
    put_split(refs, base_out, pieces_out, (own + across) + (after + before))


def join_kernel(lift, *refs):
    parts, out_ref = refs[:RING], refs[RING]
    n = 2 * BLOCK
    for k in range(RING):
        out_ref[k * n : (k + 1) * n] = parts[k][:n]
    if lift:
        put_lifted([out_ref], RING * n, 2, parts, n, 1)


def tile_kernel(lift, src_ref, dst_ref, weight_ref, own_ref, other_ref, *refs):
    parts, outs = refs[:RING], refs[RING : 2 * RING]
    gathered_ref, acc_ref = refs[2 * RING :]
    held = 2 * RING
    n = held * BLOCK
    for k in range(RING):
        gathered_ref[k * held : (k + 1) * held] = parts[k][:n].reshape(held, BLOCK, -1)
    acc_ref[...] = jnp.zeros_like(acc_ref)
    slots = own_ref.shape[0]
    for half, tiles_ref in enumerate((own_ref, other_ref)):
        for t in range(slots):
            s = half * slots + t
            term = jnp.dot(
                tiles_ref[t], gathered_ref[src_ref[s]], preferred_element_type=jnp.float32
            )
            acc_ref[dst_ref[s]] += weight_ref[s] * term
    for k in range(RING):
        sums = acc_ref[k * held : (k + 1) * held].astype(jnp.bfloat16)
        outs[k][:n] = sums.reshape(n, sums.shape[-1])
    if lift:
        put_lifted(outs, n, 2, parts, n, 2)


def sum_kernel(lift, *refs):
    parts, outs = refs[:RING], refs[RING:]
    m = 2 * BLOCK
    for k in range(RING):
        total = parts[0][k * m : (k + 1) * m].astype(jnp.float32)
        for part in parts[1:]:
            total = total + part[k * m : (k + 1) * m].astype(jnp.float32)
        outs[k][:m] = total.astype(jnp.bfloat16)
    if lift:
        put_lifted(outs, m, 1, parts, RING * m, 2)


def relay_kernel(lift, mine_ref, passing_ref, out_ref):
    m = 2 * BLOCK
    total = mine_ref[:m].astype(jnp.float32) + passing_ref[:m].astype(jnp.float32)
    out_ref[:m] = total.astype(jnp.bfloat16)
    if lift:
        out_ref[m:] = passing_ref[m:]


def last_kernel(lift, own_ref, after_ref, across_ref, before_ref, sums_ref, out_ref):
    m = 2 * BLOCK
    total = own_ref[:m].astype(jnp.float32)
    for part in (across_ref, before_ref):
        total = total + part[:m].astype(jnp.float32)
    sums_ref[...] = total
    if lift:
        out_ref[:BLOCK] = total[BLOCK:].astype(jnp.bfloat16)
        parts = (own_ref, after_ref, across_ref, before_ref)
        put_lifted([out_ref], BLOCK, 2, parts, m, 1)
    else:
        out_ref[...] = total.astype(jnp.bfloat16)


def middle_kernel(
    core_ref, sums_ref, back_ref, both_ref, scale_ref, other_ref, weight_ref, bias_ref,
    cotangent_ref, activated_ref, out_ref,
):
    packed = other_ref[BLOCK : 2 * BLOCK, :3].astype(jnp.float32)
    scales = (scale_ref[...], packed[:, 0:1] + packed[:, 1:2] + packed[:, 2:3])
    cotangents = (cotangent_ref[...], other_ref[:BLOCK])
    grads = bias_grad = None
    for c in range(2):
        rows = slice(c * BLOCK, (c + 1) * BLOCK)
        back = back_ref[(1 - c) * BLOCK : (2 - c) * BLOCK].astype(jnp.float32)
        total = sums_ref[rows] + back + both_ref[rows].astype(jnp.float32)
        spread = total.astype(jnp.bfloat16)
        hidden = jnp.dot(spread, weight_ref[...], preferred_element_type=jnp.float32)
        preact = scales[c] * hidden + bias_ref[...]
        sig = jax.nn.sigmoid(preact)
        if c == 0:
            activated_ref[...] = (preact * sig).astype(jnp.bfloat16)
        delta = cotangents[c].astype(jnp.float32) * sig * (1.0 + preact * (1.0 - sig))
        scaled_delta = (scales[c] * delta).astype(jnp.bfloat16)
        out_ref[rows] = scaled_delta
        product = lax.dot_general(
            spread, scaled_delta, (((0,), (0,)), ((), ())), preferred_element_type=jnp.float32
        )
        column = jnp.sum(delta, axis=0, keepdims=True)
        grads = product if c == 0 else grads + product
        bias_grad = column if c == 0 else bias_grad + column
    pad = LIFT - HALF
    row = lax.broadcasted_iota(jnp.int32, (pad, grads.shape[1]), 0)
    top = jnp.concatenate([grads[:HALF], jnp.where(row == 0, bias_grad, 0.0)], axis=0)
    bottom = jnp.concatenate([grads[HALF:], jnp.zeros((pad, grads.shape[1]), jnp.float32)], axis=0)
    put_split([out_ref], 2 * BLOCK, 1, jnp.where(core_ref[0] == 0, top, bottom))


def end_kernel(
    core_ref, sums_ref, sent_ref, back_ref, both_ref, scale_ref, weight_ref,
    feature_grad_ref, weight_grad_ref, bias_grad_ref,
):
    total = sums_ref[:BLOCK] + back_ref[:BLOCK].astype(jnp.float32)
    total = total + both_ref[:BLOCK].astype(jnp.float32)
    proj_grad = (scale_ref[...] * total).astype(jnp.bfloat16)
    feature_grad_ref[...] = lax.dot_general(
        proj_grad, weight_ref[...], (((1,), (1,)), ((), ())), preferred_element_type=jnp.float32
    ).astype(jnp.bfloat16)
    first = core_ref[0] == 0
    here, there = joined(sent_ref, BLOCK, 2), joined(back_ref, BLOCK, 2)
    top = jnp.where(first, here, there)
    bottom = jnp.where(first, there, here)
    weight_grad_ref[:HALF] = top[:HALF]
    weight_grad_ref[HALF:] = bottom[:HALF]
    bias_grad_ref[...] = top[HALF : HALF + 1]


def shards(
    features, weight, bias, node_scale, cotangent, tile_row, tile_col, tile_count, tile_values
):
    row_pos = lax.axis_index("row")
    col_pos = lax.axis_index("col")
    core = row_pos % 2
    x = row_pos // 2 % RING
    zl = row_pos // (2 * RING)
    y = col_pos // RING
    zh = col_pos % RING
    n_col = lax.axis_size("col")
    first = core == 0
    width = features.shape[1]

    rows_idx = tile_row[0, 0]
    cols_idx = tile_col[0, 0]
    tiles = tile_values[0, 0]
    slots = jnp.arange(rows_idx.shape[0], dtype=jnp.int32)
    same = row_pos * n_col + rows_idx == cols_idx * n_col + col_pos
    live = jnp.where(slots < tile_count[0, 0], jnp.where(same, 0.5, 1.0), 0.0)

    scale = node_scale[:, None]
    scaled = (scale * features.astype(jnp.float32)).astype(jnp.bfloat16)

    meta = jnp.stack([rows_idx.astype(jnp.float32), cols_idx.astype(jnp.float32), live])
    meta = jnp.pad(meta, ((0, 13), (0, 120))).astype(jnp.bfloat16)
    arrived = swap_cores(jnp.concatenate([scaled, meta], axis=0))
    meta_other = arrived[BLOCK : BLOCK + 3, :8]
    rows_all = jnp.concatenate([rows_idx, meta_other[0].astype(jnp.int32)])
    cols_all = jnp.concatenate([cols_idx, meta_other[1].astype(jnp.int32)])
    weights = jnp.concatenate([live, meta_other[2].astype(jnp.float32)])
    foreign = jnp.concatenate([jnp.zeros_like(slots), jnp.ones_like(slots)])
    dx = cols_all // 2 % RING - x
    dzl = cols_all // (2 * RING) - zl
    dcore = (cols_all % 2 != core).astype(jnp.int32)
    dy = rows_all // RING - y
    dzh = rows_all % RING - zh
    from_row = (jnp.mod(-dx, RING) * RING + jnp.mod(-dzl, RING)) * 2 + dcore
    from_col = (jnp.mod(-dy, RING) * RING + jnp.mod(-dzh, RING)) * 2 + foreign
    to_row = (jnp.mod(dx, RING) * RING + jnp.mod(dzl, RING)) * 2 + dcore
    to_col = (jnp.mod(dy, RING) * RING + jnp.mod(dzh, RING)) * 2 + foreign
    src = jnp.where(first, from_row, from_col)
    dst = jnp.where(first, to_col, to_row)

    def gather_far(both, lift):
        after = far_shift(both, 1, 0)
        before = far_shift(both, -1, 0)
        across = far_shift(after, 1, 0)
        rows = 2 * RING * BLOCK + (2 * LIFT if lift else 0)
        (held,) = call(
            functools.partial(join_kernel, lift),
            [((rows, width), jnp.bfloat16)],
            both, after, across, before,
        )
        return held, after

    def spread_sum(held, own, other, lift):
        bf16 = jnp.bfloat16
        m = 2 * BLOCK + (LIFT if lift else 0)
        near = [held] + [near_shift(held, k, 0) for k in range(1, RING)]
        slabs = (2 * RING * RING, BLOCK, width)
        sums = call(
            functools.partial(tile_kernel, lift),
            [(held.shape, bf16)] * RING,
            src, dst, weights, own, other, *near,
            scalars=3,
            scratch=[pltpu.VMEM(slabs, bf16), pltpu.VMEM(slabs, jnp.float32)],
        )
        near = [sums[0]] + [near_shift(sums[k], k, 1) for k in range(1, RING)]
        sums = call(functools.partial(sum_kernel, lift), [((m, width), bf16)] * RING, *near)
        after = far_shift(sums[2], 1, 1)
        before = far_shift(sums[3], -1, 1)
        (passed,) = call(
            functools.partial(relay_kernel, lift), [((m, width), bf16)], sums[1], after
        )
        across = far_shift(passed, 1, 1)
        rows = BLOCK + 2 * LIFT if lift else 2 * BLOCK
        both_sums, sent = call(
            functools.partial(last_kernel, lift),
            [((2 * BLOCK, width), jnp.float32), ((rows, width), bf16)],
            sums[0], after, across, before,
        )
        return both_sums, sent, swap_cores(sent)

    core_no = core.reshape(1)
    both = jnp.concatenate([scaled, arrived[:BLOCK]], axis=0)
    held, after = gather_far(both, False)

    tiles, _ = lax.optimization_barrier((tiles, after))
    cotangent, parts, held = lax.optimization_barrier((cotangent, scale, held))
    turned = jnp.swapaxes(tiles, 1, 2)
    own = jnp.where(first, tiles, turned)
    other = swap_cores(jnp.where(first, turned, tiles))
    packed = []
    for _ in range(3):
        piece = lax.reduce_precision(parts, exponent_bits=8, mantissa_bits=7)
        packed.append(piece)
        parts = parts - piece
    packed = jnp.pad(jnp.concatenate(packed, axis=1), ((0, 0), (0, width - 3)))
    facts = swap_cores(jnp.concatenate([cotangent, packed.astype(jnp.bfloat16)], axis=0))

    sums, _, back = spread_sum(held, own, other, False)
    activated, both = call(
        middle_kernel,
        [((BLOCK, width), jnp.bfloat16), ((2 * BLOCK + LIFT, width), jnp.bfloat16)],
        core_no, sums, back, both, scale, facts, weight, bias[None, :], cotangent,
        scalars=1,
    )
    held, _ = gather_far(both, True)
    sums, sent, back = spread_sum(held, own, other, True)
    feature_grad, weight_grad, bias_grad = call(
        end_kernel,
        [
            ((BLOCK, width), jnp.bfloat16),
            (weight.shape, jnp.float32),
            ((1, width), jnp.float32),
        ],
        core_no, sums, sent, back, both, scale, weight,
        scalars=1,
    )
    return activated, feature_grad, weight_grad, bias_grad[0]


def solution(mesh):
    placed = (
        P(AXES, None),
        P(),
        P(),
        P(AXES),
        P(AXES, None),
        P("row", "col", None),
        P("row", "col", None),
        P("row", "col"),
        P("row", "col", None, None, None),
    )
    return jax.shard_map(
        shards,
        mesh=mesh,
        in_specs=placed,
        out_specs=(P(AXES, None), P(AXES, None), P(), P()),
        check_vma=False,
    )
```

time: 232 us -> 227 us (0.978)
  waiting for transfers between devices: 94.8 us -> 85.7 us
  starting transfers between devices: 121 us -> 125 us
    ppermute x5, starting transfers between devices: 16.6 us -> 34.5 us  [swap_cores(): lax.ppermute(v, AXES, pairs(lambda zl, x, core, y, zh: (zl, x, 1 - core,...]
    ppermute x12, waiting for transfers between devices: 49.7 us -> 39 us  [far_shift(): return lax.ppermute(v, AXES, pairs(step))]
    ppermute x12, starting transfers between devices: 61.6 us -> 52.8 us  [far_shift(): return lax.ppermute(v, AXES, pairs(step))]
    ppermute x12, starting transfers between devices: 42.4 us -> 38 us  [near_shift(): return lax.ppermute(v, AXES, pairs(step))]
    ppermute x12, waiting for transfers between devices: 41.5 us -> 44.1 us  [near_shift(): return lax.ppermute(v, AXES, pairs(step))]
    pallas_call x11 -> x12, Pallas kernels: 6.14 us -> 6.2 us  [call(): pl.pallas_call(kernel, out_shape=[jax.ShapeDtypeStruct(shape, dtype) for...]
  transfers between devices with their start and end apart: 29 -> 29, of which waited for: 22 -> 22; matrix products, arithmetic and copies ran while one was open for 1% -> 0% of each run, Pallas kernels for 0% -> 0%
where the time goes in v3:
time: 227 us; the launch traced here: 226 us
  starting transfers between devices  125 us (55%)
  waiting for transfers between devices  85.7 us (38%)
  Pallas kernels  6.2 us (3%)
  local copies, waits for them, and re-layouts  4.5 us (2%)
  other arithmetic  2.45 us (1%)
    ppermute x12, starting transfers between devices, far_shift(): return lax.ppermute(v, AXES, pairs(step))  52.8 us
    ppermute x12, waiting for transfers between devices, near_shift(): return lax.ppermute(v, AXES, pairs(step))  44.1 us
    ppermute x12, waiting for transfers between devices, far_shift(): return lax.ppermute(v, AXES, pairs(step))  39 us
    ppermute x12, starting transfers between devices, near_shift(): return lax.ppermute(v, AXES, pairs(step))  38 us
    ppermute x5, starting transfers between devices, swap_cores(): lax.ppermute(v, AXES, pairs(lambda zl, x, core, y, zh: (zl, x, 1 - core,...  34.5 us
    pallas_call x12, Pallas kernels, call(): pl.pallas_call(kernel, out_shape=[jax.ShapeDtypeStruct(shape, dtype) for...  6.2 us
  transfers between devices with their start and end apart: 29, of which 22 were waited for; matrix products, arithmetic and copies ran while one was open for 0% of the time, Pallas kernels for 0%

profile of v3, /device:TPU:1, one launch (start us, length us, event | category | flops | bytes accessed | tf_op | source)
XLA Modules:
  0.0 225.9 jit_solution(1013630917002816477)
XLA Ops:
  3.6 8.8 %collective-permute-start = (bf16[272,128]{1,0:T(8,128)(2,1)S(1)}, bf16[272,128]{1,0:T(8,128)(2,1)S(1)}, u32[]{:S(2)}, u32[]{:S(2)}) collective-permute-start(bf16[272,128]{1,0:T(8,128)(2,1)S(1)} %pad_maximum_fusion.1), channel_id=1, source_target_pairs={{0,16},{1,17},{2,18},{3,19},{4,20},{5,21},{6,22},{7,23},{8,24},{9,... | collective-permute-start | bytes 208904 | tf_op jit(solution)/shard_map/ppermute | solution.py:32
  13.3 3.4 %collective-permute-start.1 = (bf16[512,128]{1,0:T(8,128)(2,1)S(1)}, bf16[512,128]{1,0:T(8,128)(2,1)S(1)}, u32[]{:S(2)}, u32[]{:S(2)}) collective-permute-start(bf16[512,128]{1,0:T(8,128)(2,1)S(1)} %pad_maximum_fusion.refs_0_.both_ref), channel_id=1, source_target_pairs={{0,128},{1,129},{2,130},{3,131},{4,132},{5,133},{6,134},{7,135},{8... | collective-permute-start | bytes 393224 | tf_op jit(solution)/shard_map/ppermute | solution.py:41
  16.8 6.5 %collective-permute-done.1.refs_1_ = bf16[512,128]{1,0:T(8,128)(2,1)S(1)} collective-permute-done((bf16[512,128]{1,0:T(8,128)(2,1)S(1)}, bf16[512,128]{1,0:T(8,128)(2,1)S(1)}, u32[]{:S(2)}, u32[]{:S(2)}) %collective-permute-start.1) | collective-permute-done | bytes 131104 | tf_op jit(solution)/shard_map/ppermute | solution.py:41
  28.0 11.8 %collective-permute-start.4 = (bf16[512,128]{1,0:T(8,128)(2,1)S(1)}, bf16[512,128]{1,0:T(8,128)(2,1)S(1)}, u32[]{:S(2)}, u32[]{:S(2)}) collective-permute-start(bf16[512,128]{1,0:T(8,128)(2,1)S(1)} %pad_maximum_fusion.refs_0_.both_ref), channel_id=1, source_target_pairs={{0,384},{1,385},{2,386},{3,387},{4,388},{5,389},{6,390},{7,391},{8... | collective-permute-start | bytes 393224 | tf_op jit(solution)/shard_map/ppermute | solution.py:41
  41.8 2.9 %collective-permute-done.4.refs_3_ = bf16[512,128]{1,0:T(8,128)(2,1)S(1)} collective-permute-done((bf16[512,128]{1,0:T(8,128)(2,1)S(1)}, bf16[512,128]{1,0:T(8,128)(2,1)S(1)}, u32[]{:S(2)}, u32[]{:S(2)}) %collective-permute-start.4) | collective-permute-done | bytes 131104 | tf_op jit(solution)/shard_map/ppermute | solution.py:41
  44.7 8.2 %collective-permute-done.3.refs_2_ = bf16[512,128]{1,0:T(8,128)(2,1)S(1)} collective-permute-done((bf16[512,128]{1,0:T(8,128)(2,1)S(1)}, bf16[512,128]{1,0:T(8,128)(2,1)S(1)}, u32[]{:S(2)}, u32[]{:S(2)}) %collective-permute-start.3) | collective-permute-done | bytes 131104 | tf_op jit(solution)/shard_map/ppermute | solution.py:41
  52.9 4.6 %collective-permute-start.7 = (bf16[2048,128]{1,0:T(8,128)(2,1)S(1)}, bf16[2048,128]{1,0:T(8,128)(2,1)S(1)}, u32[]{:S(2)}, u32[]{:S(2)}) collective-permute-start(bf16[2048,128]{1,0:T(8,128)(2,1)S(1)} %shard_map.120.refs_0_), channel_id=1, source_target_pairs={{0,96},{1,97},{2,98},{3,99},{4,100},{5,101},{6,102},{7,103},{8,104... | collective-permute-start | bytes 1572872 | tf_op jit(solution)/shard_map/ppermute | solution.py:50
  63.3 5.9 %collective-permute-done.7.refs_3_ = bf16[2048,128]{1,0:T(8,128)(2,1)S(1)} collective-permute-done((bf16[2048,128]{1,0:T(8,128)(2,1)S(1)}, bf16[2048,128]{1,0:T(8,128)(2,1)S(1)}, u32[]{:S(2)}, u32[]{:S(2)}) %collective-permute-start.7) | collective-permute-done | bytes 524320 | tf_op jit(solution)/shard_map/ppermute | solution.py:50
  69.2 5.3 %collective-permute-done.5.refs_1_ = bf16[2048,128]{1,0:T(8,128)(2,1)S(1)} collective-permute-done((bf16[2048,128]{1,0:T(8,128)(2,1)S(1)}, bf16[2048,128]{1,0:T(8,128)(2,1)S(1)}, u32[]{:S(2)}, u32[]{:S(2)}) %collective-permute-start.5) | collective-permute-done | bytes 524320 | tf_op jit(solution)/shard_map/ppermute | solution.py:50
  76.3 3.1 %collective-permute-start.8 = (bf16[2048,128]{1,0:T(8,128)(2,1)S(1)}, bf16[2048,128]{1,0:T(8,128)(2,1)S(1)}, u32[]{:S(2)}, u32[]{:S(2)}) collective-permute-start(bf16[2048,128]{1,0:T(8,128)(2,1)S(1)} %get-tuple-element.36), channel_id=1, source_target_pairs={{0,4},{1,5},{2,6},{3,7},{4,8},{5,9},{6,10},{7,11},{8,12},{9,13},{1... | collective-permute-start | bytes 1572872 | tf_op jit(solution)/shard_map/ppermute | solution.py:50
  79.4 4.4 %collective-permute-start.9 = (bf16[2048,128]{1,0:T(8,128)(2,1)S(1)}, bf16[2048,128]{1,0:T(8,128)(2,1)S(1)}, u32[]{:S(2)}, u32[]{:S(2)}) collective-permute-start(bf16[2048,128]{1,0:T(8,128)(2,1)S(1)} %get-tuple-element.37), channel_id=1, source_target_pairs={{0,8},{1,9},{2,10},{3,11},{4,12},{5,13},{6,14},{7,15},{8,0},{9,1},... | collective-permute-start | bytes 1572872 | tf_op jit(solution)/shard_map/ppermute | solution.py:50
  83.8 3.1 %collective-permute-start.10 = (bf16[2048,128]{1,0:T(8,128)(2,1)S(1)}, bf16[2048,128]{1,0:T(8,128)(2,1)S(1)}, u32[]{:S(2)}, u32[]{:S(2)}) collective-permute-start(bf16[2048,128]{1,0:T(8,128)(2,1)S(1)} %get-tuple-element.38), channel_id=1, source_target_pairs={{0,12},{1,13},{2,14},{3,15},{4,0},{5,1},{6,2},{7,3},{8,4},{9,5},{1... | collective-permute-start | bytes 1572872 | tf_op jit(solution)/shard_map/ppermute | solution.py:50
  87.7 6.3 %collective-permute-done.9.refs_2_ = bf16[2048,128]{1,0:T(8,128)(2,1)S(1)} collective-permute-done((bf16[2048,128]{1,0:T(8,128)(2,1)S(1)}, bf16[2048,128]{1,0:T(8,128)(2,1)S(1)}, u32[]{:S(2)}, u32[]{:S(2)}) %collective-permute-start.9) | collective-permute-done | bytes 524320 | tf_op jit(solution)/shard_map/ppermute | solution.py:50
  97.8 5.2 %collective-permute-start.13 = (bf16[512,128]{1,0:T(8,128)(2,1)S(1)}, bf16[512,128]{1,0:T(8,128)(2,1)S(1)}, u32[]{:S(2)}, u32[]{:S(2)}) collective-permute-start(bf16[512,128]{1,0:T(8,128)(2,1)S(1)} %get-tuple-element.42), channel_id=1, source_target_pairs={{0,3},{1,0},{2,1},{3,2},{4,7},{5,4},{6,5},{7,6},{8,11},{9,8},{10,9... | collective-permute-start | bytes 393224 | tf_op jit(solution)/shard_map/ppermute | solution.py:41
  103.0 5.3 %collective-permute-done.11.passing_ref.after_ref = bf16[512,128]{1,0:T(8,128)(2,1)S(1)} collective-permute-done((bf16[512,128]{1,0:T(8,128)(2,1)S(1)}, bf16[512,128]{1,0:T(8,128)(2,1)S(1)}, u32[]{:S(2)}, u32[]{:S(2)}) %collective-permute-start.11) | collective-permute-done | bytes 131104 | tf_op jit(solution)/shard_map/ppermute | solution.py:41
  113.1 2.9 %collective-permute-done.12.across_ref = bf16[512,128]{1,0:T(8,128)(2,1)S(1)} collective-permute-done((bf16[512,128]{1,0:T(8,128)(2,1)S(1)}, bf16[512,128]{1,0:T(8,128)(2,1)S(1)}, u32[]{:S(2)}, u32[]{:S(2)}) %collective-permute-start.12) | collective-permute-done | bytes 131104 | tf_op jit(solution)/shard_map/ppermute | solution.py:41
  116.1 4.7 %collective-permute-start.14 = (bf16[512,128]{1,0:T(8,128)(2,1)S(1)}, bf16[512,128]{1,0:T(8,128)(2,1)S(1)}, u32[]{:S(2)}, u32[]{:S(2)}) collective-permute-start(bf16[512,128]{1,0:T(8,128)(2,1)S(1)} %get-tuple-element.44), channel_id=1, source_target_pairs={{0,16},{1,17},{2,18},{3,19},{4,20},{5,21},{6,22},{7,23},{8,24},{9,... | collective-permute-start | bytes 393224 | tf_op jit(solution)/shard_map/ppermute | solution.py:32
  123.3 4.7 %collective-permute-start.16 = (bf16[592,128]{1,0:T(8,128)(2,1)S(1)}, bf16[592,128]{1,0:T(8,128)(2,1)S(1)}, u32[]{:S(2)}, u32[]{:S(2)}) collective-permute-start(bf16[592,128]{1,0:T(8,128)(2,1)S(1)} %get-tuple-element.48.refs_0_.both_ref), channel_id=1, source_target_pairs={{0,128},{1,129},{2,130},{3,131},{4,132},{5,133},{6,134},{7,135},{8... | collective-permute-start | bytes 454664 | tf_op jit(solution)/shard_map/ppermute | solution.py:41
  128.0 4.5 %collective-permute-start.18 = (bf16[592,128]{1,0:T(8,128)(2,1)S(1)}, bf16[592,128]{1,0:T(8,128)(2,1)S(1)}, u32[]{:S(2)}, u32[]{:S(2)}) collective-permute-start(bf16[592,128]{1,0:T(8,128)(2,1)S(1)} %get-tuple-element.48.refs_0_.both_ref), channel_id=1, source_target_pairs={{0,384},{1,385},{2,386},{3,387},{4,388},{5,389},{6,390},{7,391},{8... | collective-permute-start | bytes 454664 | tf_op jit(solution)/shard_map/ppermute | solution.py:41
  134.6 3.4 %collective-permute-start.17 = (bf16[592,128]{1,0:T(8,128)(2,1)S(1)}, bf16[592,128]{1,0:T(8,128)(2,1)S(1)}, u32[]{:S(2)}, u32[]{:S(2)}) collective-permute-start(bf16[592,128]{1,0:T(8,128)(2,1)S(1)} %collective-permute-done.16.refs_1_), channel_id=1, source_target_pairs={{0,128},{1,129},{2,130},{3,131},{4,132},{5,133},{6,134},{7,135},{8... | collective-permute-start | bytes 454664 | tf_op jit(solution)/shard_map/ppermute | solution.py:41
  138.8 7.1 %collective-permute-done.17.refs_2_ = bf16[592,128]{1,0:T(8,128)(2,1)S(1)} collective-permute-done((bf16[592,128]{1,0:T(8,128)(2,1)S(1)}, bf16[592,128]{1,0:T(8,128)(2,1)S(1)}, u32[]{:S(2)}, u32[]{:S(2)}) %collective-permute-start.17) | collective-permute-done | bytes 151584 | tf_op jit(solution)/shard_map/ppermute | solution.py:41
  146.0 3.8 %collective-permute-start.21 = (bf16[2208,128]{1,0:T(8,128)(2,1)S(1)}, bf16[2208,128]{1,0:T(8,128)(2,1)S(1)}, u32[]{:S(2)}, u32[]{:S(2)}) collective-permute-start(bf16[2208,128]{1,0:T(8,128)(2,1)S(1)} %shard_map.126.refs_0_), channel_id=1, source_target_pairs={{0,96},{1,97},{2,98},{3,99},{4,100},{5,101},{6,102},{7,103},{8,104... | collective-permute-start | bytes 1695752 | tf_op jit(solution)/shard_map/ppermute | solution.py:50
  149.8 3.4 %collective-permute-start.20 = (bf16[2208,128]{1,0:T(8,128)(2,1)S(1)}, bf16[2208,128]{1,0:T(8,128)(2,1)S(1)}, u32[]{:S(2)}, u32[]{:S(2)}) collective-permute-start(bf16[2208,128]{1,0:T(8,128)(2,1)S(1)} %shard_map.126.refs_0_), channel_id=1, source_target_pairs={{0,64},{1,65},{2,66},{3,67},{4,68},{5,69},{6,70},{7,71},{8,72},{9,... | collective-permute-start | bytes 1695752 | tf_op jit(solution)/shard_map/ppermute | solution.py:50
  155.1 7.3 %collective-permute-done.21.refs_3_ = bf16[2208,128]{1,0:T(8,128)(2,1)S(1)} collective-permute-done((bf16[2208,128]{1,0:T(8,128)(2,1)S(1)}, bf16[2208,128]{1,0:T(8,128)(2,1)S(1)}, u32[]{:S(2)}, u32[]{:S(2)}) %collective-permute-start.21) | collective-permute-done | bytes 565280 | tf_op jit(solution)/shard_map/ppermute | solution.py:50
  162.4 5.3 %collective-permute-done.19.refs_1_ = bf16[2208,128]{1,0:T(8,128)(2,1)S(1)} collective-permute-done((bf16[2208,128]{1,0:T(8,128)(2,1)S(1)}, bf16[2208,128]{1,0:T(8,128)(2,1)S(1)}, u32[]{:S(2)}, u32[]{:S(2)}) %collective-permute-start.19) | collective-permute-done | bytes 565280 | tf_op jit(solution)/shard_map/ppermute | solution.py:50
  171.4 4.0 %collective-permute-start.23 = (bf16[2208,128]{1,0:T(8,128)(2,1)S(1)}, bf16[2208,128]{1,0:T(8,128)(2,1)S(1)}, u32[]{:S(2)}, u32[]{:S(2)}) collective-permute-start(bf16[2208,128]{1,0:T(8,128)(2,1)S(1)} %get-tuple-element.51), channel_id=1, source_target_pairs={{0,8},{1,9},{2,10},{3,11},{4,12},{5,13},{6,14},{7,15},{8,0},{9,1},... | collective-permute-start | bytes 1695752 | tf_op jit(solution)/shard_map/ppermute | solution.py:50
  175.5 2.9 %collective-permute-start.24 = (bf16[2208,128]{1,0:T(8,128)(2,1)S(1)}, bf16[2208,128]{1,0:T(8,128)(2,1)S(1)}, u32[]{:S(2)}, u32[]{:S(2)}) collective-permute-start(bf16[2208,128]{1,0:T(8,128)(2,1)S(1)} %get-tuple-element.52), channel_id=1, source_target_pairs={{0,12},{1,13},{2,14},{3,15},{4,0},{5,1},{6,2},{7,3},{8,4},{9,5},{1... | collective-permute-start | bytes 1695752 | tf_op jit(solution)/shard_map/ppermute | solution.py:50
  178.4 9.0 %collective-permute-done.22.refs_1_ = bf16[2208,128]{1,0:T(8,128)(2,1)S(1)} collective-permute-done((bf16[2208,128]{1,0:T(8,128)(2,1)S(1)}, bf16[2208,128]{1,0:T(8,128)(2,1)S(1)}, u32[]{:S(2)}, u32[]{:S(2)}) %collective-permute-start.22) | collective-permute-done | bytes 565280 | tf_op jit(solution)/shard_map/ppermute | solution.py:50
  190.3 4.8 %collective-permute-start.25 = (bf16[592,128]{1,0:T(8,128)(2,1)S(1)}, bf16[592,128]{1,0:T(8,128)(2,1)S(1)}, u32[]{:S(2)}, u32[]{:S(2)}) collective-permute-start(bf16[592,128]{1,0:T(8,128)(2,1)S(1)} %get-tuple-element.54), channel_id=1, source_target_pairs={{0,1},{1,2},{2,3},{3,0},{4,5},{5,6},{6,7},{7,4},{8,9},{9,10},{10,1... | collective-permute-start | bytes 454664 | tf_op jit(solution)/shard_map/ppermute | solution.py:41
  198.1 6.7 %collective-permute-start.26 = (bf16[592,128]{1,0:T(8,128)(2,1)S(1)}, bf16[592,128]{1,0:T(8,128)(2,1)S(1)}, u32[]{:S(2)}, u32[]{:S(2)}) collective-permute-start(bf16[592,128]{1,0:T(8,128)(2,1)S(1)} %shard_map.129), channel_id=1, source_target_pairs={{0,1},{1,2},{2,3},{3,0},{4,5},{5,6},{6,7},{7,4},{8,9},{9,10},{10,1... | collective-permute-start | bytes 454664 | tf_op jit(solution)/shard_map/ppermute | solution.py:41
  204.8 2.6 %collective-permute-done.26.across_ref = bf16[592,128]{1,0:T(8,128)(2,1)S(1)} collective-permute-done((bf16[592,128]{1,0:T(8,128)(2,1)S(1)}, bf16[592,128]{1,0:T(8,128)(2,1)S(1)}, u32[]{:S(2)}, u32[]{:S(2)}) %collective-permute-start.26) | collective-permute-done | bytes 151584 | tf_op jit(solution)/shard_map/ppermute | solution.py:41
  207.5 16.6 %collective-permute-start.28 = (bf16[416,128]{1,0:T(8,128)(2,1)S(1)}, bf16[416,128]{1,0:T(8,128)(2,1)S(1)}, u32[]{:S(2)}, u32[]{:S(2)}) collective-permute-start(bf16[416,128]{1,0:T(8,128)(2,1)S(1)} %get-tuple-element.58.sent_ref), channel_id=1, source_target_pairs={{0,16},{1,17},{2,18},{3,19},{4,20},{5,21},{6,22},{7,23},{8,24},{9,... | collective-permute-start | bytes 319496 | tf_op jit(solution)/shard_map/ppermute | solution.py:32
  (73 shorter events, 45.5 us)
Async XLA Ops:
  3.6 9.7 %collective-permute-start = (bf16[272,128]{1,0:T(8,128)(2,1)S(1)}, bf16[272,128]{1,0:T(8,128)(2,1)S(1)}, u32[]{:S(2)}, u32[]{:S(2)}) collective-permute-start(bf16[272,128]{1,0:T(8,128)(2,1)S(1)} %pad_maximum_fusion.1), channel_id=1, source_target_pairs={{0,16},{1,17},{2,18},{3,19},{4,20},{5,21},{6,22},{7,23},{8,24},{9,... | collective-permute-start | bytes 208904 | tf_op jit(solution)/shard_map/ppermute | solution.py:32
  13.3 9.9 %collective-permute-start.1 = (bf16[512,128]{1,0:T(8,128)(2,1)S(1)}, bf16[512,128]{1,0:T(8,128)(2,1)S(1)}, u32[]{:S(2)}, u32[]{:S(2)}) collective-permute-start(bf16[512,128]{1,0:T(8,128)(2,1)S(1)} %pad_maximum_fusion.refs_0_.both_ref), channel_id=1, source_target_pairs={{0,128},{1,129},{2,130},{3,131},{4,132},{5,133},{6,134},{7,135},{8... | collective-permute-start | bytes 393224 | tf_op jit(solution)/shard_map/ppermute | solution.py:41
  23.2 1.6 copy-start.3
  26.0 48.5 %collective-permute-start.2 = (bf16[8,256,256]{2,1,0:T(8,128)(2,1)}, bf16[8,256,256]{2,1,0:T(8,128)(2,1)S(1)}, u32[]{:S(2)}, u32[]{:S(2)}) collective-permute-start(bf16[8,256,256]{2,1,0:T(8,128)(2,1)} %get-tuple-element.67), channel_id=1, source_target_pairs={{0,16},{1,17},{2,18},{3,19},{4,20},{5,21},{6,22},{7,23},{8,24},{9,... | collective-permute-start | bytes 3145736 | tf_op jit(solution)/shard_map/ppermute | solution.py:32
  28.0 16.7 %collective-permute-start.4 = (bf16[512,128]{1,0:T(8,128)(2,1)S(1)}, bf16[512,128]{1,0:T(8,128)(2,1)S(1)}, u32[]{:S(2)}, u32[]{:S(2)}) collective-permute-start(bf16[512,128]{1,0:T(8,128)(2,1)S(1)} %pad_maximum_fusion.refs_0_.both_ref), channel_id=1, source_target_pairs={{0,384},{1,385},{2,386},{3,387},{4,388},{5,389},{6,390},{7,391},{8... | collective-permute-start | bytes 393224 | tf_op jit(solution)/shard_map/ppermute | solution.py:41
  39.8 13.0 %collective-permute-start.3 = (bf16[512,128]{1,0:T(8,128)(2,1)S(1)}, bf16[512,128]{1,0:T(8,128)(2,1)S(1)}, u32[]{:S(2)}, u32[]{:S(2)}) collective-permute-start(bf16[512,128]{1,0:T(8,128)(2,1)S(1)} %collective-permute-done.1.refs_1_), channel_id=1, source_target_pairs={{0,128},{1,129},{2,130},{3,131},{4,132},{5,133},{6,134},{7,135},{8... | collective-permute-start | bytes 393224 | tf_op jit(solution)/shard_map/ppermute | solution.py:41
  52.9 16.3 %collective-permute-start.7 = (bf16[2048,128]{1,0:T(8,128)(2,1)S(1)}, bf16[2048,128]{1,0:T(8,128)(2,1)S(1)}, u32[]{:S(2)}, u32[]{:S(2)}) collective-permute-start(bf16[2048,128]{1,0:T(8,128)(2,1)S(1)} %shard_map.120.refs_0_), channel_id=1, source_target_pairs={{0,96},{1,97},{2,98},{3,99},{4,100},{5,101},{6,102},{7,103},{8,104... | collective-permute-start | bytes 1572872 | tf_op jit(solution)/shard_map/ppermute | solution.py:50
  57.5 11.7 %collective-permute-start.6 = (bf16[2048,128]{1,0:T(8,128)(2,1)S(1)}, bf16[2048,128]{1,0:T(8,128)(2,1)S(1)}, u32[]{:S(2)}, u32[]{:S(2)}) collective-permute-start(bf16[2048,128]{1,0:T(8,128)(2,1)S(1)} %shard_map.120.refs_0_), channel_id=1, source_target_pairs={{0,64},{1,65},{2,66},{3,67},{4,68},{5,69},{6,70},{7,71},{8,72},{9,... | collective-permute-start | bytes 1572872 | tf_op jit(solution)/shard_map/ppermute | solution.py:50
  59.7 14.8 %collective-permute-start.5 = (bf16[2048,128]{1,0:T(8,128)(2,1)S(1)}, bf16[2048,128]{1,0:T(8,128)(2,1)S(1)}, u32[]{:S(2)}, u32[]{:S(2)}) collective-permute-start(bf16[2048,128]{1,0:T(8,128)(2,1)S(1)} %shard_map.120.refs_0_), channel_id=1, source_target_pairs={{0,32},{1,33},{2,34},{3,35},{4,36},{5,37},{6,38},{7,39},{8,40},{9,... | collective-permute-start | bytes 1572872 | tf_op jit(solution)/shard_map/ppermute | solution.py:50
  76.3 11.4 %collective-permute-start.8 = (bf16[2048,128]{1,0:T(8,128)(2,1)S(1)}, bf16[2048,128]{1,0:T(8,128)(2,1)S(1)}, u32[]{:S(2)}, u32[]{:S(2)}) collective-permute-start(bf16[2048,128]{1,0:T(8,128)(2,1)S(1)} %get-tuple-element.36), channel_id=1, source_target_pairs={{0,4},{1,5},{2,6},{3,7},{4,8},{5,9},{6,10},{7,11},{8,12},{9,13},{1... | collective-permute-start | bytes 1572872 | tf_op jit(solution)/shard_map/ppermute | solution.py:50
  79.4 14.6 %collective-permute-start.9 = (bf16[2048,128]{1,0:T(8,128)(2,1)S(1)}, bf16[2048,128]{1,0:T(8,128)(2,1)S(1)}, u32[]{:S(2)}, u32[]{:S(2)}) collective-permute-start(bf16[2048,128]{1,0:T(8,128)(2,1)S(1)} %get-tuple-element.37), channel_id=1, source_target_pairs={{0,8},{1,9},{2,10},{3,11},{4,12},{5,13},{6,14},{7,15},{8,0},{9,1},... | collective-permute-start | bytes 1572872 | tf_op jit(solution)/shard_map/ppermute | solution.py:50
  83.8 11.8 %collective-permute-start.10 = (bf16[2048,128]{1,0:T(8,128)(2,1)S(1)}, bf16[2048,128]{1,0:T(8,128)(2,1)S(1)}, u32[]{:S(2)}, u32[]{:S(2)}) collective-permute-start(bf16[2048,128]{1,0:T(8,128)(2,1)S(1)} %get-tuple-element.38), channel_id=1, source_target_pairs={{0,12},{1,13},{2,14},{3,15},{4,0},{5,1},{6,2},{7,3},{8,4},{9,5},{1... | collective-permute-start | bytes 1572872 | tf_op jit(solution)/shard_map/ppermute | solution.py:50
  95.9 12.4 %collective-permute-start.11 = (bf16[512,128]{1,0:T(8,128)(2,1)S(1)}, bf16[512,128]{1,0:T(8,128)(2,1)S(1)}, u32[]{:S(2)}, u32[]{:S(2)}) collective-permute-start(bf16[512,128]{1,0:T(8,128)(2,1)S(1)} %get-tuple-element.40), channel_id=1, source_target_pairs={{0,1},{1,2},{2,3},{3,0},{4,5},{5,6},{6,7},{7,4},{8,9},{9,10},{10,1... | collective-permute-start | bytes 393224 | tf_op jit(solution)/shard_map/ppermute | solution.py:41
  97.8 15.3 %collective-permute-start.13 = (bf16[512,128]{1,0:T(8,128)(2,1)S(1)}, bf16[512,128]{1,0:T(8,128)(2,1)S(1)}, u32[]{:S(2)}, u32[]{:S(2)}) collective-permute-start(bf16[512,128]{1,0:T(8,128)(2,1)S(1)} %get-tuple-element.42), channel_id=1, source_target_pairs={{0,3},{1,0},{2,1},{3,2},{4,7},{5,4},{6,5},{7,6},{8,11},{9,8},{10,9... | collective-permute-start | bytes 393224 | tf_op jit(solution)/shard_map/ppermute | solution.py:41
  108.4 2.2 copy-start
  108.4 7.6 %collective-permute-start.12 = (bf16[512,128]{1,0:T(8,128)(2,1)S(1)}, bf16[512,128]{1,0:T(8,128)(2,1)S(1)}, u32[]{:S(2)}, u32[]{:S(2)}) collective-permute-start(bf16[512,128]{1,0:T(8,128)(2,1)S(1)} %shard_map.123), channel_id=1, source_target_pairs={{0,1},{1,2},{2,3},{3,0},{4,5},{5,6},{6,7},{7,4},{8,9},{9,10},{10,1... | collective-permute-start | bytes 393224 | tf_op jit(solution)/shard_map/ppermute | solution.py:41
  110.6 10.3 %collective-permute-start.15 = (bf16[512,128]{1,0:T(8,128)(2,1)S(1)}, bf16[512,128]{1,0:T(8,128)(2,1)S(1)}, u32[]{:S(2)}, u32[]{:S(2)}) collective-permute-start(bf16[512,128]{1,0:T(8,128)(2,1)S(1)} %fusion.1), channel_id=1, source_target_pairs={{0,16},{1,17},{2,18},{3,19},{4,20},{5,21},{6,22},{7,23},{8,24},{9,... | collective-permute-start | bytes 393224 | tf_op jit(solution)/shard_map/ppermute | solution.py:32
  116.1 5.7 %copy-start.1 = (bf16[128,128]{1,0:T(8,128)(2,1)S(1)}, bf16[128,128]{1,0:T(8,128)(2,1)}, u32[]{:S(2)}) copy-start(bf16[128,128]{1,0:T(8,128)(2,1)} %weight_ref.3) | copy-start | bytes 98308
  116.1 5.7 %collective-permute-start.14 = (bf16[512,128]{1,0:T(8,128)(2,1)S(1)}, bf16[512,128]{1,0:T(8,128)(2,1)S(1)}, u32[]{:S(2)}, u32[]{:S(2)}) collective-permute-start(bf16[512,128]{1,0:T(8,128)(2,1)S(1)} %get-tuple-element.44), channel_id=1, source_target_pairs={{0,16},{1,17},{2,18},{3,19},{4,20},{5,21},{6,22},{7,23},{8,24},{9,... | collective-permute-start | bytes 393224 | tf_op jit(solution)/shard_map/ppermute | solution.py:32
  123.3 11.2 %collective-permute-start.16 = (bf16[592,128]{1,0:T(8,128)(2,1)S(1)}, bf16[592,128]{1,0:T(8,128)(2,1)S(1)}, u32[]{:S(2)}, u32[]{:S(2)}) collective-permute-start(bf16[592,128]{1,0:T(8,128)(2,1)S(1)} %get-tuple-element.48.refs_0_.both_ref), channel_id=1, source_target_pairs={{0,128},{1,129},{2,130},{3,131},{4,132},{5,133},{6,134},{7,135},{8... | collective-permute-start | bytes 454664 | tf_op jit(solution)/shard_map/ppermute | solution.py:41
  128.0 10.8 %collective-permute-start.18 = (bf16[592,128]{1,0:T(8,128)(2,1)S(1)}, bf16[592,128]{1,0:T(8,128)(2,1)S(1)}, u32[]{:S(2)}, u32[]{:S(2)}) collective-permute-start(bf16[592,128]{1,0:T(8,128)(2,1)S(1)} %get-tuple-element.48.refs_0_.both_ref), channel_id=1, source_target_pairs={{0,384},{1,385},{2,386},{3,387},{4,388},{5,389},{6,390},{7,391},{8... | collective-permute-start | bytes 454664 | tf_op jit(solution)/shard_map/ppermute | solution.py:41
  134.6 11.4 %collective-permute-start.17 = (bf16[592,128]{1,0:T(8,128)(2,1)S(1)}, bf16[592,128]{1,0:T(8,128)(2,1)S(1)}, u32[]{:S(2)}, u32[]{:S(2)}) collective-permute-start(bf16[592,128]{1,0:T(8,128)(2,1)S(1)} %collective-permute-done.16.refs_1_), channel_id=1, source_target_pairs={{0,128},{1,129},{2,130},{3,131},{4,132},{5,133},{6,134},{7,135},{8... | collective-permute-start | bytes 454664 | tf_op jit(solution)/shard_map/ppermute | solution.py:41
  146.0 16.4 %collective-permute-start.21 = (bf16[2208,128]{1,0:T(8,128)(2,1)S(1)}, bf16[2208,128]{1,0:T(8,128)(2,1)S(1)}, u32[]{:S(2)}, u32[]{:S(2)}) collective-permute-start(bf16[2208,128]{1,0:T(8,128)(2,1)S(1)} %shard_map.126.refs_0_), channel_id=1, source_target_pairs={{0,96},{1,97},{2,98},{3,99},{4,100},{5,101},{6,102},{7,103},{8,104... | collective-permute-start | bytes 1695752 | tf_op jit(solution)/shard_map/ppermute | solution.py:50
  149.8 12.6 %collective-permute-start.20 = (bf16[2208,128]{1,0:T(8,128)(2,1)S(1)}, bf16[2208,128]{1,0:T(8,128)(2,1)S(1)}, u32[]{:S(2)}, u32[]{:S(2)}) collective-permute-start(bf16[2208,128]{1,0:T(8,128)(2,1)S(1)} %shard_map.126.refs_0_), channel_id=1, source_target_pairs={{0,64},{1,65},{2,66},{3,67},{4,68},{5,69},{6,70},{7,71},{8,72},{9,... | collective-permute-start | bytes 1695752 | tf_op jit(solution)/shard_map/ppermute | solution.py:50
  153.2 14.5 %collective-permute-start.19 = (bf16[2208,128]{1,0:T(8,128)(2,1)S(1)}, bf16[2208,128]{1,0:T(8,128)(2,1)S(1)}, u32[]{:S(2)}, u32[]{:S(2)}) collective-permute-start(bf16[2208,128]{1,0:T(8,128)(2,1)S(1)} %shard_map.126.refs_0_), channel_id=1, source_target_pairs={{0,32},{1,33},{2,34},{3,35},{4,36},{5,37},{6,38},{7,39},{8,40},{9,... | collective-permute-start | bytes 1695752 | tf_op jit(solution)/shard_map/ppermute | solution.py:50
  169.5 17.9 %collective-permute-start.22 = (bf16[2208,128]{1,0:T(8,128)(2,1)S(1)}, bf16[2208,128]{1,0:T(8,128)(2,1)S(1)}, u32[]{:S(2)}, u32[]{:S(2)}) collective-permute-start(bf16[2208,128]{1,0:T(8,128)(2,1)S(1)} %get-tuple-element.50), channel_id=1, source_target_pairs={{0,4},{1,5},{2,6},{3,7},{4,8},{5,9},{6,10},{7,11},{8,12},{9,13},{1... | collective-permute-start | bytes 1695752 | tf_op jit(solution)/shard_map/ppermute | solution.py:50
  171.4 16.0 %collective-permute-start.23 = (bf16[2208,128]{1,0:T(8,128)(2,1)S(1)}, bf16[2208,128]{1,0:T(8,128)(2,1)S(1)}, u32[]{:S(2)}, u32[]{:S(2)}) collective-permute-start(bf16[2208,128]{1,0:T(8,128)(2,1)S(1)} %get-tuple-element.51), channel_id=1, source_target_pairs={{0,8},{1,9},{2,10},{3,11},{4,12},{5,13},{6,14},{7,15},{8,0},{9,1},... | collective-permute-start | bytes 1695752 | tf_op jit(solution)/shard_map/ppermute | solution.py:50
  175.5 14.5 %collective-permute-start.24 = (bf16[2208,128]{1,0:T(8,128)(2,1)S(1)}, bf16[2208,128]{1,0:T(8,128)(2,1)S(1)}, u32[]{:S(2)}, u32[]{:S(2)}) collective-permute-start(bf16[2208,128]{1,0:T(8,128)(2,1)S(1)} %get-tuple-element.52), channel_id=1, source_target_pairs={{0,12},{1,13},{2,14},{3,15},{4,0},{5,1},{6,2},{7,3},{8,4},{9,5},{1... | collective-permute-start | bytes 1695752 | tf_op jit(solution)/shard_map/ppermute | solution.py:50
  190.3 7.8 %collective-permute-start.25 = (bf16[592,128]{1,0:T(8,128)(2,1)S(1)}, bf16[592,128]{1,0:T(8,128)(2,1)S(1)}, u32[]{:S(2)}, u32[]{:S(2)}) collective-permute-start(bf16[592,128]{1,0:T(8,128)(2,1)S(1)} %get-tuple-element.54), channel_id=1, source_target_pairs={{0,1},{1,2},{2,3},{3,0},{4,5},{5,6},{6,7},{7,4},{8,9},{9,10},{10,1... | collective-permute-start | bytes 454664 | tf_op jit(solution)/shard_map/ppermute | solution.py:41
  195.1 9.7 %collective-permute-start.27 = (bf16[592,128]{1,0:T(8,128)(2,1)S(1)}, bf16[592,128]{1,0:T(8,128)(2,1)S(1)}, u32[]{:S(2)}, u32[]{:S(2)}) collective-permute-start(bf16[592,128]{1,0:T(8,128)(2,1)S(1)} %get-tuple-element.56), channel_id=1, source_target_pairs={{0,3},{1,0},{2,1},{3,2},{4,7},{5,4},{6,5},{7,6},{8,11},{9,8},{10,9... | collective-permute-start | bytes 454664 | tf_op jit(solution)/shard_map/ppermute | solution.py:41
  198.1 9.4 %collective-permute-start.26 = (bf16[592,128]{1,0:T(8,128)(2,1)S(1)}, bf16[592,128]{1,0:T(8,128)(2,1)S(1)}, u32[]{:S(2)}, u32[]{:S(2)}) collective-permute-start(bf16[592,128]{1,0:T(8,128)(2,1)S(1)} %shard_map.129), channel_id=1, source_target_pairs={{0,1},{1,2},{2,3},{3,0},{4,5},{5,6},{6,7},{7,4},{8,9},{9,10},{10,1... | collective-permute-start | bytes 454664 | tf_op jit(solution)/shard_map/ppermute | solution.py:41
  207.5 17.6 %collective-permute-start.28 = (bf16[416,128]{1,0:T(8,128)(2,1)S(1)}, bf16[416,128]{1,0:T(8,128)(2,1)S(1)}, u32[]{:S(2)}, u32[]{:S(2)}) collective-permute-start(bf16[416,128]{1,0:T(8,128)(2,1)S(1)} %get-tuple-element.58.sent_ref), channel_id=1, source_target_pairs={{0,16},{1,17},{2,18},{3,19},{4,20},{5,21},{6,22},{7,23},{8,24},{9,... | collective-permute-start | bytes 319496 | tf_op jit(solution)/shard_map/ppermute | solution.py:32
  (5 other events, 3.3 us)

commit v4 on v3

v4 whole, which is shorter than its diff:
```python
import functools
import jax
import jax.numpy as jnp
from jax import lax
from jax.experimental import pallas as pl
from jax.experimental.pallas import tpu as pltpu
from jax.sharding import PartitionSpec as P

BLOCK = 256
RING = 4
HALF = 64
LIFT = 80
AXES = ("row", "col")


def rank(zl, x, core, y, zh):
    return ((zl * RING + x) * 2 + core) * RING * RING + y * RING + zh


def pairs(step):
    out = []
    for zl in range(RING):
        for x in range(RING):
            for core in range(2):
                for y in range(RING):
                    for zh in range(RING):
                        out.append((rank(zl, x, core, y, zh), rank(*step(zl, x, core, y, zh))))
    return out


def swap_cores(v):
    return lax.ppermute(v, AXES, pairs(lambda zl, x, core, y, zh: (zl, x, 1 - core, y, zh)))


def groups(row_core, near):
    out = []
    for core in range(2):
        for free in range(RING**3):
            i, j, k = free // RING**2, free // RING % RING, free % RING
            if core == row_core:
                four = [rank(i, m, core, j, k) if near else rank(m, i, core, j, k) for m in range(RING)]
            else:
                four = [rank(i, j, core, m, k) if near else rank(i, j, core, k, m) for m in range(RING)]
            out.append(four)
    return out


def exchange(v, row_core, near):
    return lax.all_to_all(
        v, AXES, split_axis=0, concat_axis=0, tiled=True, axis_index_groups=groups(row_core, near)
    )


def call(kernel, outs, *operands, scalars=0, scratch=()):
    smem = pl.BlockSpec(memory_space=pltpu.SMEM)
    vmem = pl.BlockSpec(memory_space=pltpu.VMEM)
    return pl.pallas_call(
        kernel,
        out_shape=[jax.ShapeDtypeStruct(shape, dtype) for shape, dtype in outs],
        in_specs=[smem] * scalars + [vmem] * (len(operands) - scalars),
        out_specs=[vmem] * len(outs),
        scratch_shapes=list(scratch),
        compiler_params=pltpu.CompilerParams(vmem_limit_bytes=40 * 1024 * 1024),
    )(*operands)


def joined(ref, base, pieces):
    value = ref[base : base + LIFT].astype(jnp.float32)
    if pieces == 2:
        value = value + ref[base + LIFT : base + 2 * LIFT].astype(jnp.float32)
    return value


def put_split(refs, base, pieces, value):
    high = value.astype(jnp.bfloat16)
    low = (value - high.astype(jnp.float32)).astype(jnp.bfloat16)
    for ref in refs:
        ref[base : base + LIFT] = high
        if pieces == 2:
            ref[base + LIFT : base + 2 * LIFT] = low


def lifted_sum(ref, base, pieces):
    total = joined(ref.at[0], base, pieces)
    for k in range(1, RING):
        total = total + joined(ref.at[k], base, pieces)
    return total


def block_sum(ref, rows):
    total = ref[0, rows].astype(jnp.float32)
    for k in range(1, RING):
        total = total + ref[k, rows].astype(jnp.float32)
    return total


def join_kernel(lift, far_ref, out_ref):
    n = 2 * BLOCK
    for copy in range(RING):
        for k in range(RING):
            out_ref[copy, k * n : (k + 1) * n] = far_ref[k, :n]
    if lift:
        outs = [out_ref.at[copy] for copy in range(RING)]
        put_split(outs, RING * n, 2, lifted_sum(far_ref, n, 1))


def tile_kernel(lift, src_ref, dst_ref, weight_ref, own_ref, other_ref, near_ref, out_ref, acc_ref):
    acc_ref[...] = jnp.zeros_like(acc_ref)
    held = 2 * RING
    n = held * BLOCK
    slots = own_ref.shape[0]
    for half, tiles_ref in enumerate((own_ref, other_ref)):
        for t in range(slots):
            s = half * slots + t
            place = src_ref[s]
            row = pl.multiple_of(place % held * BLOCK, BLOCK)
            operand = near_ref[place // held, pl.ds(row, BLOCK)]
            term = jnp.dot(tiles_ref[t], operand, preferred_element_type=jnp.float32)
            acc_ref[dst_ref[s]] += weight_ref[s] * term
    for k in range(RING):
        sums = acc_ref[k * held : (k + 1) * held].astype(jnp.bfloat16)
        out_ref[k, :n] = sums.reshape(n, sums.shape[-1])
    if lift:
        outs = [out_ref.at[k] for k in range(RING)]
        put_split(outs, n, 2, lifted_sum(near_ref, n, 2))


def sum_kernel(lift, near_ref, out_ref):
    m = 2 * BLOCK
    for k in range(RING):
        out_ref[k, :m] = block_sum(near_ref, slice(k * m, (k + 1) * m)).astype(jnp.bfloat16)
    if lift:
        outs = [out_ref.at[k] for k in range(RING)]
        put_split(outs, m, 1, lifted_sum(near_ref, RING * m, 2))


def last_kernel(lift, far_ref, sums_ref, out_ref):
    m = 2 * BLOCK
    total = block_sum(far_ref, slice(0, m))
    sums_ref[...] = total
    if lift:
        out_ref[:BLOCK] = total[BLOCK:].astype(jnp.bfloat16)
        put_split([out_ref], BLOCK, 2, lifted_sum(far_ref, m, 1))
    else:
        out_ref[...] = total.astype(jnp.bfloat16)


def middle_kernel(
    core_ref, sums_ref, back_ref, both_ref, scale_ref, other_ref, weight_ref, bias_ref,
    cotangent_ref, activated_ref, out_ref,
):
    packed = other_ref[2 * BLOCK : 3 * BLOCK, :3].astype(jnp.float32)
    scales = (scale_ref[...], packed[:, 0:1] + packed[:, 1:2] + packed[:, 2:3])
    cotangents = (cotangent_ref[...], other_ref[BLOCK : 2 * BLOCK])
    grads = bias_grad = None
    for c in range(2):
        rows = slice(c * BLOCK, (c + 1) * BLOCK)
        back = back_ref[(1 - c) * BLOCK : (2 - c) * BLOCK].astype(jnp.float32)
        total = sums_ref[rows] + back + both_ref[0, rows].astype(jnp.float32)
        spread = total.astype(jnp.bfloat16)
        hidden = jnp.dot(spread, weight_ref[...], preferred_element_type=jnp.float32)
        preact = scales[c] * hidden + bias_ref[...]
        sig = jax.nn.sigmoid(preact)
        if c == 0:
            activated_ref[...] = (preact * sig).astype(jnp.bfloat16)
        delta = cotangents[c].astype(jnp.float32) * sig * (1.0 + preact * (1.0 - sig))
        scaled_delta = (scales[c] * delta).astype(jnp.bfloat16)
        for copy in range(RING):
            out_ref[copy, rows] = scaled_delta
        product = lax.dot_general(
            spread, scaled_delta, (((0,), (0,)), ((), ())), preferred_element_type=jnp.float32
        )
        column = jnp.sum(delta, axis=0, keepdims=True)
        grads = product if c == 0 else grads + product
        bias_grad = column if c == 0 else bias_grad + column
    pad = LIFT - HALF
    row = lax.broadcasted_iota(jnp.int32, (pad, grads.shape[1]), 0)
    top = jnp.concatenate([grads[:HALF], jnp.where(row == 0, bias_grad, 0.0)], axis=0)
    bottom = jnp.concatenate([grads[HALF:], jnp.zeros((pad, grads.shape[1]), jnp.float32)], axis=0)
    outs = [out_ref.at[copy] for copy in range(RING)]
    put_split(outs, 2 * BLOCK, 1, jnp.where(core_ref[0] == 0, top, bottom))


def end_kernel(
    core_ref, sums_ref, sent_ref, back_ref, both_ref, scale_ref, weight_ref,
    feature_grad_ref, weight_grad_ref, bias_grad_ref,
):
    total = sums_ref[:BLOCK] + back_ref[:BLOCK].astype(jnp.float32)
    total = total + both_ref[0, :BLOCK].astype(jnp.float32)
    proj_grad = (scale_ref[...] * total).astype(jnp.bfloat16)
    feature_grad_ref[...] = lax.dot_general(
        proj_grad, weight_ref[...], (((1,), (1,)), ((), ())), preferred_element_type=jnp.float32
    ).astype(jnp.bfloat16)
    first = core_ref[0] == 0
    here, there = joined(sent_ref, BLOCK, 2), joined(back_ref, BLOCK, 2)
    top = jnp.where(first, here, there)
    bottom = jnp.where(first, there, here)
    weight_grad_ref[:HALF] = top[:HALF]
    weight_grad_ref[HALF:] = bottom[:HALF]
    bias_grad_ref[...] = top[HALF : HALF + 1]


def shards(
    features, weight, bias, node_scale, cotangent, tile_row, tile_col, tile_count, tile_values
):
    row_pos = lax.axis_index("row")
    col_pos = lax.axis_index("col")
    core = row_pos % 2
    n_col = lax.axis_size("col")
    first = core == 0
    width = features.shape[1]

    rows_idx = tile_row[0, 0]
    cols_idx = tile_col[0, 0]
    tiles = tile_values[0, 0]
    slots = jnp.arange(rows_idx.shape[0], dtype=jnp.int32)
    same = row_pos * n_col + rows_idx == cols_idx * n_col + col_pos
    live = jnp.where(slots < tile_count[0, 0], jnp.where(same, 0.5, 1.0), 0.0)

    scale = node_scale[:, None]
    scaled = (scale * features.astype(jnp.float32)).astype(jnp.bfloat16)

    meta = jnp.stack([rows_idx.astype(jnp.float32), cols_idx.astype(jnp.float32), live])
    meta = jnp.pad(meta, ((0, 13), (0, 120))).astype(jnp.bfloat16)
    parts, packed = scale, []
    for _ in range(3):
        piece = lax.reduce_precision(parts, exponent_bits=8, mantissa_bits=7)
        packed.append(piece)
        parts = parts - piece
    packed = jnp.pad(jnp.concatenate(packed, axis=1), ((0, 0), (0, width - 3)))
    arrived = swap_cores(
        jnp.concatenate([scaled, cotangent, packed.astype(jnp.bfloat16), meta], axis=0)
    )
    tiles_other = swap_cores(tiles)
    own = jnp.where(first, tiles, jnp.swapaxes(tiles, 1, 2))
    other = jnp.where(first, tiles_other, jnp.swapaxes(tiles_other, 1, 2))
    meta_other = arrived[3 * BLOCK : 3 * BLOCK + 3, :8]
    rows_all = jnp.concatenate([rows_idx, meta_other[0].astype(jnp.int32)])
    cols_all = jnp.concatenate([cols_idx, meta_other[1].astype(jnp.int32)])
    weights = jnp.concatenate([live, meta_other[2].astype(jnp.float32)])
    foreign = jnp.concatenate([jnp.zeros_like(slots), jnp.ones_like(slots)])
    by_row = (cols_all // 2 % RING * RING + cols_all // (2 * RING)) * 2
    by_row = by_row + (cols_all % 2 != core).astype(jnp.int32)
    by_col = (rows_all // RING * RING + rows_all % RING) * 2 + foreign
    src = jnp.where(first, by_row, by_col)
    dst = jnp.where(first, by_col, by_row)
    bf16 = jnp.bfloat16

    def spread_sum(both, lift):
        n = 2 * RING * BLOCK + (2 * LIFT if lift else 0)
        (near,) = call(
            functools.partial(join_kernel, lift),
            [((RING, n, width), bf16)],
            exchange(both, 0, False),
        )
        (sums,) = call(
            functools.partial(tile_kernel, lift),
            [((RING, n, width), bf16)],
            src, dst, weights, own, other, exchange(near, 0, True),
            scalars=3,
            scratch=[pltpu.VMEM((2 * RING * RING, BLOCK, width), jnp.float32)],
        )
        (sums,) = call(
            functools.partial(sum_kernel, lift),
            [(both.shape, bf16)],
            exchange(sums, 1, True),
        )
        rows = BLOCK + 2 * LIFT if lift else 2 * BLOCK
        both_sums, sent = call(
            functools.partial(last_kernel, lift),
            [((2 * BLOCK, width), jnp.float32), ((rows, width), bf16)],
            exchange(sums, 1, False),
        )
        return both_sums, sent, swap_cores(sent)

    core_no = core.reshape(1)
    both = jnp.concatenate([scaled, arrived[:BLOCK]], axis=0)
    both = jnp.broadcast_to(both, (RING, 2 * BLOCK, width))

    sums, _, back = spread_sum(both, False)
    activated, both = call(
        middle_kernel,
        [((BLOCK, width), jnp.bfloat16), ((RING, 2 * BLOCK + LIFT, width), jnp.bfloat16)],
        core_no, sums, back, both, scale, arrived, weight, bias[None, :], cotangent,
        scalars=1,
    )
    sums, sent, back = spread_sum(both, True)
    feature_grad, weight_grad, bias_grad = call(
        end_kernel,
        [
            ((BLOCK, width), jnp.bfloat16),
            (weight.shape, jnp.float32),
            ((1, width), jnp.float32),
        ],
        core_no, sums, sent, back, both, scale, weight,
        scalars=1,
    )
    return activated, feature_grad, weight_grad, bias_grad[0]


def solution(mesh):
    placed = (
        P(AXES, None),
        P(),
        P(),
        P(AXES),
        P(AXES, None),
        P("row", "col", None),
        P("row", "col", None),
        P("row", "col"),
        P("row", "col", None, None, None),
    )
    return jax.shard_map(
        shards,
        mesh=mesh,
        in_specs=placed,
        out_specs=(P(AXES, None), P(AXES, None), P(), P()),
        check_vma=False,
    )
```

time: 227 us -> 222 us (0.978)
  blocking collectives: 0 us -> 136 us
  starting transfers between devices: 125 us -> 37.7 us
  waiting for transfers between devices: 85.7 us -> 24.7 us
  other arithmetic: 2.45 us -> 6.81 us
  Pallas kernels: 6.2 us -> 9.79 us
    all_to_all x0 -> x6, blocking collectives: none -> 136 us  [exchange(): lax.all_to_all(v, AXES, split_axis=0, concat_axis=0, tiled=True, axis_ind...]
    ppermute x24 -> x0, starting transfers between devices: 90.7 us -> none  [the longest x12 52.8 us: far_shift(): return lax.ppermute(v, AXES, pairs(step))]
    ppermute x24 -> x0, waiting for transfers between devices: 83.1 us -> none  [the longest x12 44.1 us: near_shift(): return lax.ppermute(v, AXES, pairs(step))]
    all_to_all x0 -> x2, waiting for transfers between devices: none -> 21.5 us  [exchange(): lax.all_to_all(v, AXES, split_axis=0, concat_axis=0, tiled=True, axis_ind...]
    all_to_all x0 -> x2, starting transfers between devices: none -> 13.9 us  [exchange(): lax.all_to_all(v, AXES, split_axis=0, concat_axis=0, tiled=True, axis_ind...]
    ppermute x5 -> x4, starting transfers between devices: 34.5 us -> 23.9 us  [swap_cores(): lax.ppermute(v, AXES, pairs(lambda zl, x, core, y, zh: (zl, x, 1 - core,...]
    pallas_call x12 -> x10, Pallas kernels: 6.2 us -> 9.79 us  [call(): pl.pallas_call(kernel, out_shape=[jax.ShapeDtypeStruct(shape, dtype) for...]
  transfers between devices with their start and end apart: 29 -> 6, of which waited for: 22 -> 5; matrix products, arithmetic and copies ran while one was open for 0% -> 3% of each run, Pallas kernels for 0% -> 1%
where the time goes in v4:
time: 222 us; the launch traced here: 221 us
  blocking collectives  136 us (61%)
  starting transfers between devices  37.7 us (17%)
  waiting for transfers between devices  24.7 us (11%)
  Pallas kernels  9.79 us (4%)
  other arithmetic  6.81 us (3%)
  local copies, waits for them, and re-layouts  4.49 us (2%)
    all_to_all x6, blocking collectives, exchange(): lax.all_to_all(v, AXES, split_axis=0, concat_axis=0, tiled=True, axis_ind...  136 us
    ppermute x4, starting transfers between devices, swap_cores(): lax.ppermute(v, AXES, pairs(lambda zl, x, core, y, zh: (zl, x, 1 - core,...  23.9 us
    all_to_all x2, waiting for transfers between devices, exchange(): lax.all_to_all(v, AXES, split_axis=0, concat_axis=0, tiled=True, axis_ind...  21.5 us
    all_to_all x2, starting transfers between devices, exchange(): lax.all_to_all(v, AXES, split_axis=0, concat_axis=0, tiled=True, axis_ind...  13.9 us
    pallas_call x10, Pallas kernels, call(): pl.pallas_call(kernel, out_shape=[jax.ShapeDtypeStruct(shape, dtype) for...  9.79 us
  transfers between devices with their start and end apart: 6, of which 5 were waited for; matrix products, arithmetic and copies ran while one was open for 3% of the time, Pallas kernels for 1%

profile of v4, /device:TPU:1, one launch (start us, length us, event | category | flops | bytes accessed | tf_op | source)
XLA Modules:
  0.0 220.9 jit_solution(11854751682725835212)
XLA Ops:
  1.4 0.7 reduce-precision_convert_fusion.1
  2.3 0.9 multiply_convert_fusion
  3.2 0.7 convert_bitcast_fusion
  3.9 0.7 fusion.16
  4.6 0.9 fusion.3
  5.4 8.8 %collective-permute-start = (bf16[784,128]{1,0:T(8,128)(2,1)S(1)}, bf16[784,128]{1,0:T(8,128)(2,1)S(1)}, u32[]{:S(2)}, u32[]{:S(2)}) collective-permute-start(bf16[784,128]{1,0:T(8,128)(2,1)S(1)} %fusion.3), channel_id=1, source_target_pairs={{0,16},{1,17},{2,18},{3,19},{4,20},{5,21},{6,22},{7,23},{8,24},{9,... | collective-permute-start | bytes 602120 | tf_op jit(solution)/shard_map/ppermute | solution.py:32
  14.2 1.1 collective-permute-done.other_ref
  15.3 0.9 broadcast_in_dim.33.both_ref
  16.2 9.4 %all-to-all-start = ((bf16[4,512,128]{2,1,0:T(8,128)(2,1)}), bf16[4,512,128]{2,1,0:T(8,128)(2,1)S(1)}, u32[]{:S(2)}, u32[]{:S(2)}) async-start(bf16[4,512,128]{2,1,0:T(8,128)(2,1)} %broadcast_in_dim.33.both_ref), calls=%async_computation | async-start | bytes 1048576 | tf_op jit(solution)/shard_map/all_to_all | solution.py:49
  25.6 1.3 copy.31
  26.9 1.9 collective-permute-start.1
  28.8 11.1 %all-to-all-done.far_ref = bf16[4,512,128]{2,1,0:T(8,128)(2,1)S(1)} async-done(((bf16[4,512,128]{2,1,0:T(8,128)(2,1)}), bf16[4,512,128]{2,1,0:T(8,128)(2,1)S(1)}, u32[]{:S(2)}, u32[]{:S(2)}) %all-to-all-start) | async-done | bytes 524320 | tf_op jit(solution)/shard_map/all_to_all | solution.py:49
  39.9 1.6 shard_map.120
  41.5 4.5 %all-to-all-start.1 = ((bf16[4,2048,128]{2,1,0:T(8,128)(2,1)}), bf16[4,2048,128]{2,1,0:T(8,128)(2,1)}, u32[]{:S(2)}, u32[]{:S(2)}) async-start(bf16[4,2048,128]{2,1,0:T(8,128)(2,1)} %shard_map.120), calls=%async_computation.1 | async-start | bytes 4194304 | tf_op jit(solution)/shard_map/all_to_all | solution.py:49
  46.0 1.4 bitcast_select_fusion
  48.2 1.5 copy.34
  49.6 1.3 bitcast_select_fusion.1.other_ref
  51.0 10.5 %all-to-all-done.1.near_ref = bf16[4,2048,128]{2,1,0:T(8,128)(2,1)} async-done(((bf16[4,2048,128]{2,1,0:T(8,128)(2,1)}), bf16[4,2048,128]{2,1,0:T(8,128)(2,1)}, u32[]{:S(2)}, u32[]{:S(2)}) %all-to-all-start.1) | async-done | bytes 2097184 | tf_op jit(solution)/shard_map/all_to_all | solution.py:49
  61.4 2.7 %shard_map.121 = bf16[4,2048,128]{2,1,0:T(8,128)(2,1)S(1)} custom-call(s32[16]{0:T(128)S(1)} %broadcast_select_fusion.1.src_ref, s32[16]{0:T(128)S(1)} %get-tuple-element.22.dst_ref, f32[16]{0:T(128)S(1)} %pad_maximum_fusion.2.weight_ref, bf16[8,256,256]{2,1,0:T(8,128)(2,1)S(1)} %copy.35.own_ref, bf16[8,256,256]{2,1,0:T(8,128)(2,1)S(1)} %bitcast_select_fusion.1.other_ref, ...), custom_call_target="tpu_custom_call" | custom-call | tf_op jit(solution)/shard_map/pallas_call | solution.py:57
  64.2 19.2 %all_to_all.40.near_ref = bf16[4,2048,128]{2,1,0:T(8,128)(2,1)S(1)} all-to-all(bf16[4,2048,128]{2,1,0:T(8,128)(2,1)S(1)} %shard_map.121), channel_id=1, replica_groups={{0,4,8,12},{1,5,9,13},{2,6,10,14},{3,7,11,15},{32,36,40,44},{33,37,41,4..., dimensions={0} | all-to-all | bytes 4194304 | tf_op jit(solution)/shard_map/all_to_all | solution.py:49
  83.7 27.6 %all_to_all.41.far_ref = bf16[4,512,128]{2,1,0:T(8,128)(2,1)S(1)} all-to-all(bf16[4,512,128]{2,1,0:T(8,128)(2,1)S(1)} %shard_map.122), channel_id=1, replica_groups={{0,1,2,3},{4,5,6,7},{8,9,10,11},{12,13,14,15},{32,33,34,35},{36,37,38,3..., dimensions={0} | all-to-all | bytes 1048576 | tf_op jit(solution)/shard_map/all_to_all | solution.py:49
  111.3 1.9 collective-permute-start.2
  113.4 1.2 collective-permute-done.2.back_ref
  114.6 1.9 shard_map.124
  116.5 24.6 %all_to_all.42.far_ref = bf16[4,592,128]{2,1,0:T(8,128)(2,1)S(1)} all-to-all(bf16[4,592,128]{2,1,0:T(8,128)(2,1)S(1)} %get-tuple-element.16.both_ref), channel_id=1, replica_groups={{0,128,256,384},{1,129,257,385},{2,130,258,386},{3,131,259,387},{4,132,..., dimensions={0} | all-to-all | bytes 1212416 | tf_op jit(solution)/shard_map/all_to_all | solution.py:49
  141.4 18.7 %all_to_all.43.near_ref = bf16[4,2208,128]{2,1,0:T(8,128)(2,1)S(1)} all-to-all(bf16[4,2208,128]{2,1,0:T(8,128)(2,1)S(1)} %shard_map.125), channel_id=1, replica_groups={{0,32,64,96},{1,33,65,97},{2,34,66,98},{3,35,67,99},{4,36,68,100},{5,37..., dimensions={0} | all-to-all | bytes 4521984 | tf_op jit(solution)/shard_map/all_to_all | solution.py:49
  160.1 1.7 shard_map.126
  161.8 19.0 %all_to_all.44.near_ref = bf16[4,2208,128]{2,1,0:T(8,128)(2,1)S(1)} all-to-all(bf16[4,2208,128]{2,1,0:T(8,128)(2,1)S(1)} %shard_map.126), channel_id=1, replica_groups={{0,4,8,12},{1,5,9,13},{2,6,10,14},{3,7,11,15},{32,36,40,44},{33,37,41,4..., dimensions={0} | all-to-all | bytes 4521984 | tf_op jit(solution)/shard_map/all_to_all | solution.py:49
  181.0 26.8 %all_to_all.45.far_ref = bf16[4,592,128]{2,1,0:T(8,128)(2,1)S(1)} all-to-all(bf16[4,592,128]{2,1,0:T(8,128)(2,1)S(1)} %shard_map.127), channel_id=1, replica_groups={{0,1,2,3},{4,5,6,7},{8,9,10,11},{12,13,14,15},{32,33,34,35},{36,37,38,3..., dimensions={0} | all-to-all | bytes 1212416 | tf_op jit(solution)/shard_map/all_to_all | solution.py:49
  207.9 11.2 %collective-permute-start.3 = (bf16[416,128]{1,0:T(8,128)(2,1)S(1)}, bf16[416,128]{1,0:T(8,128)(2,1)S(1)}, u32[]{:S(2)}, u32[]{:S(2)}) collective-permute-start(bf16[416,128]{1,0:T(8,128)(2,1)S(1)} %get-tuple-element.18.sent_ref), channel_id=1, source_target_pairs={{0,16},{1,17},{2,18},{3,19},{4,20},{5,21},{6,22},{7,23},{8,24},{9,... | collective-permute-start | bytes 319496 | tf_op jit(solution)/shard_map/ppermute | solution.py:32
  219.1 0.9 collective-permute-done.3.back_ref
  220.1 0.9 shard_map.129
  (37 shorter events, 2.1 us)
Async XLA Ops:
  0.6 25.0 %copy-start.3 = (bf16[1,1,8,256,256]{4,3,2,1,0:T(8,128)(2,1)S(1)}, bf16[1,1,8,256,256]{4,3,2,1,0:T(8,128)(2,1)}, u32[]{:S(2)}) copy-start(bf16[1,1,8,256,256]{4,3,2,1,0:T(8,128)(2,1)} %param.17) | copy-start | bytes 3145732
  5.4 9.8 %collective-permute-start = (bf16[784,128]{1,0:T(8,128)(2,1)S(1)}, bf16[784,128]{1,0:T(8,128)(2,1)S(1)}, u32[]{:S(2)}, u32[]{:S(2)}) collective-permute-start(bf16[784,128]{1,0:T(8,128)(2,1)S(1)} %fusion.3), channel_id=1, source_target_pairs={{0,16},{1,17},{2,18},{3,19},{4,20},{5,21},{6,22},{7,23},{8,24},{9,... | collective-permute-start | bytes 602120 | tf_op jit(solution)/shard_map/ppermute | solution.py:32
  16.2 23.7 %all-to-all-start = ((bf16[4,512,128]{2,1,0:T(8,128)(2,1)}), bf16[4,512,128]{2,1,0:T(8,128)(2,1)S(1)}, u32[]{:S(2)}, u32[]{:S(2)}) async-start(bf16[4,512,128]{2,1,0:T(8,128)(2,1)} %broadcast_in_dim.33.both_ref), calls=%async_computation | async-start | bytes 1048576 | tf_op jit(solution)/shard_map/all_to_all | solution.py:49
  26.9 21.3 %collective-permute-start.1 = (bf16[8,256,256]{1,2,0:T(8,128)(2,1)}, bf16[8,256,256]{1,2,0:T(8,128)(2,1)}, u32[]{:S(2)}, u32[]{:S(2)}) collective-permute-start(bf16[8,256,256]{1,2,0:T(8,128)(2,1)} %bitcast.10), channel_id=1, source_target_pairs={{0,16},{1,17},{2,18},{3,19},{4,20},{5,21},{6,22},{7,23},{8,24},{9,... | collective-permute-start | bytes 3145736 | tf_op jit(solution)/shard_map/ppermute | solution.py:32
  41.5 20.0 %all-to-all-start.1 = ((bf16[4,2048,128]{2,1,0:T(8,128)(2,1)}), bf16[4,2048,128]{2,1,0:T(8,128)(2,1)}, u32[]{:S(2)}, u32[]{:S(2)}) async-start(bf16[4,2048,128]{2,1,0:T(8,128)(2,1)} %shard_map.120), calls=%async_computation.1 | async-start | bytes 4194304 | tf_op jit(solution)/shard_map/all_to_all | solution.py:49
  45.9 2.0 copy-start.5
  45.9 2.0 copy-start.6
  46.0 2.1 copy-start.7
  83.4 29.9 %copy-start.4 = (f32[256]{0:T(256)S(1)}, f32[256]{0:T(256)}, u32[]{:S(2)}) copy-start(f32[256]{0:T(256)} %param.12) | copy-start | bytes 3076
  83.4 31.2 %copy-start = (bf16[256,128]{1,0:T(8,128)(2,1)S(1)}, bf16[256,128]{1,0:T(8,128)(2,1)}, u32[]{:S(2)}) copy-start(bf16[256,128]{1,0:T(8,128)(2,1)} %cotangent_ref.1) | copy-start | bytes 196612
  83.4 31.2 %copy-start.1 = (bf16[128,128]{1,0:T(8,128)(2,1)S(1)}, bf16[128,128]{1,0:T(8,128)(2,1)}, u32[]{:S(2)}) copy-start(bf16[128,128]{1,0:T(8,128)(2,1)} %weight_ref.3) | copy-start | bytes 98308
  83.4 31.2 %copy-start.2 = (f32[128]{0:T(128)S(1)}, f32[128]{0:T(128)}, u32[]{:S(2)}) copy-start(f32[128]{0:T(128)} %param.11) | copy-start | bytes 1540
  111.3 3.2 %collective-permute-start.2 = (bf16[512,128]{1,0:T(8,128)(2,1)S(1)}, bf16[512,128]{1,0:T(8,128)(2,1)S(1)}, u32[]{:S(2)}, u32[]{:S(2)}) collective-permute-start(bf16[512,128]{1,0:T(8,128)(2,1)S(1)} %get-tuple-element.14), channel_id=1, source_target_pairs={{0,16},{1,17},{2,18},{3,19},{4,20},{5,21},{6,22},{7,23},{8,24},{9,... | collective-permute-start | bytes 393224 | tf_op jit(solution)/shard_map/ppermute | solution.py:32
  207.9 12.2 %collective-permute-start.3 = (bf16[416,128]{1,0:T(8,128)(2,1)S(1)}, bf16[416,128]{1,0:T(8,128)(2,1)S(1)}, u32[]{:S(2)}, u32[]{:S(2)}) collective-permute-start(bf16[416,128]{1,0:T(8,128)(2,1)S(1)} %get-tuple-element.18.sent_ref), channel_id=1, source_target_pairs={{0,16},{1,17},{2,18},{3,19},{4,20},{5,21},{6,22},{7,23},{8,24},{9,... | collective-permute-start | bytes 319496 | tf_op jit(solution)/shard_map/ppermute | solution.py:32

commit v5 on v4

--- a/solution.py
+++ b/solution.py
@@ -32,22 +32,26 @@
     return lax.ppermute(v, AXES, pairs(lambda zl, x, core, y, zh: (zl, x, 1 - core, y, zh)))
 
 
-def groups(row_core, near):
-    out = []
+def far_shift(v, k, row_core):
+    def step(zl, x, core, y, zh):
+        if core == row_core:
+            return (zl + k) % RING, x, core, y, zh
+        return zl, x, core, y, (zh + (k if zl % 2 == 0 else -k)) % RING
+
+    return lax.ppermute(v, AXES, pairs(step))
+
+
+def near_exchange(v, row_core):
+    groups = []
     for core in range(2):
         for free in range(RING**3):
             i, j, k = free // RING**2, free // RING % RING, free % RING
             if core == row_core:
-                four = [rank(i, m, core, j, k) if near else rank(m, i, core, j, k) for m in range(RING)]
+                groups.append([rank(i, m, core, j, k) for m in range(RING)])
             else:
-                four = [rank(i, j, core, m, k) if near else rank(i, j, core, k, m) for m in range(RING)]
-            out.append(four)
-    return out
-
-
-def exchange(v, row_core, near):
+                groups.append([rank(i, j, core, m, k) for m in range(RING)])
     return lax.all_to_all(
-        v, AXES, split_axis=0, concat_axis=0, tiled=True, axis_index_groups=groups(row_core, near)
+        v, AXES, split_axis=0, concat_axis=0, tiled=True, axis_index_groups=groups
     )
 
 
@@ -80,28 +84,23 @@
             ref[base + LIFT : base + 2 * LIFT] = low
 
 
-def lifted_sum(ref, base, pieces):
-    total = joined(ref.at[0], base, pieces)
-    for k in range(1, RING):
-        total = total + joined(ref.at[k], base, pieces)
-    return total
-
-
-def block_sum(ref, rows):
-    total = ref[0, rows].astype(jnp.float32)
-    for k in range(1, RING):
-        total = total + ref[k, rows].astype(jnp.float32)
-    return total
-
-
-def join_kernel(lift, far_ref, out_ref):
+def lifted_sum(parts, base, pieces):
+    own, after, across, before = [joined(part, base, pieces) for part in parts]
+    return (own + across) + (after + before)
+
+
+def slots_of(ref):
+    return [ref.at[k] for k in range(RING)]
+
+
+def join_kernel(lift, *refs):
+    parts, out_ref = refs[:RING], refs[RING]
     n = 2 * BLOCK
     for copy in range(RING):
         for k in range(RING):
-            out_ref[copy, k * n : (k + 1) * n] = far_ref[k, :n]
-    if lift:
-        outs = [out_ref.at[copy] for copy in range(RING)]
-        put_split(outs, RING * n, 2, lifted_sum(far_ref, n, 1))
+            out_ref[copy, k * n : (k + 1) * n] = parts[k][:n]
+    if lift:
+        put_split(slots_of(out_ref), RING * n, 2, lifted_sum(parts, n, 1))
 
 
 def tile_kernel(lift, src_ref, dst_ref, weight_ref, own_ref, other_ref, near_ref, out_ref, acc_ref):
@@ -121,26 +120,42 @@
         sums = acc_ref[k * held : (k + 1) * held].astype(jnp.bfloat16)
         out_ref[k, :n] = sums.reshape(n, sums.shape[-1])
     if lift:
-        outs = [out_ref.at[k] for k in range(RING)]
-        put_split(outs, n, 2, lifted_sum(near_ref, n, 2))
-
-
-def sum_kernel(lift, near_ref, out_ref):
+        put_split(slots_of(out_ref), n, 2, lifted_sum(slots_of(near_ref), n, 2))
+
+
+def sum_kernel(lift, near_ref, mine_ref, *outs):
     m = 2 * BLOCK
     for k in range(RING):
-        out_ref[k, :m] = block_sum(near_ref, slice(k * m, (k + 1) * m)).astype(jnp.bfloat16)
-    if lift:
-        outs = [out_ref.at[k] for k in range(RING)]
-        put_split(outs, m, 1, lifted_sum(near_ref, RING * m, 2))
-
-
-def last_kernel(lift, far_ref, sums_ref, out_ref):
+        rows = slice(k * m, (k + 1) * m)
+        total = near_ref[0, rows].astype(jnp.float32)
+        for j in range(1, RING):
+            total = total + near_ref[j, rows].astype(jnp.float32)
+        if k == 0:
+            mine_ref[...] = total
+        else:
+            outs[k - 1][:m] = total.astype(jnp.bfloat16)
+    if lift:
+        put_split(outs, m, 1, lifted_sum(slots_of(near_ref), RING * m, 2))
+
+
+def relay_kernel(lift, own_ref, passing_ref, out_ref):
     m = 2 * BLOCK
-    total = block_sum(far_ref, slice(0, m))
+    total = own_ref[:m].astype(jnp.float32) + passing_ref[:m].astype(jnp.float32)
+    out_ref[:m] = total.astype(jnp.bfloat16)
+    if lift:
+        out_ref[m:] = passing_ref[m:]
+
+
+def last_kernel(lift, mine_ref, own_ref, after_ref, across_ref, before_ref, sums_ref, out_ref):
+    m = 2 * BLOCK
+    total = mine_ref[...]
+    for part in (across_ref, before_ref):
+        total = total + part[:m].astype(jnp.float32)
     sums_ref[...] = total
     if lift:
         out_ref[:BLOCK] = total[BLOCK:].astype(jnp.bfloat16)
-        put_split([out_ref], BLOCK, 2, lifted_sum(far_ref, m, 1))
+        parts = (own_ref, after_ref, across_ref, before_ref)
+        put_split([out_ref], BLOCK, 2, lifted_sum(parts, m, 1))
     else:
         out_ref[...] = total.astype(jnp.bfloat16)
 
@@ -156,7 +171,7 @@
     for c in range(2):
         rows = slice(c * BLOCK, (c + 1) * BLOCK)
         back = back_ref[(1 - c) * BLOCK : (2 - c) * BLOCK].astype(jnp.float32)
-        total = sums_ref[rows] + back + both_ref[0, rows].astype(jnp.float32)
+        total = sums_ref[rows] + back + both_ref[rows].astype(jnp.float32)
         spread = total.astype(jnp.bfloat16)
         hidden = jnp.dot(spread, weight_ref[...], preferred_element_type=jnp.float32)
         preact = scales[c] * hidden + bias_ref[...]
@@ -165,8 +180,7 @@
             activated_ref[...] = (preact * sig).astype(jnp.bfloat16)
         delta = cotangents[c].astype(jnp.float32) * sig * (1.0 + preact * (1.0 - sig))
         scaled_delta = (scales[c] * delta).astype(jnp.bfloat16)
-        for copy in range(RING):
-            out_ref[copy, rows] = scaled_delta
+        out_ref[rows] = scaled_delta
         product = lax.dot_general(
             spread, scaled_delta, (((0,), (0,)), ((), ())), preferred_element_type=jnp.float32
         )
@@ -177,8 +191,7 @@
     row = lax.broadcasted_iota(jnp.int32, (pad, grads.shape[1]), 0)
     top = jnp.concatenate([grads[:HALF], jnp.where(row == 0, bias_grad, 0.0)], axis=0)
     bottom = jnp.concatenate([grads[HALF:], jnp.zeros((pad, grads.shape[1]), jnp.float32)], axis=0)
-    outs = [out_ref.at[copy] for copy in range(RING)]
-    put_split(outs, 2 * BLOCK, 1, jnp.where(core_ref[0] == 0, top, bottom))
+    put_split([out_ref], 2 * BLOCK, 1, jnp.where(core_ref[0] == 0, top, bottom))
 
 
 def end_kernel(
@@ -186,7 +199,7 @@
     feature_grad_ref, weight_grad_ref, bias_grad_ref,
 ):
     total = sums_ref[:BLOCK] + back_ref[:BLOCK].astype(jnp.float32)
-    total = total + both_ref[0, :BLOCK].astype(jnp.float32)
+    total = total + both_ref[:BLOCK].astype(jnp.float32)
     proj_grad = (scale_ref[...] * total).astype(jnp.bfloat16)
     feature_grad_ref[...] = lax.dot_general(
         proj_grad, weight_ref[...], (((1,), (1,)), ((), ())), preferred_element_type=jnp.float32
@@ -239,48 +252,58 @@
     cols_all = jnp.concatenate([cols_idx, meta_other[1].astype(jnp.int32)])
     weights = jnp.concatenate([live, meta_other[2].astype(jnp.float32)])
     foreign = jnp.concatenate([jnp.zeros_like(slots), jnp.ones_like(slots)])
-    by_row = (cols_all // 2 % RING * RING + cols_all // (2 * RING)) * 2
-    by_row = by_row + (cols_all % 2 != core).astype(jnp.int32)
-    by_col = (rows_all // RING * RING + rows_all % RING) * 2 + foreign
-    src = jnp.where(first, by_row, by_col)
-    dst = jnp.where(first, by_col, by_row)
+    dzl = cols_all // (2 * RING) - row_pos // (2 * RING)
+    dzh = (rows_all % RING - col_pos % RING) * (1 - 2 * (row_pos // (2 * RING) % 2))
+    dcore = (cols_all % 2 != core).astype(jnp.int32)
+    in_row = cols_all // 2 % RING * 2 * RING + dcore
+    in_col = rows_all // RING * 2 * RING + foreign
+    src = jnp.where(first, in_row + jnp.mod(-dzl, RING) * 2, in_col + jnp.mod(-dzh, RING) * 2)
+    dst = jnp.where(first, in_col + jnp.mod(dzh, RING) * 2, in_row + jnp.mod(dzl, RING) * 2)
     bf16 = jnp.bfloat16
 
     def spread_sum(both, lift):
         n = 2 * RING * BLOCK + (2 * LIFT if lift else 0)
+        after = far_shift(both, 1, 0)
+        before = far_shift(both, -1, 0)
+        across = far_shift(after, 1, 0)
         (near,) = call(
             functools.partial(join_kernel, lift),
             [((RING, n, width), bf16)],
-            exchange(both, 0, False),
+            both, after, across, before,
         )
         (sums,) = call(
             functools.partial(tile_kernel, lift),
             [((RING, n, width), bf16)],
-            src, dst, weights, own, other, exchange(near, 0, True),
+            src, dst, weights, own, other, near_exchange(near, 0),
             scalars=3,
             scratch=[pltpu.VMEM((2 * RING * RING, BLOCK, width), jnp.float32)],
         )
-        (sums,) = call(
+        mine, to_after, to_across, to_before = call(
             functools.partial(sum_kernel, lift),
-            [(both.shape, bf16)],
-            exchange(sums, 1, True),
-        )
+            [((2 * BLOCK, width), jnp.float32)] + [(both.shape, bf16)] * 3,
+            near_exchange(sums, 1),
+        )
+        after = far_shift(to_across, 1, 1)
+        before = far_shift(to_before, -1, 1)
+        (passed,) = call(
+            functools.partial(relay_kernel, lift), [(both.shape, bf16)], to_after, after
+        )
+        across = far_shift(passed, 1, 1)
         rows = BLOCK + 2 * LIFT if lift else 2 * BLOCK
         both_sums, sent = call(
             functools.partial(last_kernel, lift),
             [((2 * BLOCK, width), jnp.float32), ((rows, width), bf16)],
-            exchange(sums, 1, False),
+            mine, to_after, after, across, before,
         )
         return both_sums, sent, swap_cores(sent)
 
     core_no = core.reshape(1)
     both = jnp.concatenate([scaled, arrived[:BLOCK]], axis=0)
-    both = jnp.broadcast_to(both, (RING, 2 * BLOCK, width))
 
     sums, _, back = spread_sum(both, False)
     activated, both = call(
         middle_kernel,
-        [((BLOCK, width), jnp.bfloat16), ((RING, 2 * BLOCK + LIFT, width), jnp.bfloat16)],
+        [((BLOCK, width), jnp.bfloat16), ((2 * BLOCK + LIFT, width), jnp.bfloat16)],
         core_no, sums, back, both, scale, arrived, weight, bias[None, :], cotangent,
         scalars=1,
     )

time: 222 us -> 207 us (0.932)
  blocking collectives: 136 us -> 56.7 us
  starting transfers between devices: 37.7 us -> 90 us
  waiting for transfers between devices: 24.7 us -> 37.3 us
    all_to_all x6 -> x3, blocking collectives: 136 us -> 56.7 us  [near_exchange(): lax.all_to_all(v, AXES, split_axis=0, concat_axis=0, tiled=True, axis_ind...]
    ppermute x0 -> x12, starting transfers between devices: none -> 62.5 us  [far_shift(): return lax.ppermute(v, AXES, pairs(step))]
    ppermute x0 -> x12, waiting for transfers between devices: none -> 22.7 us  [far_shift(): return lax.ppermute(v, AXES, pairs(step))]
    all_to_all x2 -> x1, waiting for transfers between devices: 21.5 us -> 11.5 us  [near_exchange(): lax.all_to_all(v, AXES, split_axis=0, concat_axis=0, tiled=True, axis_ind...]
    all_to_all x2 -> x1, starting transfers between devices: 13.9 us -> 5.14 us  [near_exchange(): lax.all_to_all(v, AXES, split_axis=0, concat_axis=0, tiled=True, axis_ind...]
    pallas_call x10 -> x12, Pallas kernels: 9.79 us -> 8.75 us  [call(): pl.pallas_call(kernel, out_shape=[jax.ShapeDtypeStruct(shape, dtype) for...]
  transfers between devices with their start and end apart: 6 -> 17, of which waited for: 5 -> 12; matrix products, arithmetic and copies ran while one was open for 3% -> 3% of each run, Pallas kernels for 1% -> 1%
where the time goes in v5:
time: 207 us; the launch traced here: 204 us
  starting transfers between devices  90 us (43%)
  blocking collectives  56.7 us (27%)
  waiting for transfers between devices  37.3 us (18%)
  Pallas kernels  8.75 us (4%)
  other arithmetic  5.45 us (3%)
  local copies, waits for them, and re-layouts  4.62 us (2%)
    ppermute x12, starting transfers between devices, far_shift(): return lax.ppermute(v, AXES, pairs(step))  62.5 us
    all_to_all x3, blocking collectives, near_exchange(): lax.all_to_all(v, AXES, split_axis=0, concat_axis=0, tiled=True, axis_ind...  56.7 us
    ppermute x12, waiting for transfers between devices, far_shift(): return lax.ppermute(v, AXES, pairs(step))  22.7 us
    ppermute x4, starting transfers between devices, swap_cores(): lax.ppermute(v, AXES, pairs(lambda zl, x, core, y, zh: (zl, x, 1 - core,...  22.3 us
    all_to_all x1, waiting for transfers between devices, near_exchange(): lax.all_to_all(v, AXES, split_axis=0, concat_axis=0, tiled=True, axis_ind...  11.5 us
    pallas_call x12, Pallas kernels, call(): pl.pallas_call(kernel, out_shape=[jax.ShapeDtypeStruct(shape, dtype) for...  8.75 us
    all_to_all x1, starting transfers between devices, near_exchange(): lax.all_to_all(v, AXES, split_axis=0, concat_axis=0, tiled=True, axis_ind...  5.14 us
  transfers between devices with their start and end apart: 17, of which 12 were waited for; matrix products, arithmetic and copies ran while one was open for 3% of the time, Pallas kernels for 1%

profile of v5, /device:TPU:1, one launch (start us, length us, event | category | flops | bytes accessed | tf_op | source)
XLA Modules:
  0.0 204.5 jit_solution(11703237964110961404)
XLA Ops:
  5.3 8.8 %collective-permute-start = (bf16[784,128]{1,0:T(8,128)(2,1)S(1)}, bf16[784,128]{1,0:T(8,128)(2,1)S(1)}, u32[]{:S(2)}, u32[]{:S(2)}) collective-permute-start(bf16[784,128]{1,0:T(8,128)(2,1)S(1)} %fusion.3), channel_id=1, source_target_pairs={{0,16},{1,17},{2,18},{3,19},{4,20},{5,21},{6,22},{7,23},{8,24},{9,... | collective-permute-start | bytes 602120 | tf_op jit(solution)/shard_map/ppermute | solution.py:32
  15.2 3.4 %collective-permute-start.2 = (bf16[512,128]{1,0:T(8,128)(2,1)S(1)}, bf16[512,128]{1,0:T(8,128)(2,1)S(1)}, u32[]{:S(2)}, u32[]{:S(2)}) collective-permute-start(bf16[512,128]{1,0:T(8,128)(2,1)S(1)} %pad_maximum_fusion.refs_0_.both_ref), channel_id=1, source_target_pairs={{0,128},{1,129},{2,130},{3,131},{4,132},{5,133},{6,134},{7,135},{8... | collective-permute-start | bytes 393224 | tf_op jit(solution)/shard_map/ppermute | solution.py:41
  18.7 5.7 %collective-permute-start.4 = (bf16[512,128]{1,0:T(8,128)(2,1)S(1)}, bf16[512,128]{1,0:T(8,128)(2,1)S(1)}, u32[]{:S(2)}, u32[]{:S(2)}) collective-permute-start(bf16[512,128]{1,0:T(8,128)(2,1)S(1)} %pad_maximum_fusion.refs_0_.both_ref), channel_id=1, source_target_pairs={{0,384},{1,385},{2,386},{3,387},{4,388},{5,389},{6,390},{7,391},{8... | collective-permute-start | bytes 393224 | tf_op jit(solution)/shard_map/ppermute | solution.py:41
  24.9 8.7 %collective-permute-start.3 = (bf16[512,128]{1,0:T(8,128)(2,1)S(1)}, bf16[512,128]{1,0:T(8,128)(2,1)S(1)}, u32[]{:S(2)}, u32[]{:S(2)}) collective-permute-start(bf16[512,128]{1,0:T(8,128)(2,1)S(1)} %collective-permute-done.2.refs_1_), channel_id=1, source_target_pairs={{0,128},{1,129},{2,130},{3,131},{4,132},{5,133},{6,134},{7,135},{8... | collective-permute-start | bytes 393224 | tf_op jit(solution)/shard_map/ppermute | solution.py:41
  33.7 1.5 copy.31
  35.2 1.9 collective-permute-start.1
  37.6 1.6 shard_map.120
  39.2 5.1 %all-to-all-start = ((bf16[4,2048,128]{2,1,0:T(8,128)(2,1)}), bf16[4,2048,128]{2,1,0:T(8,128)(2,1)}, u32[]{:S(2)}, u32[]{:S(2)}) async-start(bf16[4,2048,128]{2,1,0:T(8,128)(2,1)} %shard_map.120), calls=%async_computation | async-start | bytes 4194304 | tf_op jit(solution)/shard_map/all_to_all | solution.py:53
  45.5 1.5 copy.35.own_ref
  47.4 1.3 copy.34
  48.8 11.5 %all-to-all-done.near_ref = bf16[4,2048,128]{2,1,0:T(8,128)(2,1)} async-done(((bf16[4,2048,128]{2,1,0:T(8,128)(2,1)}), bf16[4,2048,128]{2,1,0:T(8,128)(2,1)}, u32[]{:S(2)}, u32[]{:S(2)}) %all-to-all-start) | async-done | bytes 2097184 | tf_op jit(solution)/shard_map/all_to_all | solution.py:53
  60.2 2.7 %shard_map.121 = bf16[4,2048,128]{2,1,0:T(8,128)(2,1)S(1)} custom-call(s32[16]{0:T(128)S(1)} %broadcast_select_fusion.1.src_ref, s32[16]{0:T(128)S(1)} %get-tuple-element.38.dst_ref, f32[16]{0:T(128)S(1)} %pad_maximum_fusion.2.weight_ref, bf16[8,256,256]{2,1,0:T(8,128)(2,1)S(1)} %copy.35.own_ref, bf16[8,256,256]{2,1,0:T(8,128)(2,1)S(1)} %bitcast_select_fusion.1.other_ref, ...), custom_call_target="tpu_custom_call" | custom-call | tf_op jit(solution)/shard_map/pallas_call | solution.py:61
  63.0 19.2 %all_to_all.20.near_ref = bf16[4,2048,128]{2,1,0:T(8,128)(2,1)S(1)} all-to-all(bf16[4,2048,128]{2,1,0:T(8,128)(2,1)S(1)} %shard_map.121), channel_id=1, replica_groups={{0,4,8,12},{1,5,9,13},{2,6,10,14},{3,7,11,15},{32,36,40,44},{33,37,41,4..., dimensions={0} | all-to-all | bytes 4194304 | tf_op jit(solution)/shard_map/all_to_all | solution.py:53
  82.5 4.8 %collective-permute-start.5 = (bf16[512,128]{1,0:T(8,128)(2,1)S(1)}, bf16[512,128]{1,0:T(8,128)(2,1)S(1)}, u32[]{:S(2)}, u32[]{:S(2)}) collective-permute-start(bf16[512,128]{1,0:T(8,128)(2,1)S(1)} %get-tuple-element.23), channel_id=1, source_target_pairs={{0,1},{1,2},{2,3},{3,0},{4,5},{5,6},{6,7},{7,4},{8,9},{9,10},{10,1... | collective-permute-start | bytes 393224 | tf_op jit(solution)/shard_map/ppermute | solution.py:41
  87.3 2.3 %collective-permute-start.7 = (bf16[512,128]{1,0:T(8,128)(2,1)S(1)}, bf16[512,128]{1,0:T(8,128)(2,1)S(1)}, u32[]{:S(2)}, u32[]{:S(2)}) collective-permute-start(bf16[512,128]{1,0:T(8,128)(2,1)S(1)} %get-tuple-element.24), channel_id=1, source_target_pairs={{0,3},{1,0},{2,1},{3,2},{4,7},{5,4},{6,5},{7,6},{8,11},{9,8},{10,9... | collective-permute-start | bytes 393224 | tf_op jit(solution)/shard_map/ppermute | solution.py:41
  90.0 3.0 %collective-permute-start.6 = (bf16[512,128]{1,0:T(8,128)(2,1)S(1)}, bf16[512,128]{1,0:T(8,128)(2,1)S(1)}, u32[]{:S(2)}, u32[]{:S(2)}) collective-permute-start(bf16[512,128]{1,0:T(8,128)(2,1)S(1)} %shard_map.123), channel_id=1, source_target_pairs={{0,1},{1,2},{2,3},{3,0},{4,5},{5,6},{6,7},{7,4},{8,9},{9,10},{10,1... | collective-permute-start | bytes 393224 | tf_op jit(solution)/shard_map/ppermute | solution.py:41
  93.1 7.8 %collective-permute-done.6.across_ref = bf16[512,128]{1,0:T(8,128)(2,1)S(1)} collective-permute-done((bf16[512,128]{1,0:T(8,128)(2,1)S(1)}, bf16[512,128]{1,0:T(8,128)(2,1)S(1)}, u32[]{:S(2)}, u32[]{:S(2)}) %collective-permute-start.6) | collective-permute-done | bytes 131104 | tf_op jit(solution)/shard_map/ppermute | solution.py:41
  101.0 9.7 %collective-permute-start.8 = (bf16[512,128]{1,0:T(8,128)(2,1)S(1)}, bf16[512,128]{1,0:T(8,128)(2,1)S(1)}, u32[]{:S(2)}, u32[]{:S(2)}) collective-permute-start(bf16[512,128]{1,0:T(8,128)(2,1)S(1)} %get-tuple-element.26), channel_id=1, source_target_pairs={{0,16},{1,17},{2,18},{3,19},{4,20},{5,21},{6,22},{7,23},{8,24},{9,... | collective-permute-start | bytes 393224 | tf_op jit(solution)/shard_map/ppermute | solution.py:32
  112.5 6.9 %collective-permute-start.9 = (bf16[592,128]{1,0:T(8,128)(2,1)S(1)}, bf16[592,128]{1,0:T(8,128)(2,1)S(1)}, u32[]{:S(2)}, u32[]{:S(2)}) collective-permute-start(bf16[592,128]{1,0:T(8,128)(2,1)S(1)} %get-tuple-element.28.refs_0_.both_ref), channel_id=1, source_target_pairs={{0,128},{1,129},{2,130},{3,131},{4,132},{5,133},{6,134},{7,135},{8... | collective-permute-start | bytes 454664 | tf_op jit(solution)/shard_map/ppermute | solution.py:41
  119.4 2.3 %collective-permute-start.11 = (bf16[592,128]{1,0:T(8,128)(2,1)S(1)}, bf16[592,128]{1,0:T(8,128)(2,1)S(1)}, u32[]{:S(2)}, u32[]{:S(2)}) collective-permute-start(bf16[592,128]{1,0:T(8,128)(2,1)S(1)} %get-tuple-element.28.refs_0_.both_ref), channel_id=1, source_target_pairs={{0,384},{1,385},{2,386},{3,387},{4,388},{5,389},{6,390},{7,391},{8... | collective-permute-start | bytes 454664 | tf_op jit(solution)/shard_map/ppermute | solution.py:41
  121.7 1.5 collective-permute-done.9.refs_1_
  123.2 7.7 %collective-permute-start.10 = (bf16[592,128]{1,0:T(8,128)(2,1)S(1)}, bf16[592,128]{1,0:T(8,128)(2,1)S(1)}, u32[]{:S(2)}, u32[]{:S(2)}) collective-permute-start(bf16[592,128]{1,0:T(8,128)(2,1)S(1)} %collective-permute-done.9.refs_1_), channel_id=1, source_target_pairs={{0,128},{1,129},{2,130},{3,131},{4,132},{5,133},{6,134},{7,135},{8... | collective-permute-start | bytes 454664 | tf_op jit(solution)/shard_map/ppermute | solution.py:41
  130.9 5.3 %collective-permute-done.10.refs_2_ = bf16[592,128]{1,0:T(8,128)(2,1)S(1)} collective-permute-done((bf16[592,128]{1,0:T(8,128)(2,1)S(1)}, bf16[592,128]{1,0:T(8,128)(2,1)S(1)}, u32[]{:S(2)}, u32[]{:S(2)}) %collective-permute-start.10) | collective-permute-done | bytes 151584 | tf_op jit(solution)/shard_map/ppermute | solution.py:41
  136.5 18.7 %all_to_all.21.near_ref = bf16[4,2208,128]{2,1,0:T(8,128)(2,1)S(1)} all-to-all(bf16[4,2208,128]{2,1,0:T(8,128)(2,1)S(1)} %shard_map.126), channel_id=1, replica_groups={{0,32,64,96},{1,33,65,97},{2,34,66,98},{3,35,67,99},{4,36,68,100},{5,37..., dimensions={0} | all-to-all | bytes 4521984 | tf_op jit(solution)/shard_map/all_to_all | solution.py:53
  155.1 1.7 shard_map.127
  156.9 18.8 %all_to_all.22.near_ref = bf16[4,2208,128]{2,1,0:T(8,128)(2,1)S(1)} all-to-all(bf16[4,2208,128]{2,1,0:T(8,128)(2,1)S(1)} %shard_map.127), channel_id=1, replica_groups={{0,4,8,12},{1,5,9,13},{2,6,10,14},{3,7,11,15},{32,36,40,44},{33,37,41,4..., dimensions={0} | all-to-all | bytes 4521984 | tf_op jit(solution)/shard_map/all_to_all | solution.py:53
  176.0 11.6 %collective-permute-start.12 = (bf16[592,128]{1,0:T(8,128)(2,1)S(1)}, bf16[592,128]{1,0:T(8,128)(2,1)S(1)}, u32[]{:S(2)}, u32[]{:S(2)}) collective-permute-start(bf16[592,128]{1,0:T(8,128)(2,1)S(1)} %get-tuple-element.31), channel_id=1, source_target_pairs={{0,1},{1,2},{2,3},{3,0},{4,5},{5,6},{6,7},{7,4},{8,9},{9,10},{10,1... | collective-permute-start | bytes 454664 | tf_op jit(solution)/shard_map/ppermute | solution.py:41
  187.6 1.9 collective-permute-start.14
  189.5 1.9 collective-permute-done.12.passing_ref.after_ref
  191.5 4.1 %collective-permute-start.13 = (bf16[592,128]{1,0:T(8,128)(2,1)S(1)}, bf16[592,128]{1,0:T(8,128)(2,1)S(1)}, u32[]{:S(2)}, u32[]{:S(2)}) collective-permute-start(bf16[592,128]{1,0:T(8,128)(2,1)S(1)} %shard_map.129), channel_id=1, source_target_pairs={{0,1},{1,2},{2,3},{3,0},{4,5},{5,6},{6,7},{7,4},{8,9},{9,10},{10,1... | collective-permute-start | bytes 454664 | tf_op jit(solution)/shard_map/ppermute | solution.py:41
  195.6 4.7 %collective-permute-done.13.across_ref = bf16[592,128]{1,0:T(8,128)(2,1)S(1)} collective-permute-done((bf16[592,128]{1,0:T(8,128)(2,1)S(1)}, bf16[592,128]{1,0:T(8,128)(2,1)S(1)}, u32[]{:S(2)}, u32[]{:S(2)}) %collective-permute-start.13) | collective-permute-done | bytes 151584 | tf_op jit(solution)/shard_map/ppermute | solution.py:41
  200.4 1.9 collective-permute-start.15
  (57 shorter events, 13.0 us)
Async XLA Ops:
  5.3 9.8 %collective-permute-start = (bf16[784,128]{1,0:T(8,128)(2,1)S(1)}, bf16[784,128]{1,0:T(8,128)(2,1)S(1)}, u32[]{:S(2)}, u32[]{:S(2)}) collective-permute-start(bf16[784,128]{1,0:T(8,128)(2,1)S(1)} %fusion.3), channel_id=1, source_target_pairs={{0,16},{1,17},{2,18},{3,19},{4,20},{5,21},{6,22},{7,23},{8,24},{9,... | collective-permute-start | bytes 602120 | tf_op jit(solution)/shard_map/ppermute | solution.py:32
  15.2 9.7 %collective-permute-start.2 = (bf16[512,128]{1,0:T(8,128)(2,1)S(1)}, bf16[512,128]{1,0:T(8,128)(2,1)S(1)}, u32[]{:S(2)}, u32[]{:S(2)}) collective-permute-start(bf16[512,128]{1,0:T(8,128)(2,1)S(1)} %pad_maximum_fusion.refs_0_.both_ref), channel_id=1, source_target_pairs={{0,128},{1,129},{2,130},{3,131},{4,132},{5,133},{6,134},{7,135},{8... | collective-permute-start | bytes 393224 | tf_op jit(solution)/shard_map/ppermute | solution.py:41
  18.7 18.4 %collective-permute-start.4 = (bf16[512,128]{1,0:T(8,128)(2,1)S(1)}, bf16[512,128]{1,0:T(8,128)(2,1)S(1)}, u32[]{:S(2)}, u32[]{:S(2)}) collective-permute-start(bf16[512,128]{1,0:T(8,128)(2,1)S(1)} %pad_maximum_fusion.refs_0_.both_ref), channel_id=1, source_target_pairs={{0,384},{1,385},{2,386},{3,387},{4,388},{5,389},{6,390},{7,391},{8... | collective-permute-start | bytes 393224 | tf_op jit(solution)/shard_map/ppermute | solution.py:41
  24.9 12.7 %collective-permute-start.3 = (bf16[512,128]{1,0:T(8,128)(2,1)S(1)}, bf16[512,128]{1,0:T(8,128)(2,1)S(1)}, u32[]{:S(2)}, u32[]{:S(2)}) collective-permute-start(bf16[512,128]{1,0:T(8,128)(2,1)S(1)} %collective-permute-done.2.refs_1_), channel_id=1, source_target_pairs={{0,128},{1,129},{2,130},{3,131},{4,132},{5,133},{6,134},{7,135},{8... | collective-permute-start | bytes 393224 | tf_op jit(solution)/shard_map/ppermute | solution.py:41
  35.2 12.2 %collective-permute-start.1 = (bf16[8,256,256]{1,2,0:T(8,128)(2,1)S(1)}, bf16[8,256,256]{1,2,0:T(8,128)(2,1)S(1)}, u32[]{:S(2)}, u32[]{:S(2)}) collective-permute-start(bf16[8,256,256]{1,2,0:T(8,128)(2,1)S(1)} %bitcast.43), channel_id=1, source_target_pairs={{0,16},{1,17},{2,18},{3,19},{4,20},{5,21},{6,22},{7,23},{8,24},{9,... | collective-permute-start | bytes 3145736 | tf_op jit(solution)/shard_map/ppermute | solution.py:32
  39.2 5.1 %copy-start.3 = (bf16[1,1,8,256,256]{4,3,2,1,0:T(8,128)(2,1)S(1)}, bf16[1,1,8,256,256]{4,3,2,1,0:T(8,128)(2,1)}, u32[]{:S(2)}) copy-start(bf16[1,1,8,256,256]{4,3,2,1,0:T(8,128)(2,1)} %param.17) | copy-start | bytes 3145732
  39.2 21.1 %all-to-all-start = ((bf16[4,2048,128]{2,1,0:T(8,128)(2,1)}), bf16[4,2048,128]{2,1,0:T(8,128)(2,1)}, u32[]{:S(2)}, u32[]{:S(2)}) async-start(bf16[4,2048,128]{2,1,0:T(8,128)(2,1)} %shard_map.120), calls=%async_computation | async-start | bytes 4194304 | tf_op jit(solution)/shard_map/all_to_all | solution.py:53
  44.3 2.7 %copy-start.4 = (s32[1,1,8]{2,1,0:T(1,128)S(1)}, s32[1,1,8]{2,1,0:T(1,128)}, u32[]{:S(2)}) copy-start(s32[1,1,8]{2,1,0:T(1,128)} %param.14) | copy-start | bytes 100
  44.3 2.7 %copy-start.6 = (s32[1,1,8]{2,1,0:T(1,128)S(1)}, s32[1,1,8]{2,1,0:T(1,128)}, u32[]{:S(2)}) copy-start(s32[1,1,8]{2,1,0:T(1,128)} %param.15) | copy-start | bytes 100
  44.3 2.8 %copy-start.7 = (s32[16]{0:T(128)S(1)}, s32[16]{0:T(128)}, u32[]{:S(2)}) copy-start(s32[16]{0:T(128)} %constant.134.clone.1) | copy-start | bytes 196
  82.2 28.4 %copy-start.5 = (f32[256]{0:T(256)S(1)}, f32[256]{0:T(256)}, u32[]{:S(2)}) copy-start(f32[256]{0:T(256)} %param.12) | copy-start | bytes 3076
  82.2 29.4 %copy-start = (bf16[256,128]{1,0:T(8,128)(2,1)S(1)}, bf16[256,128]{1,0:T(8,128)(2,1)}, u32[]{:S(2)}) copy-start(bf16[256,128]{1,0:T(8,128)(2,1)} %cotangent_ref.1) | copy-start | bytes 196612
  82.2 29.4 %copy-start.1 = (bf16[128,128]{1,0:T(8,128)(2,1)S(1)}, bf16[128,128]{1,0:T(8,128)(2,1)}, u32[]{:S(2)}) copy-start(bf16[128,128]{1,0:T(8,128)(2,1)} %weight_ref.3) | copy-start | bytes 98308
  82.2 29.4 %copy-start.2 = (f32[128]{0:T(128)S(1)}, f32[128]{0:T(128)}, u32[]{:S(2)}) copy-start(f32[128]{0:T(128)} %param.11) | copy-start | bytes 1540
  82.5 7.5 %collective-permute-start.5 = (bf16[512,128]{1,0:T(8,128)(2,1)S(1)}, bf16[512,128]{1,0:T(8,128)(2,1)S(1)}, u32[]{:S(2)}, u32[]{:S(2)}) collective-permute-start(bf16[512,128]{1,0:T(8,128)(2,1)S(1)} %get-tuple-element.23), channel_id=1, source_target_pairs={{0,1},{1,2},{2,3},{3,0},{4,5},{5,6},{6,7},{7,4},{8,9},{9,10},{10,1... | collective-permute-start | bytes 393224 | tf_op jit(solution)/shard_map/ppermute | solution.py:41
  87.3 5.8 %collective-permute-start.7 = (bf16[512,128]{1,0:T(8,128)(2,1)S(1)}, bf16[512,128]{1,0:T(8,128)(2,1)S(1)}, u32[]{:S(2)}, u32[]{:S(2)}) collective-permute-start(bf16[512,128]{1,0:T(8,128)(2,1)S(1)} %get-tuple-element.24), channel_id=1, source_target_pairs={{0,3},{1,0},{2,1},{3,2},{4,7},{5,4},{6,5},{7,6},{8,11},{9,8},{10,9... | collective-permute-start | bytes 393224 | tf_op jit(solution)/shard_map/ppermute | solution.py:41
  90.0 10.9 %collective-permute-start.6 = (bf16[512,128]{1,0:T(8,128)(2,1)S(1)}, bf16[512,128]{1,0:T(8,128)(2,1)S(1)}, u32[]{:S(2)}, u32[]{:S(2)}) collective-permute-start(bf16[512,128]{1,0:T(8,128)(2,1)S(1)} %shard_map.123), channel_id=1, source_target_pairs={{0,1},{1,2},{2,3},{3,0},{4,5},{5,6},{6,7},{7,4},{8,9},{9,10},{10,1... | collective-permute-start | bytes 393224 | tf_op jit(solution)/shard_map/ppermute | solution.py:41
  101.0 10.7 %collective-permute-start.8 = (bf16[512,128]{1,0:T(8,128)(2,1)S(1)}, bf16[512,128]{1,0:T(8,128)(2,1)S(1)}, u32[]{:S(2)}, u32[]{:S(2)}) collective-permute-start(bf16[512,128]{1,0:T(8,128)(2,1)S(1)} %get-tuple-element.26), channel_id=1, source_target_pairs={{0,16},{1,17},{2,18},{3,19},{4,20},{5,21},{6,22},{7,23},{8,24},{9,... | collective-permute-start | bytes 393224 | tf_op jit(solution)/shard_map/ppermute | solution.py:32
  112.5 10.7 %collective-permute-start.9 = (bf16[592,128]{1,0:T(8,128)(2,1)S(1)}, bf16[592,128]{1,0:T(8,128)(2,1)S(1)}, u32[]{:S(2)}, u32[]{:S(2)}) collective-permute-start(bf16[592,128]{1,0:T(8,128)(2,1)S(1)} %get-tuple-element.28.refs_0_.both_ref), channel_id=1, source_target_pairs={{0,128},{1,129},{2,130},{3,131},{4,132},{5,133},{6,134},{7,135},{8... | collective-permute-start | bytes 454664 | tf_op jit(solution)/shard_map/ppermute | solution.py:41
  119.4 11.5 %collective-permute-start.11 = (bf16[592,128]{1,0:T(8,128)(2,1)S(1)}, bf16[592,128]{1,0:T(8,128)(2,1)S(1)}, u32[]{:S(2)}, u32[]{:S(2)}) collective-permute-start(bf16[592,128]{1,0:T(8,128)(2,1)S(1)} %get-tuple-element.28.refs_0_.both_ref), channel_id=1, source_target_pairs={{0,384},{1,385},{2,386},{3,387},{4,388},{5,389},{6,390},{7,391},{8... | collective-permute-start | bytes 454664 | tf_op jit(solution)/shard_map/ppermute | solution.py:41
  123.2 13.0 %collective-permute-start.10 = (bf16[592,128]{1,0:T(8,128)(2,1)S(1)}, bf16[592,128]{1,0:T(8,128)(2,1)S(1)}, u32[]{:S(2)}, u32[]{:S(2)}) collective-permute-start(bf16[592,128]{1,0:T(8,128)(2,1)S(1)} %collective-permute-done.9.refs_1_), channel_id=1, source_target_pairs={{0,128},{1,129},{2,130},{3,131},{4,132},{5,133},{6,134},{7,135},{8... | collective-permute-start | bytes 454664 | tf_op jit(solution)/shard_map/ppermute | solution.py:41
  176.0 15.5 %collective-permute-start.12 = (bf16[592,128]{1,0:T(8,128)(2,1)S(1)}, bf16[592,128]{1,0:T(8,128)(2,1)S(1)}, u32[]{:S(2)}, u32[]{:S(2)}) collective-permute-start(bf16[592,128]{1,0:T(8,128)(2,1)S(1)} %get-tuple-element.31), channel_id=1, source_target_pairs={{0,1},{1,2},{2,3},{3,0},{4,5},{5,6},{6,7},{7,4},{8,9},{9,10},{10,1... | collective-permute-start | bytes 454664 | tf_op jit(solution)/shard_map/ppermute | solution.py:41
  187.6 8.0 %collective-permute-start.14 = (bf16[592,128]{1,0:T(8,128)(2,1)S(1)}, bf16[592,128]{1,0:T(8,128)(2,1)S(1)}, u32[]{:S(2)}, u32[]{:S(2)}) collective-permute-start(bf16[592,128]{1,0:T(8,128)(2,1)S(1)} %get-tuple-element.32), channel_id=1, source_target_pairs={{0,3},{1,0},{2,1},{3,2},{4,7},{5,4},{6,5},{7,6},{8,11},{9,8},{10,9... | collective-permute-start | bytes 454664 | tf_op jit(solution)/shard_map/ppermute | solution.py:41
  191.5 8.9 %collective-permute-start.13 = (bf16[592,128]{1,0:T(8,128)(2,1)S(1)}, bf16[592,128]{1,0:T(8,128)(2,1)S(1)}, u32[]{:S(2)}, u32[]{:S(2)}) collective-permute-start(bf16[592,128]{1,0:T(8,128)(2,1)S(1)} %shard_map.129), channel_id=1, source_target_pairs={{0,1},{1,2},{2,3},{3,0},{4,5},{5,6},{6,7},{7,4},{8,9},{9,10},{10,1... | collective-permute-start | bytes 454664 | tf_op jit(solution)/shard_map/ppermute | solution.py:41
  200.4 3.2 %collective-permute-start.15 = (bf16[416,128]{1,0:T(8,128)(2,1)S(1)}, bf16[416,128]{1,0:T(8,128)(2,1)S(1)}, u32[]{:S(2)}, u32[]{:S(2)}) collective-permute-start(bf16[416,128]{1,0:T(8,128)(2,1)S(1)} %get-tuple-element.34.sent_ref), channel_id=1, source_target_pairs={{0,16},{1,17},{2,18},{3,19},{4,20},{5,21},{6,22},{7,23},{8,24},{9,... | collective-permute-start | bytes 319496 | tf_op jit(solution)/shard_map/ppermute | solution.py:32

commit v6 on v5

--- a/solution.py
+++ b/solution.py
@@ -55,16 +55,16 @@
     )
 
 
-def call(kernel, outs, *operands, scalars=0, scratch=()):
+def call(kernel, outs, *operands, scalars=0, scratch=(), mebibytes=8, in_place=False):
     smem = pl.BlockSpec(memory_space=pltpu.SMEM)
-    vmem = pl.BlockSpec(memory_space=pltpu.VMEM)
+    vmem = pl.BlockSpec(memory_space=pl.ANY if in_place else pltpu.VMEM)
     return pl.pallas_call(
         kernel,
         out_shape=[jax.ShapeDtypeStruct(shape, dtype) for shape, dtype in outs],
         in_specs=[smem] * scalars + [vmem] * (len(operands) - scalars),
-        out_specs=[vmem] * len(outs),
+        out_specs=[pl.BlockSpec(memory_space=pltpu.VMEM)] * len(outs),
         scratch_shapes=list(scratch),
-        compiler_params=pltpu.CompilerParams(vmem_limit_bytes=40 * 1024 * 1024),
+        compiler_params=pltpu.CompilerParams(vmem_limit_bytes=mebibytes * 1024 * 1024),
     )(*operands)
 
 
@@ -91,6 +91,59 @@
 
 def slots_of(ref):
     return [ref.at[k] for k in range(RING)]
+
+
+def pack_kernel(*refs):
+    sources, out_ref, landed, sems = refs[:7], refs[7], refs[8:-1], refs[-1]
+    tiles_ref = sources[-1]
+    landed = landed + (out_ref.at[pl.ds(2 * BLOCK, tiles_ref.shape[0])],)
+    copies = [
+        pltpu.make_async_copy(source, target, sems.at[k])
+        for k, (source, target) in enumerate(zip(sources, landed))
+    ]
+    for copy in copies:
+        copy.start()
+    row_ref, col_ref, count_ref, features_ref, cotangent_ref, scale_ref = landed[:-1]
+    for copy in copies[:-1]:
+        copy.wait()
+    lines, width = scale_ref.shape
+    out_ref[:BLOCK, width:] = cotangent_ref[...]
+    lane = lax.broadcasted_iota(jnp.int32, (width, width), 1)
+    line = lax.broadcasted_iota(jnp.int32, (width, width), 0)
+    for half in range(lines):
+        row = scale_ref[half : half + 1]
+        scale = jnp.sum(jnp.where(lane == line, row, 0.0), axis=1, keepdims=True)
+        rows = slice(half * width, (half + 1) * width)
+        scaled = scale * features_ref[rows].astype(jnp.float32)
+        out_ref[rows, :width] = scaled.astype(jnp.bfloat16)
+        packed = jnp.zeros((width, width), jnp.float32)
+        rest = scale
+        for k in range(3):
+            piece = rest.astype(jnp.bfloat16).astype(jnp.float32)
+            packed = jnp.where(lane == k, piece, packed)
+            rest = rest - piece
+        start = BLOCK + half * width
+        out_ref[start : start + width, :width] = packed.astype(jnp.bfloat16)
+    row_pos, col_pos = lax.axis_index("row"), lax.axis_index("col")
+    n_col = lax.axis_size("col")
+    shape = (16, width)
+    lane = lax.broadcasted_iota(jnp.int32, shape, 1)
+    line = lax.broadcasted_iota(jnp.int32, shape, 0)
+    meta = jnp.zeros(shape, jnp.float32)
+    for t in range(row_ref.shape[2]):
+        i, j = row_ref[0, 0, t], col_ref[0, 0, t]
+        same = row_pos * n_col + i == j * n_col + col_pos
+        live = jnp.where(t < count_ref[0, 0], jnp.where(same, 0.5, 1.0), 0.0)
+        for k, value in enumerate((i.astype(jnp.float32), j.astype(jnp.float32), live)):
+            meta = jnp.where((line == k) & (lane == t), value, meta)
+    out_ref[BLOCK : BLOCK + 16, width:] = meta.astype(jnp.bfloat16)
+    out_ref[BLOCK + 16 : 2 * BLOCK, width:] = jnp.zeros((BLOCK - 16, width), jnp.bfloat16)
+    copies[-1].wait()
+
+
+def scale_of(facts_ref):
+    packed = facts_ref[BLOCK : 2 * BLOCK, :3].astype(jnp.float32)
+    return packed[:, 0:1] + packed[:, 1:2] + packed[:, 2:3]
 
 
 def join_kernel(lift, *refs):
@@ -103,19 +156,36 @@
         put_split(slots_of(out_ref), RING * n, 2, lifted_sum(parts, n, 1))
 
 
-def tile_kernel(lift, src_ref, dst_ref, weight_ref, own_ref, other_ref, near_ref, out_ref, acc_ref):
+def tile_kernel(
+    lift, core_ref, src_ref, dst_ref, weight_ref, own_ref, other_ref, near_ref, out_ref, acc_ref
+):
     acc_ref[...] = jnp.zeros_like(acc_ref)
     held = 2 * RING
     n = held * BLOCK
-    slots = own_ref.shape[0]
-    for half, tiles_ref in enumerate((own_ref, other_ref)):
-        for t in range(slots):
-            s = half * slots + t
-            place = src_ref[s]
-            row = pl.multiple_of(place % held * BLOCK, BLOCK)
-            operand = near_ref[place // held, pl.ds(row, BLOCK)]
-            term = jnp.dot(tiles_ref[t], operand, preferred_element_type=jnp.float32)
-            acc_ref[dst_ref[s]] += weight_ref[s] * term
+    slots = (own_ref.shape[0] - 2 * BLOCK) // BLOCK
+
+    def products(contracted):
+        for half, tiles_ref in enumerate((own_ref, other_ref)):
+            for t in range(slots):
+                s = half * slots + t
+                place = src_ref[s]
+                row = pl.multiple_of(place % held * BLOCK, BLOCK)
+                term = lax.dot_general(
+                    tiles_ref[(t + 2) * BLOCK : (t + 3) * BLOCK],
+                    near_ref[place // held, pl.ds(row, BLOCK)],
+                    (((contracted,), (0,)), ((), ())),
+                    preferred_element_type=jnp.float32,
+                )
+                acc_ref[dst_ref[s]] += weight_ref[s] * term
+
+    @pl.when(core_ref[0] == 0)
+    def _():
+        products(1)
+
+    @pl.when(core_ref[0] != 0)
+    def _():
+        products(0)
+
     for k in range(RING):
         sums = acc_ref[k * held : (k + 1) * held].astype(jnp.bfloat16)
         out_ref[k, :n] = sums.reshape(n, sums.shape[-1])
@@ -161,12 +231,12 @@
 
 
 def middle_kernel(
-    core_ref, sums_ref, back_ref, both_ref, scale_ref, other_ref, weight_ref, bias_ref,
-    cotangent_ref, activated_ref, out_ref,
+    core_ref, sums_ref, back_ref, both_ref, facts_ref, other_ref, weight_ref, bias_ref,
+    activated_ref, out_ref,
 ):
-    packed = other_ref[2 * BLOCK : 3 * BLOCK, :3].astype(jnp.float32)
-    scales = (scale_ref[...], packed[:, 0:1] + packed[:, 1:2] + packed[:, 2:3])
-    cotangents = (cotangent_ref[...], other_ref[BLOCK : 2 * BLOCK])
+    scales = (scale_of(facts_ref), scale_of(other_ref))
+    width = out_ref.shape[1]
+    cotangents = (facts_ref[:BLOCK, width:], other_ref[:BLOCK, width:])
     grads = bias_grad = None
     for c in range(2):
         rows = slice(c * BLOCK, (c + 1) * BLOCK)
@@ -195,12 +265,12 @@
 
 
 def end_kernel(
-    core_ref, sums_ref, sent_ref, back_ref, both_ref, scale_ref, weight_ref,
+    core_ref, sums_ref, sent_ref, back_ref, both_ref, facts_ref, weight_ref,
     feature_grad_ref, weight_grad_ref, bias_grad_ref,
 ):
     total = sums_ref[:BLOCK] + back_ref[:BLOCK].astype(jnp.float32)
     total = total + both_ref[:BLOCK].astype(jnp.float32)
-    proj_grad = (scale_ref[...] * total).astype(jnp.bfloat16)
+    proj_grad = (scale_of(facts_ref) * total).astype(jnp.bfloat16)
     feature_grad_ref[...] = lax.dot_general(
         proj_grad, weight_ref[...], (((1,), (1,)), ((), ())), preferred_element_type=jnp.float32
     ).astype(jnp.bfloat16)
@@ -220,6 +290,7 @@
     col_pos = lax.axis_index("col")
     core = row_pos % 2
     n_col = lax.axis_size("col")
+    core_no = core.reshape(1)
     first = core == 0
     width = features.shape[1]
 
@@ -230,24 +301,26 @@
     same = row_pos * n_col + rows_idx == cols_idx * n_col + col_pos
     live = jnp.where(slots < tile_count[0, 0], jnp.where(same, 0.5, 1.0), 0.0)
 
-    scale = node_scale[:, None]
-    scaled = (scale * features.astype(jnp.float32)).astype(jnp.bfloat16)
-
-    meta = jnp.stack([rows_idx.astype(jnp.float32), cols_idx.astype(jnp.float32), live])
-    meta = jnp.pad(meta, ((0, 13), (0, 120))).astype(jnp.bfloat16)
-    parts, packed = scale, []
-    for _ in range(3):
-        piece = lax.reduce_precision(parts, exponent_bits=8, mantissa_bits=7)
-        packed.append(piece)
-        parts = parts - piece
-    packed = jnp.pad(jnp.concatenate(packed, axis=1), ((0, 0), (0, width - 3)))
-    arrived = swap_cores(
-        jnp.concatenate([scaled, cotangent, packed.astype(jnp.bfloat16), meta], axis=0)
-    )
-    tiles_other = swap_cores(tiles)
-    own = jnp.where(first, tiles, jnp.swapaxes(tiles, 1, 2))
-    other = jnp.where(first, tiles_other, jnp.swapaxes(tiles_other, 1, 2))
-    meta_other = arrived[3 * BLOCK : 3 * BLOCK + 3, :8]
+    (facts,) = call(
+        pack_kernel,
+        [((2 * BLOCK + tiles.shape[0] * BLOCK, BLOCK), jnp.bfloat16)],
+        tile_row, tile_col, tile_count, features, cotangent, node_scale.reshape(2, -1),
+        tiles.reshape(-1, BLOCK),
+        scratch=[
+            pltpu.SMEM(tile_row.shape, jnp.int32),
+            pltpu.SMEM(tile_col.shape, jnp.int32),
+            pltpu.SMEM(tile_count.shape, jnp.int32),
+            pltpu.VMEM(features.shape, jnp.bfloat16),
+            pltpu.VMEM(cotangent.shape, jnp.bfloat16),
+            pltpu.VMEM((2, width), jnp.float32),
+            pltpu.SemaphoreType.DMA((7,)),
+        ],
+        mebibytes=60,
+        in_place=True,
+    )
+    arrived = swap_cores(facts)
+    meta_other = arrived[BLOCK : BLOCK + 3, width : width + tiles.shape[0]]
+
     rows_all = jnp.concatenate([rows_idx, meta_other[0].astype(jnp.int32)])
     cols_all = jnp.concatenate([cols_idx, meta_other[1].astype(jnp.int32)])
     weights = jnp.concatenate([live, meta_other[2].astype(jnp.float32)])
@@ -274,9 +347,10 @@
         (sums,) = call(
             functools.partial(tile_kernel, lift),
             [((RING, n, width), bf16)],
-            src, dst, weights, own, other, near_exchange(near, 0),
-            scalars=3,
+            core_no, src, dst, weights, facts, arrived, near_exchange(near, 0),
+            scalars=4,
             scratch=[pltpu.VMEM((2 * RING * RING, BLOCK, width), jnp.float32)],
+            mebibytes=20,
         )
         mine, to_after, to_across, to_before = call(
             functools.partial(sum_kernel, lift),
@@ -297,14 +371,13 @@
         )
         return both_sums, sent, swap_cores(sent)
 
-    core_no = core.reshape(1)
-    both = jnp.concatenate([scaled, arrived[:BLOCK]], axis=0)
+    both = jnp.concatenate([facts[:BLOCK, :width], arrived[:BLOCK, :width]], axis=0)
 
     sums, _, back = spread_sum(both, False)
     activated, both = call(
         middle_kernel,
         [((BLOCK, width), jnp.bfloat16), ((2 * BLOCK + LIFT, width), jnp.bfloat16)],
-        core_no, sums, back, both, scale, arrived, weight, bias[None, :], cotangent,
+        core_no, sums, back, both, facts, arrived, weight, bias[None, :],
         scalars=1,
     )
     sums, sent, back = spread_sum(both, True)
@@ -315,7 +388,7 @@
             (weight.shape, jnp.float32),
             ((1, width), jnp.float32),
         ],
-        core_no, sums, sent, back, both, scale, weight,
+        core_no, sums, sent, back, both, facts, weight,
         scalars=1,
     )
     return activated, feature_grad, weight_grad, bias_grad[0]

time: 207 us -> 206 us (level)
  waiting for transfers between devices: 37.3 us -> 48.8 us
  starting transfers between devices: 90 us -> 84.3 us
  other arithmetic: 5.45 us -> 0.29 us
  local copies, waits for them, and re-layouts: 4.62 us -> 2.18 us
    ppermute x12, starting transfers between devices: 62.5 us -> 53.8 us  [far_shift(): return lax.ppermute(v, AXES, pairs(step))]
    ppermute x12, waiting for transfers between devices: 22.7 us -> 29.6 us  [far_shift(): return lax.ppermute(v, AXES, pairs(step))]
    all_to_all x1, waiting for transfers between devices: 11.5 us -> 15.4 us  [near_exchange(): lax.all_to_all(v, AXES, split_axis=0, concat_axis=0, tiled=True, axis_ind...]
    ppermute x4 -> x3, starting transfers between devices: 22.3 us -> 25.3 us  [swap_cores(): lax.ppermute(v, AXES, pairs(lambda zl, x, core, y, zh: (zl, x, 1 - core,...]
    pallas_call x12 -> x13, Pallas kernels: 8.75 us -> 10.2 us  [call(): pl.pallas_call(kernel, out_shape=[jax.ShapeDtypeStruct(shape, dtype) for...]
  transfers between devices with their start and end apart: 17 -> 16, of which waited for: 12 -> 14; matrix products, arithmetic and copies ran while one was open for 3% -> 1% of each run, Pallas kernels for 1% -> 0%
where the time goes in v6:
time: 206 us; the launch traced here: 205 us
  starting transfers between devices  84.3 us (41%)
  blocking collectives  57.7 us (28%)
  waiting for transfers between devices  48.8 us (24%)
  Pallas kernels  10.2 us (5%)
  local copies, waits for them, and re-layouts  2.18 us (1%)
    all_to_all x3, blocking collectives, near_exchange(): lax.all_to_all(v, AXES, split_axis=0, concat_axis=0, tiled=True, axis_ind...  57.7 us
    ppermute x12, starting transfers between devices, far_shift(): return lax.ppermute(v, AXES, pairs(step))  53.8 us
    ppermute x12, waiting for transfers between devices, far_shift(): return lax.ppermute(v, AXES, pairs(step))  29.6 us
    ppermute x3, starting transfers between devices, swap_cores(): lax.ppermute(v, AXES, pairs(lambda zl, x, core, y, zh: (zl, x, 1 - core,...  25.3 us
    all_to_all x1, waiting for transfers between devices, near_exchange(): lax.all_to_all(v, AXES, split_axis=0, concat_axis=0, tiled=True, axis_ind...  15.4 us
    pallas_call x13, Pallas kernels, call(): pl.pallas_call(kernel, out_shape=[jax.ShapeDtypeStruct(shape, dtype) for...  10.2 us
    all_to_all x1, starting transfers between devices, near_exchange(): lax.all_to_all(v, AXES, split_axis=0, concat_axis=0, tiled=True, axis_ind...  5.15 us
  transfers between devices with their start and end apart: 16, of which 14 were waited for; matrix products, arithmetic and copies ran while one was open for 1% of the time, Pallas kernels for 0%

profile of v6, /device:TPU:1, one launch (start us, length us, event | category | flops | bytes accessed | tf_op | source)
XLA Modules:
  0.0 204.9 jit_solution(10449028455080409647)
XLA Ops:
  1.3 2.5 %shard_map.120.own_ref.facts_ref = bf16[2560,256]{1,0:T(8,128)(2,1)} custom-call(s32[1,1,8]{2,1,0:T(1,128)} %refs_0_.1, s32[1,1,8]{2,1,0:T(1,128)} %refs_1_.1, s32[1,1]{1,0:T(1,128)} %copy.13.refs_2_, bf16[256,128]{1,0:T(8,128)(2,1)} %refs_3_.1, bf16[256,128]{1,0:T(8,128)(2,1)} %refs_4_.1, f32[2,128]{1,0:T(2,128)} %bitcast.31, bf16[2048,256]{1,0:T(8,128)(2,1)} %bitcast.27), custom_call_target="tpu_custom_call" | custom-call | tf_op jit(solution)/shard_map/pallas_call | solution.py:61
  3.8 8.8 %collective-permute-start = (bf16[2560,256]{1,0:T(8,128)(2,1)}, bf16[2560,256]{1,0:T(8,128)(2,1)S(1)}, u32[]{:S(2)}, u32[]{:S(2)}) collective-permute-start(bf16[2560,256]{1,0:T(8,128)(2,1)} %shard_map.120.own_ref.facts_ref), channel_id=1, source_target_pairs={{0,16},{1,17},{2,18},{3,19},{4,20},{5,21},{6,22},{7,23},{8,24},{9,... | collective-permute-start | bytes 3932168 | tf_op jit(solution)/shard_map/ppermute | solution.py:32
  13.4 2.0 collective-permute-done.other_ref
  15.4 3.4 %collective-permute-start.1 = (bf16[512,128]{1,0:T(8,128)(2,1)S(1)}, bf16[512,128]{1,0:T(8,128)(2,1)S(1)}, u32[]{:S(2)}, u32[]{:S(2)}) collective-permute-start(bf16[512,128]{1,0:T(8,128)(2,1)S(1)} %pad_maximum_fusion.refs_0_.both_ref), channel_id=1, source_target_pairs={{0,128},{1,129},{2,130},{3,131},{4,132},{5,133},{6,134},{7,135},{8... | collective-permute-start | bytes 393224 | tf_op jit(solution)/shard_map/ppermute | solution.py:41
  18.9 5.7 %collective-permute-start.3 = (bf16[512,128]{1,0:T(8,128)(2,1)S(1)}, bf16[512,128]{1,0:T(8,128)(2,1)S(1)}, u32[]{:S(2)}, u32[]{:S(2)}) collective-permute-start(bf16[512,128]{1,0:T(8,128)(2,1)S(1)} %pad_maximum_fusion.refs_0_.both_ref), channel_id=1, source_target_pairs={{0,384},{1,385},{2,386},{3,387},{4,388},{5,389},{6,390},{7,391},{8... | collective-permute-start | bytes 393224 | tf_op jit(solution)/shard_map/ppermute | solution.py:41
  25.2 8.7 %collective-permute-start.2 = (bf16[512,128]{1,0:T(8,128)(2,1)S(1)}, bf16[512,128]{1,0:T(8,128)(2,1)S(1)}, u32[]{:S(2)}, u32[]{:S(2)}) collective-permute-start(bf16[512,128]{1,0:T(8,128)(2,1)S(1)} %collective-permute-done.1.refs_1_), channel_id=1, source_target_pairs={{0,128},{1,129},{2,130},{3,131},{4,132},{5,133},{6,134},{7,135},{8... | collective-permute-start | bytes 393224 | tf_op jit(solution)/shard_map/ppermute | solution.py:41
  33.9 3.9 %collective-permute-done.2.refs_2_ = bf16[512,128]{1,0:T(8,128)(2,1)S(1)} collective-permute-done((bf16[512,128]{1,0:T(8,128)(2,1)S(1)}, bf16[512,128]{1,0:T(8,128)(2,1)S(1)}, u32[]{:S(2)}, u32[]{:S(2)}) %collective-permute-start.2) | collective-permute-done | bytes 131104 | tf_op jit(solution)/shard_map/ppermute | solution.py:41
  39.4 5.2 %all-to-all-start = ((bf16[4,2048,128]{2,1,0:T(8,128)(2,1)}), bf16[4,2048,128]{2,1,0:T(8,128)(2,1)}, u32[]{:S(2)}, u32[]{:S(2)}) async-start(bf16[4,2048,128]{2,1,0:T(8,128)(2,1)} %copy-done.1), calls=%async_computation | async-start | bytes 4194304 | tf_op jit(solution)/shard_map/all_to_all | solution.py:53
  44.8 15.4 %all-to-all-done.near_ref = bf16[4,2048,128]{2,1,0:T(8,128)(2,1)} async-done(((bf16[4,2048,128]{2,1,0:T(8,128)(2,1)}), bf16[4,2048,128]{2,1,0:T(8,128)(2,1)}, u32[]{:S(2)}, u32[]{:S(2)}) %all-to-all-start) | async-done | bytes 2097184 | tf_op jit(solution)/shard_map/all_to_all | solution.py:53
  60.2 2.8 %shard_map.122 = bf16[4,2048,128]{2,1,0:T(8,128)(2,1)S(1)} custom-call(s32[1]{0:T(128)} %bitcast.core_ref, s32[16]{0:T(128)S(1)} %broadcast_select_fusion.1.src_ref, s32[16]{0:T(128)S(1)} %get-tuple-element.38.dst_ref, f32[16]{0:T(128)S(1)} %pad_maximum_fusion.1.weight_ref, bf16[2560,256]{1,0:T(8,128)(2,1)S(1)} %copy-done, ...), custom_call_target="tpu_custom_call" | custom-call | tf_op jit(solution)/shard_map/pallas_call | solution.py:61
  63.0 19.2 %all_to_all.20.near_ref = bf16[4,2048,128]{2,1,0:T(8,128)(2,1)S(1)} all-to-all(bf16[4,2048,128]{2,1,0:T(8,128)(2,1)S(1)} %shard_map.122), channel_id=1, replica_groups={{0,4,8,12},{1,5,9,13},{2,6,10,14},{3,7,11,15},{32,36,40,44},{33,37,41,4..., dimensions={0} | all-to-all | bytes 4194304 | tf_op jit(solution)/shard_map/all_to_all | solution.py:53
  82.5 4.3 %collective-permute-start.4 = (bf16[512,128]{1,0:T(8,128)(2,1)S(1)}, bf16[512,128]{1,0:T(8,128)(2,1)S(1)}, u32[]{:S(2)}, u32[]{:S(2)}) collective-permute-start(bf16[512,128]{1,0:T(8,128)(2,1)S(1)} %get-tuple-element.23), channel_id=1, source_target_pairs={{0,1},{1,2},{2,3},{3,0},{4,5},{5,6},{6,7},{7,4},{8,9},{9,10},{10,1... | collective-permute-start | bytes 393224 | tf_op jit(solution)/shard_map/ppermute | solution.py:41
  86.8 2.8 %collective-permute-start.6 = (bf16[512,128]{1,0:T(8,128)(2,1)S(1)}, bf16[512,128]{1,0:T(8,128)(2,1)S(1)}, u32[]{:S(2)}, u32[]{:S(2)}) collective-permute-start(bf16[512,128]{1,0:T(8,128)(2,1)S(1)} %get-tuple-element.24), channel_id=1, source_target_pairs={{0,3},{1,0},{2,1},{3,2},{4,7},{5,4},{6,5},{7,6},{8,11},{9,8},{10,9... | collective-permute-start | bytes 393224 | tf_op jit(solution)/shard_map/ppermute | solution.py:41
  90.3 3.0 %collective-permute-start.5 = (bf16[512,128]{1,0:T(8,128)(2,1)S(1)}, bf16[512,128]{1,0:T(8,128)(2,1)S(1)}, u32[]{:S(2)}, u32[]{:S(2)}) collective-permute-start(bf16[512,128]{1,0:T(8,128)(2,1)S(1)} %shard_map.124), channel_id=1, source_target_pairs={{0,1},{1,2},{2,3},{3,0},{4,5},{5,6},{6,7},{7,4},{8,9},{9,10},{10,1... | collective-permute-start | bytes 393224 | tf_op jit(solution)/shard_map/ppermute | solution.py:41
  93.4 2.4 %collective-permute-done.6.before_ref = bf16[512,128]{1,0:T(8,128)(2,1)S(1)} collective-permute-done((bf16[512,128]{1,0:T(8,128)(2,1)S(1)}, bf16[512,128]{1,0:T(8,128)(2,1)S(1)}, u32[]{:S(2)}, u32[]{:S(2)}) %collective-permute-start.6) | collective-permute-done | bytes 131104 | tf_op jit(solution)/shard_map/ppermute | solution.py:41
  95.8 4.3 %collective-permute-done.5.across_ref = bf16[512,128]{1,0:T(8,128)(2,1)S(1)} collective-permute-done((bf16[512,128]{1,0:T(8,128)(2,1)S(1)}, bf16[512,128]{1,0:T(8,128)(2,1)S(1)}, u32[]{:S(2)}, u32[]{:S(2)}) %collective-permute-start.5) | collective-permute-done | bytes 131104 | tf_op jit(solution)/shard_map/ppermute | solution.py:41
  100.1 6.1 %collective-permute-start.7 = (bf16[512,128]{1,0:T(8,128)(2,1)S(1)}, bf16[512,128]{1,0:T(8,128)(2,1)S(1)}, u32[]{:S(2)}, u32[]{:S(2)}) collective-permute-start(bf16[512,128]{1,0:T(8,128)(2,1)S(1)} %get-tuple-element.26), channel_id=1, source_target_pairs={{0,16},{1,17},{2,18},{3,19},{4,20},{5,21},{6,22},{7,23},{8,24},{9,... | collective-permute-start | bytes 393224 | tf_op jit(solution)/shard_map/ppermute | solution.py:32
  108.2 7.7 %collective-permute-start.8 = (bf16[592,128]{1,0:T(8,128)(2,1)S(1)}, bf16[592,128]{1,0:T(8,128)(2,1)S(1)}, u32[]{:S(2)}, u32[]{:S(2)}) collective-permute-start(bf16[592,128]{1,0:T(8,128)(2,1)S(1)} %get-tuple-element.28.refs_0_.both_ref), channel_id=1, source_target_pairs={{0,128},{1,129},{2,130},{3,131},{4,132},{5,133},{6,134},{7,135},{8... | collective-permute-start | bytes 454664 | tf_op jit(solution)/shard_map/ppermute | solution.py:41
  115.9 2.2 %collective-permute-start.10 = (bf16[592,128]{1,0:T(8,128)(2,1)S(1)}, bf16[592,128]{1,0:T(8,128)(2,1)S(1)}, u32[]{:S(2)}, u32[]{:S(2)}) collective-permute-start(bf16[592,128]{1,0:T(8,128)(2,1)S(1)} %get-tuple-element.28.refs_0_.both_ref), channel_id=1, source_target_pairs={{0,384},{1,385},{2,386},{3,387},{4,388},{5,389},{6,390},{7,391},{8... | collective-permute-start | bytes 454664 | tf_op jit(solution)/shard_map/ppermute | solution.py:41
  118.1 3.4 %collective-permute-done.8.refs_1_ = bf16[592,128]{1,0:T(8,128)(2,1)S(1)} collective-permute-done((bf16[592,128]{1,0:T(8,128)(2,1)S(1)}, bf16[592,128]{1,0:T(8,128)(2,1)S(1)}, u32[]{:S(2)}, u32[]{:S(2)}) %collective-permute-start.8) | collective-permute-done | bytes 151584 | tf_op jit(solution)/shard_map/ppermute | solution.py:41
  121.5 6.9 %collective-permute-start.9 = (bf16[592,128]{1,0:T(8,128)(2,1)S(1)}, bf16[592,128]{1,0:T(8,128)(2,1)S(1)}, u32[]{:S(2)}, u32[]{:S(2)}) collective-permute-start(bf16[592,128]{1,0:T(8,128)(2,1)S(1)} %collective-permute-done.8.refs_1_), channel_id=1, source_target_pairs={{0,128},{1,129},{2,130},{3,131},{4,132},{5,133},{6,134},{7,135},{8... | collective-permute-start | bytes 454664 | tf_op jit(solution)/shard_map/ppermute | solution.py:41
  128.4 4.3 %collective-permute-done.9.refs_2_ = bf16[592,128]{1,0:T(8,128)(2,1)S(1)} collective-permute-done((bf16[592,128]{1,0:T(8,128)(2,1)S(1)}, bf16[592,128]{1,0:T(8,128)(2,1)S(1)}, u32[]{:S(2)}, u32[]{:S(2)}) %collective-permute-start.9) | collective-permute-done | bytes 151584 | tf_op jit(solution)/shard_map/ppermute | solution.py:41
  133.0 19.8 %all_to_all.21.near_ref = bf16[4,2208,128]{2,1,0:T(8,128)(2,1)S(1)} all-to-all(bf16[4,2208,128]{2,1,0:T(8,128)(2,1)S(1)} %shard_map.127), channel_id=1, replica_groups={{0,32,64,96},{1,33,65,97},{2,34,66,98},{3,35,67,99},{4,36,68,100},{5,37..., dimensions={0} | all-to-all | bytes 4521984 | tf_op jit(solution)/shard_map/all_to_all | solution.py:53
  152.7 1.8 shard_map.128
  154.6 18.7 %all_to_all.22.near_ref = bf16[4,2208,128]{2,1,0:T(8,128)(2,1)S(1)} all-to-all(bf16[4,2208,128]{2,1,0:T(8,128)(2,1)S(1)} %shard_map.128), channel_id=1, replica_groups={{0,4,8,12},{1,5,9,13},{2,6,10,14},{3,7,11,15},{32,36,40,44},{33,37,41,4..., dimensions={0} | all-to-all | bytes 4521984 | tf_op jit(solution)/shard_map/all_to_all | solution.py:53
  173.5 1.9 collective-permute-start.11
  175.5 5.2 %collective-permute-start.13 = (bf16[592,128]{1,0:T(8,128)(2,1)S(1)}, bf16[592,128]{1,0:T(8,128)(2,1)S(1)}, u32[]{:S(2)}, u32[]{:S(2)}) collective-permute-start(bf16[592,128]{1,0:T(8,128)(2,1)S(1)} %get-tuple-element.32), channel_id=1, source_target_pairs={{0,3},{1,0},{2,1},{3,2},{4,7},{5,4},{6,5},{7,6},{8,11},{9,8},{10,9... | collective-permute-start | bytes 454664 | tf_op jit(solution)/shard_map/ppermute | solution.py:41
  180.6 1.9 collective-permute-done.11.passing_ref.after_ref
  182.5 1.9 collective-permute-start.12
  184.5 3.5 %collective-permute-done.13.before_ref = bf16[592,128]{1,0:T(8,128)(2,1)S(1)} collective-permute-done((bf16[592,128]{1,0:T(8,128)(2,1)S(1)}, bf16[592,128]{1,0:T(8,128)(2,1)S(1)}, u32[]{:S(2)}, u32[]{:S(2)}) %collective-permute-start.13) | collective-permute-done | bytes 151584 | tf_op jit(solution)/shard_map/ppermute | solution.py:41
  187.9 4.7 %collective-permute-done.12.across_ref = bf16[592,128]{1,0:T(8,128)(2,1)S(1)} collective-permute-done((bf16[592,128]{1,0:T(8,128)(2,1)S(1)}, bf16[592,128]{1,0:T(8,128)(2,1)S(1)}, u32[]{:S(2)}, u32[]{:S(2)}) %collective-permute-start.12) | collective-permute-done | bytes 151584 | tf_op jit(solution)/shard_map/ppermute | solution.py:41
  192.7 10.3 %collective-permute-start.14 = (bf16[416,128]{1,0:T(8,128)(2,1)S(1)}, bf16[416,128]{1,0:T(8,128)(2,1)S(1)}, u32[]{:S(2)}, u32[]{:S(2)}) collective-permute-start(bf16[416,128]{1,0:T(8,128)(2,1)S(1)} %get-tuple-element.34.sent_ref), channel_id=1, source_target_pairs={{0,16},{1,17},{2,18},{3,19},{4,20},{5,21},{6,22},{7,23},{8,24},{9,... | collective-permute-start | bytes 319496 | tf_op jit(solution)/shard_map/ppermute | solution.py:32
  (38 shorter events, 8.6 us)
Async XLA Ops:
  3.8 11.6 %collective-permute-start = (bf16[2560,256]{1,0:T(8,128)(2,1)}, bf16[2560,256]{1,0:T(8,128)(2,1)S(1)}, u32[]{:S(2)}, u32[]{:S(2)}) collective-permute-start(bf16[2560,256]{1,0:T(8,128)(2,1)} %shard_map.120.own_ref.facts_ref), channel_id=1, source_target_pairs={{0,16},{1,17},{2,18},{3,19},{4,20},{5,21},{6,22},{7,23},{8,24},{9,... | collective-permute-start | bytes 3932168 | tf_op jit(solution)/shard_map/ppermute | solution.py:32
  15.4 9.7 %collective-permute-start.1 = (bf16[512,128]{1,0:T(8,128)(2,1)S(1)}, bf16[512,128]{1,0:T(8,128)(2,1)S(1)}, u32[]{:S(2)}, u32[]{:S(2)}) collective-permute-start(bf16[512,128]{1,0:T(8,128)(2,1)S(1)} %pad_maximum_fusion.refs_0_.both_ref), channel_id=1, source_target_pairs={{0,128},{1,129},{2,130},{3,131},{4,132},{5,133},{6,134},{7,135},{8... | collective-permute-start | bytes 393224 | tf_op jit(solution)/shard_map/ppermute | solution.py:41
  18.9 15.0 %collective-permute-start.3 = (bf16[512,128]{1,0:T(8,128)(2,1)S(1)}, bf16[512,128]{1,0:T(8,128)(2,1)S(1)}, u32[]{:S(2)}, u32[]{:S(2)}) collective-permute-start(bf16[512,128]{1,0:T(8,128)(2,1)S(1)} %pad_maximum_fusion.refs_0_.both_ref), channel_id=1, source_target_pairs={{0,384},{1,385},{2,386},{3,387},{4,388},{5,389},{6,390},{7,391},{8... | collective-permute-start | bytes 393224 | tf_op jit(solution)/shard_map/ppermute | solution.py:41
  25.2 12.7 %collective-permute-start.2 = (bf16[512,128]{1,0:T(8,128)(2,1)S(1)}, bf16[512,128]{1,0:T(8,128)(2,1)S(1)}, u32[]{:S(2)}, u32[]{:S(2)}) collective-permute-start(bf16[512,128]{1,0:T(8,128)(2,1)S(1)} %collective-permute-done.1.refs_1_), channel_id=1, source_target_pairs={{0,128},{1,129},{2,130},{3,131},{4,132},{5,133},{6,134},{7,135},{8... | collective-permute-start | bytes 393224 | tf_op jit(solution)/shard_map/ppermute | solution.py:41
  38.0 1.3 copy-start.1
  39.4 5.2 %copy-start.4 = (s32[1,1,8]{2,1,0:T(1,128)S(1)}, s32[1,1,8]{2,1,0:T(1,128)}, u32[]{:S(2)}) copy-start(s32[1,1,8]{2,1,0:T(1,128)} %refs_0_.1) | copy-start | bytes 100
  39.4 5.2 %copy-start.5 = (s32[1,1,8]{2,1,0:T(1,128)S(1)}, s32[1,1,8]{2,1,0:T(1,128)}, u32[]{:S(2)}) copy-start(s32[1,1,8]{2,1,0:T(1,128)} %refs_1_.1) | copy-start | bytes 100
  39.4 5.3 %copy-start.6 = (s32[16]{0:T(128)S(1)}, s32[16]{0:T(128)}, u32[]{:S(2)}) copy-start(s32[16]{0:T(128)} %constant.126.clone.1) | copy-start | bytes 196
  39.4 20.8 %copy-start = (bf16[2560,256]{1,0:T(8,128)(2,1)S(1)}, bf16[2560,256]{1,0:T(8,128)(2,1)}, u32[]{:S(2)}) copy-start(bf16[2560,256]{1,0:T(8,128)(2,1)} %shard_map.120.own_ref.facts_ref) | copy-start | bytes 3932164
  39.4 20.8 %all-to-all-start = ((bf16[4,2048,128]{2,1,0:T(8,128)(2,1)}), bf16[4,2048,128]{2,1,0:T(8,128)(2,1)}, u32[]{:S(2)}, u32[]{:S(2)}) async-start(bf16[4,2048,128]{2,1,0:T(8,128)(2,1)} %copy-done.1), calls=%async_computation | async-start | bytes 4194304 | tf_op jit(solution)/shard_map/all_to_all | solution.py:53
  82.2 25.0 %copy-start.2 = (bf16[128,128]{1,0:T(8,128)(2,1)S(1)}, bf16[128,128]{1,0:T(8,128)(2,1)}, u32[]{:S(2)}) copy-start(bf16[128,128]{1,0:T(8,128)(2,1)} %weight_ref.3) | copy-start | bytes 98308
  82.2 25.0 %copy-start.3 = (f32[128]{0:T(128)S(1)}, f32[128]{0:T(128)}, u32[]{:S(2)}) copy-start(f32[128]{0:T(128)} %param.11) | copy-start | bytes 1540
  82.5 7.8 %collective-permute-start.4 = (bf16[512,128]{1,0:T(8,128)(2,1)S(1)}, bf16[512,128]{1,0:T(8,128)(2,1)S(1)}, u32[]{:S(2)}, u32[]{:S(2)}) collective-permute-start(bf16[512,128]{1,0:T(8,128)(2,1)S(1)} %get-tuple-element.23), channel_id=1, source_target_pairs={{0,1},{1,2},{2,3},{3,0},{4,5},{5,6},{6,7},{7,4},{8,9},{9,10},{10,1... | collective-permute-start | bytes 393224 | tf_op jit(solution)/shard_map/ppermute | solution.py:41
  86.8 8.9 %collective-permute-start.6 = (bf16[512,128]{1,0:T(8,128)(2,1)S(1)}, bf16[512,128]{1,0:T(8,128)(2,1)S(1)}, u32[]{:S(2)}, u32[]{:S(2)}) collective-permute-start(bf16[512,128]{1,0:T(8,128)(2,1)S(1)} %get-tuple-element.24), channel_id=1, source_target_pairs={{0,3},{1,0},{2,1},{3,2},{4,7},{5,4},{6,5},{7,6},{8,11},{9,8},{10,9... | collective-permute-start | bytes 393224 | tf_op jit(solution)/shard_map/ppermute | solution.py:41
  90.3 9.7 %collective-permute-start.5 = (bf16[512,128]{1,0:T(8,128)(2,1)S(1)}, bf16[512,128]{1,0:T(8,128)(2,1)S(1)}, u32[]{:S(2)}, u32[]{:S(2)}) collective-permute-start(bf16[512,128]{1,0:T(8,128)(2,1)S(1)} %shard_map.124), channel_id=1, source_target_pairs={{0,1},{1,2},{2,3},{3,0},{4,5},{5,6},{6,7},{7,4},{8,9},{9,10},{10,1... | collective-permute-start | bytes 393224 | tf_op jit(solution)/shard_map/ppermute | solution.py:41
  100.1 7.1 %collective-permute-start.7 = (bf16[512,128]{1,0:T(8,128)(2,1)S(1)}, bf16[512,128]{1,0:T(8,128)(2,1)S(1)}, u32[]{:S(2)}, u32[]{:S(2)}) collective-permute-start(bf16[512,128]{1,0:T(8,128)(2,1)S(1)} %get-tuple-element.26), channel_id=1, source_target_pairs={{0,16},{1,17},{2,18},{3,19},{4,20},{5,21},{6,22},{7,23},{8,24},{9,... | collective-permute-start | bytes 393224 | tf_op jit(solution)/shard_map/ppermute | solution.py:32
  108.2 13.3 %collective-permute-start.8 = (bf16[592,128]{1,0:T(8,128)(2,1)S(1)}, bf16[592,128]{1,0:T(8,128)(2,1)S(1)}, u32[]{:S(2)}, u32[]{:S(2)}) collective-permute-start(bf16[592,128]{1,0:T(8,128)(2,1)S(1)} %get-tuple-element.28.refs_0_.both_ref), channel_id=1, source_target_pairs={{0,128},{1,129},{2,130},{3,131},{4,132},{5,133},{6,134},{7,135},{8... | collective-permute-start | bytes 454664 | tf_op jit(solution)/shard_map/ppermute | solution.py:41
  115.9 12.5 %collective-permute-start.10 = (bf16[592,128]{1,0:T(8,128)(2,1)S(1)}, bf16[592,128]{1,0:T(8,128)(2,1)S(1)}, u32[]{:S(2)}, u32[]{:S(2)}) collective-permute-start(bf16[592,128]{1,0:T(8,128)(2,1)S(1)} %get-tuple-element.28.refs_0_.both_ref), channel_id=1, source_target_pairs={{0,384},{1,385},{2,386},{3,387},{4,388},{5,389},{6,390},{7,391},{8... | collective-permute-start | bytes 454664 | tf_op jit(solution)/shard_map/ppermute | solution.py:41
  121.5 11.2 %collective-permute-start.9 = (bf16[592,128]{1,0:T(8,128)(2,1)S(1)}, bf16[592,128]{1,0:T(8,128)(2,1)S(1)}, u32[]{:S(2)}, u32[]{:S(2)}) collective-permute-start(bf16[592,128]{1,0:T(8,128)(2,1)S(1)} %collective-permute-done.8.refs_1_), channel_id=1, source_target_pairs={{0,128},{1,129},{2,130},{3,131},{4,132},{5,133},{6,134},{7,135},{8... | collective-permute-start | bytes 454664 | tf_op jit(solution)/shard_map/ppermute | solution.py:41
  173.5 9.0 %collective-permute-start.11 = (bf16[592,128]{1,0:T(8,128)(2,1)S(1)}, bf16[592,128]{1,0:T(8,128)(2,1)S(1)}, u32[]{:S(2)}, u32[]{:S(2)}) collective-permute-start(bf16[592,128]{1,0:T(8,128)(2,1)S(1)} %get-tuple-element.31), channel_id=1, source_target_pairs={{0,1},{1,2},{2,3},{3,0},{4,5},{5,6},{6,7},{7,4},{8,9},{9,10},{10,1... | collective-permute-start | bytes 454664 | tf_op jit(solution)/shard_map/ppermute | solution.py:41
  175.5 12.5 %collective-permute-start.13 = (bf16[592,128]{1,0:T(8,128)(2,1)S(1)}, bf16[592,128]{1,0:T(8,128)(2,1)S(1)}, u32[]{:S(2)}, u32[]{:S(2)}) collective-permute-start(bf16[592,128]{1,0:T(8,128)(2,1)S(1)} %get-tuple-element.32), channel_id=1, source_target_pairs={{0,3},{1,0},{2,1},{3,2},{4,7},{5,4},{6,5},{7,6},{8,11},{9,8},{10,9... | collective-permute-start | bytes 454664 | tf_op jit(solution)/shard_map/ppermute | solution.py:41
  182.5 10.1 %collective-permute-start.12 = (bf16[592,128]{1,0:T(8,128)(2,1)S(1)}, bf16[592,128]{1,0:T(8,128)(2,1)S(1)}, u32[]{:S(2)}, u32[]{:S(2)}) collective-permute-start(bf16[592,128]{1,0:T(8,128)(2,1)S(1)} %shard_map.130), channel_id=1, source_target_pairs={{0,1},{1,2},{2,3},{3,0},{4,5},{5,6},{6,7},{7,4},{8,9},{9,10},{10,1... | collective-permute-start | bytes 454664 | tf_op jit(solution)/shard_map/ppermute | solution.py:41
  192.7 11.3 %collective-permute-start.14 = (bf16[416,128]{1,0:T(8,128)(2,1)S(1)}, bf16[416,128]{1,0:T(8,128)(2,1)S(1)}, u32[]{:S(2)}, u32[]{:S(2)}) collective-permute-start(bf16[416,128]{1,0:T(8,128)(2,1)S(1)} %get-tuple-element.34.sent_ref), channel_id=1, source_target_pairs={{0,16},{1,17},{2,18},{3,19},{4,20},{5,21},{6,22},{7,23},{8,24},{9,... | collective-permute-start | bytes 319496 | tf_op jit(solution)/shard_map/ppermute | solution.py:32

commit v7 on v6

--- a/solution.py
+++ b/solution.py
@@ -333,21 +333,24 @@
     src = jnp.where(first, in_row + jnp.mod(-dzl, RING) * 2, in_col + jnp.mod(-dzh, RING) * 2)
     dst = jnp.where(first, in_col + jnp.mod(dzh, RING) * 2, in_row + jnp.mod(dzl, RING) * 2)
     bf16 = jnp.bfloat16
-
-    def spread_sum(both, lift):
+    places = (src, dst, weights)
+
+    def spread_sum(both, places, lift):
         n = 2 * RING * BLOCK + (2 * LIFT if lift else 0)
         after = far_shift(both, 1, 0)
-        before = far_shift(both, -1, 0)
+        held, places = lax.optimization_barrier((both, places))
+        before = far_shift(held, -1, 0)
         across = far_shift(after, 1, 0)
         (near,) = call(
             functools.partial(join_kernel, lift),
             [((RING, n, width), bf16)],
             both, after, across, before,
         )
+        near, places = lax.optimization_barrier((near, places))
         (sums,) = call(
             functools.partial(tile_kernel, lift),
             [((RING, n, width), bf16)],
-            core_no, src, dst, weights, facts, arrived, near_exchange(near, 0),
+            core_no, *places, facts, arrived, near_exchange(near, 0),
             scalars=4,
             scratch=[pltpu.VMEM((2 * RING * RING, BLOCK, width), jnp.float32)],
             mebibytes=20,
@@ -373,14 +376,14 @@
 
     both = jnp.concatenate([facts[:BLOCK, :width], arrived[:BLOCK, :width]], axis=0)
 
-    sums, _, back = spread_sum(both, False)
+    sums, _, back = spread_sum(both, places, False)
     activated, both = call(
         middle_kernel,
         [((BLOCK, width), jnp.bfloat16), ((2 * BLOCK + LIFT, width), jnp.bfloat16)],
         core_no, sums, back, both, facts, arrived, weight, bias[None, :],
         scalars=1,
     )
-    sums, sent, back = spread_sum(both, True)
+    sums, sent, back = spread_sum(both, places, True)
     feature_grad, weight_grad, bias_grad = call(
         end_kernel,
         [

time: 206 us -> 200 us (0.971)
  blocking collectives: 57.7 us -> 76.6 us
  waiting for transfers between devices: 48.8 us -> 34.5 us
  starting transfers between devices: 84.3 us -> 76.2 us
    all_to_all x3 -> x4, blocking collectives: 57.7 us -> 76.6 us  [near_exchange(): lax.all_to_all(v, AXES, split_axis=0, concat_axis=0, tiled=True, axis_ind...]
    all_to_all x1 -> x0, waiting for transfers between devices: 15.4 us -> none  [near_exchange(): lax.all_to_all(v, AXES, split_axis=0, concat_axis=0, tiled=True, axis_ind...]
    ppermute x3, starting transfers between devices: 25.3 us -> 16.9 us  [swap_cores(): lax.ppermute(v, AXES, pairs(lambda zl, x, core, y, zh: (zl, x, 1 - core,...]
    ppermute x12, starting transfers between devices: 53.8 us -> 59.3 us  [far_shift(): return lax.ppermute(v, AXES, pairs(step))]
    all_to_all x1 -> x0, starting transfers between devices: 5.15 us -> none  [near_exchange(): lax.all_to_all(v, AXES, split_axis=0, concat_axis=0, tiled=True, axis_ind...]
  transfers between devices with their start and end apart: 16 -> 15, of which waited for: 14 -> 12; matrix products, arithmetic and copies ran while one was open for 1% -> 1% of each run, Pallas kernels for 0% -> 0%
where the time goes in v7:
time: 200 us; the launch traced here: 199 us
  blocking collectives  76.6 us (38%)
  starting transfers between devices  76.2 us (38%)
  waiting for transfers between devices  34.5 us (17%)
  Pallas kernels  9.08 us (5%)
    all_to_all x4, blocking collectives, near_exchange(): lax.all_to_all(v, AXES, split_axis=0, concat_axis=0, tiled=True, axis_ind...  76.6 us
    ppermute x12, starting transfers between devices, far_shift(): return lax.ppermute(v, AXES, pairs(step))  59.3 us
    ppermute x12, waiting for transfers between devices, far_shift(): return lax.ppermute(v, AXES, pairs(step))  30.7 us
    ppermute x3, starting transfers between devices, swap_cores(): lax.ppermute(v, AXES, pairs(lambda zl, x, core, y, zh: (zl, x, 1 - core,...  16.9 us
    pallas_call x13, Pallas kernels, call(): pl.pallas_call(kernel, out_shape=[jax.ShapeDtypeStruct(shape, dtype) for...  9.08 us
  transfers between devices with their start and end apart: 15, of which 12 were waited for; matrix products, arithmetic and copies ran while one was open for 1% of the time, Pallas kernels for 0%

profile of v7, /device:TPU:1, one launch (start us, length us, event | category | flops | bytes accessed | tf_op | source)
XLA Modules:
  0.0 199.2 jit_solution(12379249250211927815)
XLA Ops:
  1.3 2.5 %shard_map.120.own_ref.facts_ref = bf16[2560,256]{1,0:T(8,128)(2,1)} custom-call(s32[1,1,8]{2,1,0:T(1,128)} %refs_0_.1, s32[1,1,8]{2,1,0:T(1,128)} %refs_1_.1, s32[1,1]{1,0:T(1,128)} %copy.13.refs_2_, bf16[256,128]{1,0:T(8,128)(2,1)} %refs_3_.1, bf16[256,128]{1,0:T(8,128)(2,1)} %refs_4_.1, f32[2,128]{1,0:T(2,128)} %bitcast.31, bf16[2048,256]{1,0:T(8,128)(2,1)} %bitcast.27), custom_call_target="tpu_custom_call" | custom-call | tf_op jit(solution)/shard_map/pallas_call | solution.py:61
  3.8 8.8 %collective-permute-start = (bf16[2560,256]{1,0:T(8,128)(2,1)}, bf16[2560,256]{1,0:T(8,128)(2,1)S(1)}, u32[]{:S(2)}, u32[]{:S(2)}) collective-permute-start(bf16[2560,256]{1,0:T(8,128)(2,1)} %shard_map.120.own_ref.facts_ref), channel_id=1, source_target_pairs={{0,16},{1,17},{2,18},{3,19},{4,20},{5,21},{6,22},{7,23},{8,24},{9,... | collective-permute-start | bytes 3932168 | tf_op jit(solution)/shard_map/ppermute | solution.py:32
  13.5 1.9 collective-permute-done.other_ref
  15.5 3.4 %collective-permute-start.1 = (bf16[512,128]{1,0:T(8,128)(2,1)S(1)}, bf16[512,128]{1,0:T(8,128)(2,1)S(1)}, u32[]{:S(2)}, u32[]{:S(2)}) collective-permute-start(bf16[512,128]{1,0:T(8,128)(2,1)S(1)} %pad_maximum_fusion.refs_0_.both_ref), channel_id=1, source_target_pairs={{0,128},{1,129},{2,130},{3,131},{4,132},{5,133},{6,134},{7,135},{8... | collective-permute-start | bytes 393224 | tf_op jit(solution)/shard_map/ppermute | solution.py:41
  19.2 5.7 %collective-permute-start.3 = (bf16[512,128]{1,0:T(8,128)(2,1)S(1)}, bf16[512,128]{1,0:T(8,128)(2,1)S(1)}, u32[]{:S(2)}, u32[]{:S(2)}) collective-permute-start(bf16[512,128]{1,0:T(8,128)(2,1)S(1)} %pad_maximum_fusion.refs_0_.both_ref), channel_id=1, source_target_pairs={{0,384},{1,385},{2,386},{3,387},{4,388},{5,389},{6,390},{7,391},{8... | collective-permute-start | bytes 393224 | tf_op jit(solution)/shard_map/ppermute | solution.py:41
  25.2 8.3 %collective-permute-start.2 = (bf16[512,128]{1,0:T(8,128)(2,1)S(1)}, bf16[512,128]{1,0:T(8,128)(2,1)S(1)}, u32[]{:S(2)}, u32[]{:S(2)}) collective-permute-start(bf16[512,128]{1,0:T(8,128)(2,1)S(1)} %collective-permute-done.1.refs_1_), channel_id=1, source_target_pairs={{0,128},{1,129},{2,130},{3,131},{4,132},{5,133},{6,134},{7,135},{8... | collective-permute-start | bytes 393224 | tf_op jit(solution)/shard_map/ppermute | solution.py:41
  33.5 4.6 %collective-permute-done.2.refs_2_ = bf16[512,128]{1,0:T(8,128)(2,1)S(1)} collective-permute-done((bf16[512,128]{1,0:T(8,128)(2,1)S(1)}, bf16[512,128]{1,0:T(8,128)(2,1)S(1)}, u32[]{:S(2)}, u32[]{:S(2)}) %collective-permute-start.2) | collective-permute-done | bytes 131104 | tf_op jit(solution)/shard_map/ppermute | solution.py:41
  38.3 20.1 %all_to_all.20.near_ref = bf16[4,2048,128]{2,1,0:T(8,128)(2,1)S(1)} all-to-all(bf16[4,2048,128]{2,1,0:T(8,128)(2,1)S(1)} %shard_map.121), channel_id=1, replica_groups={{0,32,64,96},{1,33,65,97},{2,34,66,98},{3,35,67,99},{4,36,68,100},{5,37..., dimensions={0} | all-to-all | bytes 4194304 | tf_op jit(solution)/shard_map/all_to_all | solution.py:53
  58.4 1.8 shard_map.122
  60.2 19.2 %all_to_all.21.near_ref = bf16[4,2048,128]{2,1,0:T(8,128)(2,1)S(1)} all-to-all(bf16[4,2048,128]{2,1,0:T(8,128)(2,1)S(1)} %shard_map.122), channel_id=1, replica_groups={{0,4,8,12},{1,5,9,13},{2,6,10,14},{3,7,11,15},{32,36,40,44},{33,37,41,4..., dimensions={0} | all-to-all | bytes 4194304 | tf_op jit(solution)/shard_map/all_to_all | solution.py:53
  79.6 8.4 %collective-permute-start.4 = (bf16[512,128]{1,0:T(8,128)(2,1)S(1)}, bf16[512,128]{1,0:T(8,128)(2,1)S(1)}, u32[]{:S(2)}, u32[]{:S(2)}) collective-permute-start(bf16[512,128]{1,0:T(8,128)(2,1)S(1)} %get-tuple-element.47), channel_id=1, source_target_pairs={{0,1},{1,2},{2,3},{3,0},{4,5},{5,6},{6,7},{7,4},{8,9},{9,10},{10,1... | collective-permute-start | bytes 393224 | tf_op jit(solution)/shard_map/ppermute | solution.py:41
  88.0 1.9 collective-permute-start.6
  90.1 5.9 %collective-permute-start.5 = (bf16[512,128]{1,0:T(8,128)(2,1)S(1)}, bf16[512,128]{1,0:T(8,128)(2,1)S(1)}, u32[]{:S(2)}, u32[]{:S(2)}) collective-permute-start(bf16[512,128]{1,0:T(8,128)(2,1)S(1)} %shard_map.124), channel_id=1, source_target_pairs={{0,1},{1,2},{2,3},{3,0},{4,5},{5,6},{6,7},{7,4},{8,9},{9,10},{10,1... | collective-permute-start | bytes 393224 | tf_op jit(solution)/shard_map/ppermute | solution.py:41
  96.0 3.5 %collective-permute-done.5.across_ref = bf16[512,128]{1,0:T(8,128)(2,1)S(1)} collective-permute-done((bf16[512,128]{1,0:T(8,128)(2,1)S(1)}, bf16[512,128]{1,0:T(8,128)(2,1)S(1)}, u32[]{:S(2)}, u32[]{:S(2)}) %collective-permute-start.5) | collective-permute-done | bytes 131104 | tf_op jit(solution)/shard_map/ppermute | solution.py:41
  99.6 4.2 %collective-permute-start.7 = (bf16[512,128]{1,0:T(8,128)(2,1)S(1)}, bf16[512,128]{1,0:T(8,128)(2,1)S(1)}, u32[]{:S(2)}, u32[]{:S(2)}) collective-permute-start(bf16[512,128]{1,0:T(8,128)(2,1)S(1)} %get-tuple-element.50), channel_id=1, source_target_pairs={{0,16},{1,17},{2,18},{3,19},{4,20},{5,21},{6,22},{7,23},{8,24},{9,... | collective-permute-start | bytes 393224 | tf_op jit(solution)/shard_map/ppermute | solution.py:32
  103.8 1.0 collective-permute-done.7.back_ref
  105.7 7.4 %collective-permute-start.8 = (bf16[592,128]{1,0:T(8,128)(2,1)S(1)}, bf16[592,128]{1,0:T(8,128)(2,1)S(1)}, u32[]{:S(2)}, u32[]{:S(2)}) collective-permute-start(bf16[592,128]{1,0:T(8,128)(2,1)S(1)} %get-tuple-element.53.refs_0_.both_ref), channel_id=1, source_target_pairs={{0,128},{1,129},{2,130},{3,131},{4,132},{5,133},{6,134},{7,135},{8... | collective-permute-start | bytes 454664 | tf_op jit(solution)/shard_map/ppermute | solution.py:41
  113.1 3.1 %collective-permute-start.10 = (bf16[592,128]{1,0:T(8,128)(2,1)S(1)}, bf16[592,128]{1,0:T(8,128)(2,1)S(1)}, u32[]{:S(2)}, u32[]{:S(2)}) collective-permute-start(bf16[592,128]{1,0:T(8,128)(2,1)S(1)} %get-tuple-element.53.refs_0_.both_ref), channel_id=1, source_target_pairs={{0,384},{1,385},{2,386},{3,387},{4,388},{5,389},{6,390},{7,391},{8... | collective-permute-start | bytes 454664 | tf_op jit(solution)/shard_map/ppermute | solution.py:41
  116.2 3.6 %collective-permute-done.8.refs_1_ = bf16[592,128]{1,0:T(8,128)(2,1)S(1)} collective-permute-done((bf16[592,128]{1,0:T(8,128)(2,1)S(1)}, bf16[592,128]{1,0:T(8,128)(2,1)S(1)}, u32[]{:S(2)}, u32[]{:S(2)}) %collective-permute-start.8) | collective-permute-done | bytes 151584 | tf_op jit(solution)/shard_map/ppermute | solution.py:41
  119.8 6.1 %collective-permute-start.9 = (bf16[592,128]{1,0:T(8,128)(2,1)S(1)}, bf16[592,128]{1,0:T(8,128)(2,1)S(1)}, u32[]{:S(2)}, u32[]{:S(2)}) collective-permute-start(bf16[592,128]{1,0:T(8,128)(2,1)S(1)} %collective-permute-done.8.refs_1_), channel_id=1, source_target_pairs={{0,128},{1,129},{2,130},{3,131},{4,132},{5,133},{6,134},{7,135},{8... | collective-permute-start | bytes 454664 | tf_op jit(solution)/shard_map/ppermute | solution.py:41
  126.0 6.9 %collective-permute-done.9.refs_2_ = bf16[592,128]{1,0:T(8,128)(2,1)S(1)} collective-permute-done((bf16[592,128]{1,0:T(8,128)(2,1)S(1)}, bf16[592,128]{1,0:T(8,128)(2,1)S(1)}, u32[]{:S(2)}, u32[]{:S(2)}) %collective-permute-start.9) | collective-permute-done | bytes 151584 | tf_op jit(solution)/shard_map/ppermute | solution.py:41
  133.1 18.7 %all_to_all.22.near_ref = bf16[4,2208,128]{2,1,0:T(8,128)(2,1)S(1)} all-to-all(bf16[4,2208,128]{2,1,0:T(8,128)(2,1)S(1)} %shard_map.127), channel_id=1, replica_groups={{0,32,64,96},{1,33,65,97},{2,34,66,98},{3,35,67,99},{4,36,68,100},{5,37..., dimensions={0} | all-to-all | bytes 4521984 | tf_op jit(solution)/shard_map/all_to_all | solution.py:53
  151.8 1.8 shard_map.128
  153.6 18.7 %all_to_all.23.near_ref = bf16[4,2208,128]{2,1,0:T(8,128)(2,1)S(1)} all-to-all(bf16[4,2208,128]{2,1,0:T(8,128)(2,1)S(1)} %shard_map.128), channel_id=1, replica_groups={{0,4,8,12},{1,5,9,13},{2,6,10,14},{3,7,11,15},{32,36,40,44},{33,37,41,4..., dimensions={0} | all-to-all | bytes 4521984 | tf_op jit(solution)/shard_map/all_to_all | solution.py:53
  172.6 1.9 collective-permute-start.11
  174.5 5.2 %collective-permute-start.13 = (bf16[592,128]{1,0:T(8,128)(2,1)S(1)}, bf16[592,128]{1,0:T(8,128)(2,1)S(1)}, u32[]{:S(2)}, u32[]{:S(2)}) collective-permute-start(bf16[592,128]{1,0:T(8,128)(2,1)S(1)} %get-tuple-element.64), channel_id=1, source_target_pairs={{0,3},{1,0},{2,1},{3,2},{4,7},{5,4},{6,5},{7,6},{8,11},{9,8},{10,9... | collective-permute-start | bytes 454664 | tf_op jit(solution)/shard_map/ppermute | solution.py:41
  179.7 1.7 collective-permute-done.11.passing_ref.after_ref
  181.4 1.9 collective-permute-start.12
  183.3 1.9 collective-permute-done.13.before_ref
  185.2 8.1 %collective-permute-done.12.across_ref = bf16[592,128]{1,0:T(8,128)(2,1)S(1)} collective-permute-done((bf16[592,128]{1,0:T(8,128)(2,1)S(1)}, bf16[592,128]{1,0:T(8,128)(2,1)S(1)}, u32[]{:S(2)}, u32[]{:S(2)}) %collective-permute-start.12) | collective-permute-done | bytes 151584 | tf_op jit(solution)/shard_map/ppermute | solution.py:41
  193.4 3.9 %collective-permute-start.14 = (bf16[416,128]{1,0:T(8,128)(2,1)S(1)}, bf16[416,128]{1,0:T(8,128)(2,1)S(1)}, u32[]{:S(2)}, u32[]{:S(2)}) collective-permute-start(bf16[416,128]{1,0:T(8,128)(2,1)S(1)} %get-tuple-element.66.sent_ref), channel_id=1, source_target_pairs={{0,16},{1,17},{2,18},{3,19},{4,20},{5,21},{6,22},{7,23},{8,24},{9,... | collective-permute-start | bytes 319496 | tf_op jit(solution)/shard_map/ppermute | solution.py:32
  197.3 0.9 collective-permute-done.14.back_ref
  (35 shorter events, 4.6 us)
Async XLA Ops:
  0.6 18.3 %copy-start.5 = (s32[16]{0:T(128)S(1)}, s32[16]{0:T(128)}, u32[]{:S(2)}) copy-start(s32[16]{0:T(128)} %constant.126.clone.1) | copy-start | bytes 196
  0.6 12.8 %copy-start.4 = (s32[1,1,8]{2,1,0:T(1,128)S(1)}, s32[1,1,8]{2,1,0:T(1,128)}, u32[]{:S(2)}) copy-start(s32[1,1,8]{2,1,0:T(1,128)} %refs_1_.1) | copy-start | bytes 100
  0.7 12.8 %copy-start.3 = (s32[1,1,8]{2,1,0:T(1,128)S(1)}, s32[1,1,8]{2,1,0:T(1,128)}, u32[]{:S(2)}) copy-start(s32[1,1,8]{2,1,0:T(1,128)} %refs_0_.1) | copy-start | bytes 100
  3.8 11.6 %collective-permute-start = (bf16[2560,256]{1,0:T(8,128)(2,1)}, bf16[2560,256]{1,0:T(8,128)(2,1)S(1)}, u32[]{:S(2)}, u32[]{:S(2)}) collective-permute-start(bf16[2560,256]{1,0:T(8,128)(2,1)} %shard_map.120.own_ref.facts_ref), channel_id=1, source_target_pairs={{0,16},{1,17},{2,18},{3,19},{4,20},{5,21},{6,22},{7,23},{8,24},{9,... | collective-permute-start | bytes 3932168 | tf_op jit(solution)/shard_map/ppermute | solution.py:32
  15.5 9.7 %collective-permute-start.1 = (bf16[512,128]{1,0:T(8,128)(2,1)S(1)}, bf16[512,128]{1,0:T(8,128)(2,1)S(1)}, u32[]{:S(2)}, u32[]{:S(2)}) collective-permute-start(bf16[512,128]{1,0:T(8,128)(2,1)S(1)} %pad_maximum_fusion.refs_0_.both_ref), channel_id=1, source_target_pairs={{0,128},{1,129},{2,130},{3,131},{4,132},{5,133},{6,134},{7,135},{8... | collective-permute-start | bytes 393224 | tf_op jit(solution)/shard_map/ppermute | solution.py:41
  19.2 14.3 %collective-permute-start.3 = (bf16[512,128]{1,0:T(8,128)(2,1)S(1)}, bf16[512,128]{1,0:T(8,128)(2,1)S(1)}, u32[]{:S(2)}, u32[]{:S(2)}) collective-permute-start(bf16[512,128]{1,0:T(8,128)(2,1)S(1)} %pad_maximum_fusion.refs_0_.both_ref), channel_id=1, source_target_pairs={{0,384},{1,385},{2,386},{3,387},{4,388},{5,389},{6,390},{7,391},{8... | collective-permute-start | bytes 393224 | tf_op jit(solution)/shard_map/ppermute | solution.py:41
  25.2 12.9 %collective-permute-start.2 = (bf16[512,128]{1,0:T(8,128)(2,1)S(1)}, bf16[512,128]{1,0:T(8,128)(2,1)S(1)}, u32[]{:S(2)}, u32[]{:S(2)}) collective-permute-start(bf16[512,128]{1,0:T(8,128)(2,1)S(1)} %collective-permute-done.1.refs_1_), channel_id=1, source_target_pairs={{0,128},{1,129},{2,130},{3,131},{4,132},{5,133},{6,134},{7,135},{8... | collective-permute-start | bytes 393224 | tf_op jit(solution)/shard_map/ppermute | solution.py:41
  38.3 20.1 %copy-start = (bf16[2560,256]{1,0:T(8,128)(2,1)S(1)}, bf16[2560,256]{1,0:T(8,128)(2,1)}, u32[]{:S(2)}) copy-start(bf16[2560,256]{1,0:T(8,128)(2,1)} %shard_map.120.own_ref.facts_ref) | copy-start | bytes 3932164
  79.4 25.4 %copy-start.1 = (bf16[128,128]{1,0:T(8,128)(2,1)S(1)}, bf16[128,128]{1,0:T(8,128)(2,1)}, u32[]{:S(2)}) copy-start(bf16[128,128]{1,0:T(8,128)(2,1)} %weight_ref.3) | copy-start | bytes 98308
  79.4 25.4 %copy-start.2 = (f32[128]{0:T(128)S(1)}, f32[128]{0:T(128)}, u32[]{:S(2)}) copy-start(f32[128]{0:T(128)} %param.11) | copy-start | bytes 1540
  79.6 10.4 %collective-permute-start.4 = (bf16[512,128]{1,0:T(8,128)(2,1)S(1)}, bf16[512,128]{1,0:T(8,128)(2,1)S(1)}, u32[]{:S(2)}, u32[]{:S(2)}) collective-permute-start(bf16[512,128]{1,0:T(8,128)(2,1)S(1)} %get-tuple-element.47), channel_id=1, source_target_pairs={{0,1},{1,2},{2,3},{3,0},{4,5},{5,6},{6,7},{7,4},{8,9},{9,10},{10,1... | collective-permute-start | bytes 393224 | tf_op jit(solution)/shard_map/ppermute | solution.py:41
  88.0 8.0 %collective-permute-start.6 = (bf16[512,128]{1,0:T(8,128)(2,1)S(1)}, bf16[512,128]{1,0:T(8,128)(2,1)S(1)}, u32[]{:S(2)}, u32[]{:S(2)}) collective-permute-start(bf16[512,128]{1,0:T(8,128)(2,1)S(1)} %get-tuple-element.48), channel_id=1, source_target_pairs={{0,3},{1,0},{2,1},{3,2},{4,7},{5,4},{6,5},{7,6},{8,11},{9,8},{10,9... | collective-permute-start | bytes 393224 | tf_op jit(solution)/shard_map/ppermute | solution.py:41
  90.1 9.4 %collective-permute-start.5 = (bf16[512,128]{1,0:T(8,128)(2,1)S(1)}, bf16[512,128]{1,0:T(8,128)(2,1)S(1)}, u32[]{:S(2)}, u32[]{:S(2)}) collective-permute-start(bf16[512,128]{1,0:T(8,128)(2,1)S(1)} %shard_map.124), channel_id=1, source_target_pairs={{0,1},{1,2},{2,3},{3,0},{4,5},{5,6},{6,7},{7,4},{8,9},{9,10},{10,1... | collective-permute-start | bytes 393224 | tf_op jit(solution)/shard_map/ppermute | solution.py:41
  99.6 5.2 %collective-permute-start.7 = (bf16[512,128]{1,0:T(8,128)(2,1)S(1)}, bf16[512,128]{1,0:T(8,128)(2,1)S(1)}, u32[]{:S(2)}, u32[]{:S(2)}) collective-permute-start(bf16[512,128]{1,0:T(8,128)(2,1)S(1)} %get-tuple-element.50), channel_id=1, source_target_pairs={{0,16},{1,17},{2,18},{3,19},{4,20},{5,21},{6,22},{7,23},{8,24},{9,... | collective-permute-start | bytes 393224 | tf_op jit(solution)/shard_map/ppermute | solution.py:32
  105.7 14.2 %collective-permute-start.8 = (bf16[592,128]{1,0:T(8,128)(2,1)S(1)}, bf16[592,128]{1,0:T(8,128)(2,1)S(1)}, u32[]{:S(2)}, u32[]{:S(2)}) collective-permute-start(bf16[592,128]{1,0:T(8,128)(2,1)S(1)} %get-tuple-element.53.refs_0_.both_ref), channel_id=1, source_target_pairs={{0,128},{1,129},{2,130},{3,131},{4,132},{5,133},{6,134},{7,135},{8... | collective-permute-start | bytes 454664 | tf_op jit(solution)/shard_map/ppermute | solution.py:41
  113.1 12.8 %collective-permute-start.10 = (bf16[592,128]{1,0:T(8,128)(2,1)S(1)}, bf16[592,128]{1,0:T(8,128)(2,1)S(1)}, u32[]{:S(2)}, u32[]{:S(2)}) collective-permute-start(bf16[592,128]{1,0:T(8,128)(2,1)S(1)} %get-tuple-element.53.refs_0_.both_ref), channel_id=1, source_target_pairs={{0,384},{1,385},{2,386},{3,387},{4,388},{5,389},{6,390},{7,391},{8... | collective-permute-start | bytes 454664 | tf_op jit(solution)/shard_map/ppermute | solution.py:41
  119.8 13.0 %collective-permute-start.9 = (bf16[592,128]{1,0:T(8,128)(2,1)S(1)}, bf16[592,128]{1,0:T(8,128)(2,1)S(1)}, u32[]{:S(2)}, u32[]{:S(2)}) collective-permute-start(bf16[592,128]{1,0:T(8,128)(2,1)S(1)} %collective-permute-done.8.refs_1_), channel_id=1, source_target_pairs={{0,128},{1,129},{2,130},{3,131},{4,132},{5,133},{6,134},{7,135},{8... | collective-permute-start | bytes 454664 | tf_op jit(solution)/shard_map/ppermute | solution.py:41
  172.6 8.7 %collective-permute-start.11 = (bf16[592,128]{1,0:T(8,128)(2,1)S(1)}, bf16[592,128]{1,0:T(8,128)(2,1)S(1)}, u32[]{:S(2)}, u32[]{:S(2)}) collective-permute-start(bf16[592,128]{1,0:T(8,128)(2,1)S(1)} %get-tuple-element.63), channel_id=1, source_target_pairs={{0,1},{1,2},{2,3},{3,0},{4,5},{5,6},{6,7},{7,4},{8,9},{9,10},{10,1... | collective-permute-start | bytes 454664 | tf_op jit(solution)/shard_map/ppermute | solution.py:41
  174.5 10.7 %collective-permute-start.13 = (bf16[592,128]{1,0:T(8,128)(2,1)S(1)}, bf16[592,128]{1,0:T(8,128)(2,1)S(1)}, u32[]{:S(2)}, u32[]{:S(2)}) collective-permute-start(bf16[592,128]{1,0:T(8,128)(2,1)S(1)} %get-tuple-element.64), channel_id=1, source_target_pairs={{0,3},{1,0},{2,1},{3,2},{4,7},{5,4},{6,5},{7,6},{8,11},{9,8},{10,9... | collective-permute-start | bytes 454664 | tf_op jit(solution)/shard_map/ppermute | solution.py:41
  181.4 12.0 %collective-permute-start.12 = (bf16[592,128]{1,0:T(8,128)(2,1)S(1)}, bf16[592,128]{1,0:T(8,128)(2,1)S(1)}, u32[]{:S(2)}, u32[]{:S(2)}) collective-permute-start(bf16[592,128]{1,0:T(8,128)(2,1)S(1)} %shard_map.130), channel_id=1, source_target_pairs={{0,1},{1,2},{2,3},{3,0},{4,5},{5,6},{6,7},{7,4},{8,9},{9,10},{10,1... | collective-permute-start | bytes 454664 | tf_op jit(solution)/shard_map/ppermute | solution.py:41
  193.4 4.9 %collective-permute-start.14 = (bf16[416,128]{1,0:T(8,128)(2,1)S(1)}, bf16[416,128]{1,0:T(8,128)(2,1)S(1)}, u32[]{:S(2)}, u32[]{:S(2)}) collective-permute-start(bf16[416,128]{1,0:T(8,128)(2,1)S(1)} %get-tuple-element.66.sent_ref), channel_id=1, source_target_pairs={{0,16},{1,17},{2,18},{3,19},{4,20},{5,21},{6,22},{7,23},{8,24},{9,... | collective-permute-start | bytes 319496 | tf_op jit(solution)/shard_map/ppermute | solution.py:32

commit v8 on v7

--- a/solution.py
+++ b/solution.py
@@ -153,7 +153,7 @@
         for k in range(RING):
             out_ref[copy, k * n : (k + 1) * n] = parts[k][:n]
     if lift:
-        put_split(slots_of(out_ref), RING * n, 2, lifted_sum(parts, n, 1))
+        put_split(slots_of(out_ref), RING * n, 1, lifted_sum(parts, n, 1))
 
 
 def tile_kernel(
@@ -190,7 +190,7 @@
         sums = acc_ref[k * held : (k + 1) * held].astype(jnp.bfloat16)
         out_ref[k, :n] = sums.reshape(n, sums.shape[-1])
     if lift:
-        put_split(slots_of(out_ref), n, 2, lifted_sum(slots_of(near_ref), n, 2))
+        put_split(slots_of(out_ref), n, 1, lifted_sum(slots_of(near_ref), n, 1))
 
 
 def sum_kernel(lift, near_ref, mine_ref, *outs):
@@ -205,7 +205,7 @@
         else:
             outs[k - 1][:m] = total.astype(jnp.bfloat16)
     if lift:
-        put_split(outs, m, 1, lifted_sum(slots_of(near_ref), RING * m, 2))
+        put_split(outs, m, 1, lifted_sum(slots_of(near_ref), RING * m, 1))
 
 
 def relay_kernel(lift, own_ref, passing_ref, out_ref):
@@ -336,7 +336,7 @@
     places = (src, dst, weights)
 
     def spread_sum(both, places, lift):
-        n = 2 * RING * BLOCK + (2 * LIFT if lift else 0)
+        n = 2 * RING * BLOCK + (LIFT if lift else 0)
         after = far_shift(both, 1, 0)
         held, places = lax.optimization_barrier((both, places))
         before = far_shift(held, -1, 0)

time: 200 us -> 199 us (level)
  no operation moved by 1% of the time
where the time goes in v8:
time: 199 us; the launch traced here: 198 us
  starting transfers between devices  76.2 us (38%)
  blocking collectives  75.8 us (38%)
  waiting for transfers between devices  34.5 us (17%)
  Pallas kernels  9.06 us (5%)
    all_to_all x4, blocking collectives, near_exchange(): lax.all_to_all(v, AXES, split_axis=0, concat_axis=0, tiled=True, axis_ind...  75.8 us
    ppermute x12, starting transfers between devices, far_shift(): return lax.ppermute(v, AXES, pairs(step))  59.3 us
    ppermute x12, waiting for transfers between devices, far_shift(): return lax.ppermute(v, AXES, pairs(step))  30.7 us
    ppermute x3, starting transfers between devices, swap_cores(): lax.ppermute(v, AXES, pairs(lambda zl, x, core, y, zh: (zl, x, 1 - core,...  16.9 us
    pallas_call x13, Pallas kernels, call(): pl.pallas_call(kernel, out_shape=[jax.ShapeDtypeStruct(shape, dtype) for...  9.06 us
  transfers between devices with their start and end apart: 15, of which 12 were waited for; matrix products, arithmetic and copies ran while one was open for 1% of the time, Pallas kernels for 0%

profile of v8, /device:TPU:1, one launch (start us, length us, event | category | flops | bytes accessed | tf_op | source)
XLA Modules:
  0.0 198.3 jit_solution(13292261295648509749)
XLA Ops:
  1.3 2.5 %shard_map.120.own_ref.facts_ref = bf16[2560,256]{1,0:T(8,128)(2,1)} custom-call(s32[1,1,8]{2,1,0:T(1,128)} %refs_0_.1, s32[1,1,8]{2,1,0:T(1,128)} %refs_1_.1, s32[1,1]{1,0:T(1,128)} %copy.13.refs_2_, bf16[256,128]{1,0:T(8,128)(2,1)} %refs_3_.1, bf16[256,128]{1,0:T(8,128)(2,1)} %refs_4_.1, f32[2,128]{1,0:T(2,128)} %bitcast.31, bf16[2048,256]{1,0:T(8,128)(2,1)} %bitcast.27), custom_call_target="tpu_custom_call" | custom-call | tf_op jit(solution)/shard_map/pallas_call | solution.py:61
  3.8 8.8 %collective-permute-start = (bf16[2560,256]{1,0:T(8,128)(2,1)}, bf16[2560,256]{1,0:T(8,128)(2,1)S(1)}, u32[]{:S(2)}, u32[]{:S(2)}) collective-permute-start(bf16[2560,256]{1,0:T(8,128)(2,1)} %shard_map.120.own_ref.facts_ref), channel_id=1, source_target_pairs={{0,16},{1,17},{2,18},{3,19},{4,20},{5,21},{6,22},{7,23},{8,24},{9,... | collective-permute-start | bytes 3932168 | tf_op jit(solution)/shard_map/ppermute | solution.py:32
  13.5 1.9 collective-permute-done.other_ref
  15.5 3.4 %collective-permute-start.1 = (bf16[512,128]{1,0:T(8,128)(2,1)S(1)}, bf16[512,128]{1,0:T(8,128)(2,1)S(1)}, u32[]{:S(2)}, u32[]{:S(2)}) collective-permute-start(bf16[512,128]{1,0:T(8,128)(2,1)S(1)} %pad_maximum_fusion.refs_0_.both_ref), channel_id=1, source_target_pairs={{0,128},{1,129},{2,130},{3,131},{4,132},{5,133},{6,134},{7,135},{8... | collective-permute-start | bytes 393224 | tf_op jit(solution)/shard_map/ppermute | solution.py:41
  19.2 5.7 %collective-permute-start.3 = (bf16[512,128]{1,0:T(8,128)(2,1)S(1)}, bf16[512,128]{1,0:T(8,128)(2,1)S(1)}, u32[]{:S(2)}, u32[]{:S(2)}) collective-permute-start(bf16[512,128]{1,0:T(8,128)(2,1)S(1)} %pad_maximum_fusion.refs_0_.both_ref), channel_id=1, source_target_pairs={{0,384},{1,385},{2,386},{3,387},{4,388},{5,389},{6,390},{7,391},{8... | collective-permute-start | bytes 393224 | tf_op jit(solution)/shard_map/ppermute | solution.py:41
  25.2 8.3 %collective-permute-start.2 = (bf16[512,128]{1,0:T(8,128)(2,1)S(1)}, bf16[512,128]{1,0:T(8,128)(2,1)S(1)}, u32[]{:S(2)}, u32[]{:S(2)}) collective-permute-start(bf16[512,128]{1,0:T(8,128)(2,1)S(1)} %collective-permute-done.1.refs_1_), channel_id=1, source_target_pairs={{0,128},{1,129},{2,130},{3,131},{4,132},{5,133},{6,134},{7,135},{8... | collective-permute-start | bytes 393224 | tf_op jit(solution)/shard_map/ppermute | solution.py:41
  33.5 4.6 %collective-permute-done.2.refs_2_ = bf16[512,128]{1,0:T(8,128)(2,1)S(1)} collective-permute-done((bf16[512,128]{1,0:T(8,128)(2,1)S(1)}, bf16[512,128]{1,0:T(8,128)(2,1)S(1)}, u32[]{:S(2)}, u32[]{:S(2)}) %collective-permute-start.2) | collective-permute-done | bytes 131104 | tf_op jit(solution)/shard_map/ppermute | solution.py:41
  38.3 20.1 %all_to_all.20.near_ref = bf16[4,2048,128]{2,1,0:T(8,128)(2,1)S(1)} all-to-all(bf16[4,2048,128]{2,1,0:T(8,128)(2,1)S(1)} %shard_map.121), channel_id=1, replica_groups={{0,32,64,96},{1,33,65,97},{2,34,66,98},{3,35,67,99},{4,36,68,100},{5,37..., dimensions={0} | all-to-all | bytes 4194304 | tf_op jit(solution)/shard_map/all_to_all | solution.py:53
  58.4 1.8 shard_map.122
  60.2 19.2 %all_to_all.21.near_ref = bf16[4,2048,128]{2,1,0:T(8,128)(2,1)S(1)} all-to-all(bf16[4,2048,128]{2,1,0:T(8,128)(2,1)S(1)} %shard_map.122), channel_id=1, replica_groups={{0,4,8,12},{1,5,9,13},{2,6,10,14},{3,7,11,15},{32,36,40,44},{33,37,41,4..., dimensions={0} | all-to-all | bytes 4194304 | tf_op jit(solution)/shard_map/all_to_all | solution.py:53
  79.6 8.4 %collective-permute-start.4 = (bf16[512,128]{1,0:T(8,128)(2,1)S(1)}, bf16[512,128]{1,0:T(8,128)(2,1)S(1)}, u32[]{:S(2)}, u32[]{:S(2)}) collective-permute-start(bf16[512,128]{1,0:T(8,128)(2,1)S(1)} %get-tuple-element.47), channel_id=1, source_target_pairs={{0,1},{1,2},{2,3},{3,0},{4,5},{5,6},{6,7},{7,4},{8,9},{9,10},{10,1... | collective-permute-start | bytes 393224 | tf_op jit(solution)/shard_map/ppermute | solution.py:41
  88.0 1.9 collective-permute-start.6
  90.1 5.9 %collective-permute-start.5 = (bf16[512,128]{1,0:T(8,128)(2,1)S(1)}, bf16[512,128]{1,0:T(8,128)(2,1)S(1)}, u32[]{:S(2)}, u32[]{:S(2)}) collective-permute-start(bf16[512,128]{1,0:T(8,128)(2,1)S(1)} %shard_map.124), channel_id=1, source_target_pairs={{0,1},{1,2},{2,3},{3,0},{4,5},{5,6},{6,7},{7,4},{8,9},{9,10},{10,1... | collective-permute-start | bytes 393224 | tf_op jit(solution)/shard_map/ppermute | solution.py:41
  96.0 3.5 %collective-permute-done.5.across_ref = bf16[512,128]{1,0:T(8,128)(2,1)S(1)} collective-permute-done((bf16[512,128]{1,0:T(8,128)(2,1)S(1)}, bf16[512,128]{1,0:T(8,128)(2,1)S(1)}, u32[]{:S(2)}, u32[]{:S(2)}) %collective-permute-start.5) | collective-permute-done | bytes 131104 | tf_op jit(solution)/shard_map/ppermute | solution.py:41
  99.6 4.2 %collective-permute-start.7 = (bf16[512,128]{1,0:T(8,128)(2,1)S(1)}, bf16[512,128]{1,0:T(8,128)(2,1)S(1)}, u32[]{:S(2)}, u32[]{:S(2)}) collective-permute-start(bf16[512,128]{1,0:T(8,128)(2,1)S(1)} %get-tuple-element.50), channel_id=1, source_target_pairs={{0,16},{1,17},{2,18},{3,19},{4,20},{5,21},{6,22},{7,23},{8,24},{9,... | collective-permute-start | bytes 393224 | tf_op jit(solution)/shard_map/ppermute | solution.py:32
  103.8 1.0 collective-permute-done.7.back_ref
  105.7 7.5 %collective-permute-start.8 = (bf16[592,128]{1,0:T(8,128)(2,1)S(1)}, bf16[592,128]{1,0:T(8,128)(2,1)S(1)}, u32[]{:S(2)}, u32[]{:S(2)}) collective-permute-start(bf16[592,128]{1,0:T(8,128)(2,1)S(1)} %get-tuple-element.53.refs_0_.both_ref), channel_id=1, source_target_pairs={{0,128},{1,129},{2,130},{3,131},{4,132},{5,133},{6,134},{7,135},{8... | collective-permute-start | bytes 454664 | tf_op jit(solution)/shard_map/ppermute | solution.py:41
  113.2 3.1 %collective-permute-start.10 = (bf16[592,128]{1,0:T(8,128)(2,1)S(1)}, bf16[592,128]{1,0:T(8,128)(2,1)S(1)}, u32[]{:S(2)}, u32[]{:S(2)}) collective-permute-start(bf16[592,128]{1,0:T(8,128)(2,1)S(1)} %get-tuple-element.53.refs_0_.both_ref), channel_id=1, source_target_pairs={{0,384},{1,385},{2,386},{3,387},{4,388},{5,389},{6,390},{7,391},{8... | collective-permute-start | bytes 454664 | tf_op jit(solution)/shard_map/ppermute | solution.py:41
  116.2 3.6 %collective-permute-done.8.refs_1_ = bf16[592,128]{1,0:T(8,128)(2,1)S(1)} collective-permute-done((bf16[592,128]{1,0:T(8,128)(2,1)S(1)}, bf16[592,128]{1,0:T(8,128)(2,1)S(1)}, u32[]{:S(2)}, u32[]{:S(2)}) %collective-permute-start.8) | collective-permute-done | bytes 151584 | tf_op jit(solution)/shard_map/ppermute | solution.py:41
  119.8 6.1 %collective-permute-start.9 = (bf16[592,128]{1,0:T(8,128)(2,1)S(1)}, bf16[592,128]{1,0:T(8,128)(2,1)S(1)}, u32[]{:S(2)}, u32[]{:S(2)}) collective-permute-start(bf16[592,128]{1,0:T(8,128)(2,1)S(1)} %collective-permute-done.8.refs_1_), channel_id=1, source_target_pairs={{0,128},{1,129},{2,130},{3,131},{4,132},{5,133},{6,134},{7,135},{8... | collective-permute-start | bytes 454664 | tf_op jit(solution)/shard_map/ppermute | solution.py:41
  126.0 6.9 %collective-permute-done.9.refs_2_ = bf16[592,128]{1,0:T(8,128)(2,1)S(1)} collective-permute-done((bf16[592,128]{1,0:T(8,128)(2,1)S(1)}, bf16[592,128]{1,0:T(8,128)(2,1)S(1)}, u32[]{:S(2)}, u32[]{:S(2)}) %collective-permute-start.9) | collective-permute-done | bytes 151584 | tf_op jit(solution)/shard_map/ppermute | solution.py:41
  133.1 18.3 %all_to_all.22.near_ref = bf16[4,2128,128]{2,1,0:T(8,128)(2,1)S(1)} all-to-all(bf16[4,2128,128]{2,1,0:T(8,128)(2,1)S(1)} %shard_map.127), channel_id=1, replica_groups={{0,32,64,96},{1,33,65,97},{2,34,66,98},{3,35,67,99},{4,36,68,100},{5,37..., dimensions={0} | all-to-all | bytes 4358144 | tf_op jit(solution)/shard_map/all_to_all | solution.py:53
  151.4 1.8 shard_map.128
  153.2 18.3 %all_to_all.23.near_ref = bf16[4,2128,128]{2,1,0:T(8,128)(2,1)S(1)} all-to-all(bf16[4,2128,128]{2,1,0:T(8,128)(2,1)S(1)} %shard_map.128), channel_id=1, replica_groups={{0,4,8,12},{1,5,9,13},{2,6,10,14},{3,7,11,15},{32,36,40,44},{33,37,41,4..., dimensions={0} | all-to-all | bytes 4358144 | tf_op jit(solution)/shard_map/all_to_all | solution.py:53
  171.7 1.9 collective-permute-start.11
  173.6 5.2 %collective-permute-start.13 = (bf16[592,128]{1,0:T(8,128)(2,1)S(1)}, bf16[592,128]{1,0:T(8,128)(2,1)S(1)}, u32[]{:S(2)}, u32[]{:S(2)}) collective-permute-start(bf16[592,128]{1,0:T(8,128)(2,1)S(1)} %get-tuple-element.64), channel_id=1, source_target_pairs={{0,3},{1,0},{2,1},{3,2},{4,7},{5,4},{6,5},{7,6},{8,11},{9,8},{10,9... | collective-permute-start | bytes 454664 | tf_op jit(solution)/shard_map/ppermute | solution.py:41
  178.8 1.7 collective-permute-done.11.passing_ref.after_ref
  180.5 1.9 collective-permute-start.12
  182.4 1.9 collective-permute-done.13.before_ref
  184.4 8.1 %collective-permute-done.12.across_ref = bf16[592,128]{1,0:T(8,128)(2,1)S(1)} collective-permute-done((bf16[592,128]{1,0:T(8,128)(2,1)S(1)}, bf16[592,128]{1,0:T(8,128)(2,1)S(1)}, u32[]{:S(2)}, u32[]{:S(2)}) %collective-permute-start.12) | collective-permute-done | bytes 151584 | tf_op jit(solution)/shard_map/ppermute | solution.py:41
  192.5 3.9 %collective-permute-start.14 = (bf16[416,128]{1,0:T(8,128)(2,1)S(1)}, bf16[416,128]{1,0:T(8,128)(2,1)S(1)}, u32[]{:S(2)}, u32[]{:S(2)}) collective-permute-start(bf16[416,128]{1,0:T(8,128)(2,1)S(1)} %get-tuple-element.66.sent_ref), channel_id=1, source_target_pairs={{0,16},{1,17},{2,18},{3,19},{4,20},{5,21},{6,22},{7,23},{8,24},{9,... | collective-permute-start | bytes 319496 | tf_op jit(solution)/shard_map/ppermute | solution.py:32
  196.5 0.9 collective-permute-done.14.back_ref
  (35 shorter events, 4.5 us)
Async XLA Ops:
  0.6 18.3 %copy-start.5 = (s32[16]{0:T(128)S(1)}, s32[16]{0:T(128)}, u32[]{:S(2)}) copy-start(s32[16]{0:T(128)} %constant.126.clone.1) | copy-start | bytes 196
  0.6 12.8 %copy-start.4 = (s32[1,1,8]{2,1,0:T(1,128)S(1)}, s32[1,1,8]{2,1,0:T(1,128)}, u32[]{:S(2)}) copy-start(s32[1,1,8]{2,1,0:T(1,128)} %refs_1_.1) | copy-start | bytes 100
  0.7 12.8 %copy-start.3 = (s32[1,1,8]{2,1,0:T(1,128)S(1)}, s32[1,1,8]{2,1,0:T(1,128)}, u32[]{:S(2)}) copy-start(s32[1,1,8]{2,1,0:T(1,128)} %refs_0_.1) | copy-start | bytes 100
  3.8 11.6 %collective-permute-start = (bf16[2560,256]{1,0:T(8,128)(2,1)}, bf16[2560,256]{1,0:T(8,128)(2,1)S(1)}, u32[]{:S(2)}, u32[]{:S(2)}) collective-permute-start(bf16[2560,256]{1,0:T(8,128)(2,1)} %shard_map.120.own_ref.facts_ref), channel_id=1, source_target_pairs={{0,16},{1,17},{2,18},{3,19},{4,20},{5,21},{6,22},{7,23},{8,24},{9,... | collective-permute-start | bytes 3932168 | tf_op jit(solution)/shard_map/ppermute | solution.py:32
  15.5 9.7 %collective-permute-start.1 = (bf16[512,128]{1,0:T(8,128)(2,1)S(1)}, bf16[512,128]{1,0:T(8,128)(2,1)S(1)}, u32[]{:S(2)}, u32[]{:S(2)}) collective-permute-start(bf16[512,128]{1,0:T(8,128)(2,1)S(1)} %pad_maximum_fusion.refs_0_.both_ref), channel_id=1, source_target_pairs={{0,128},{1,129},{2,130},{3,131},{4,132},{5,133},{6,134},{7,135},{8... | collective-permute-start | bytes 393224 | tf_op jit(solution)/shard_map/ppermute | solution.py:41
  19.2 14.3 %collective-permute-start.3 = (bf16[512,128]{1,0:T(8,128)(2,1)S(1)}, bf16[512,128]{1,0:T(8,128)(2,1)S(1)}, u32[]{:S(2)}, u32[]{:S(2)}) collective-permute-start(bf16[512,128]{1,0:T(8,128)(2,1)S(1)} %pad_maximum_fusion.refs_0_.both_ref), channel_id=1, source_target_pairs={{0,384},{1,385},{2,386},{3,387},{4,388},{5,389},{6,390},{7,391},{8... | collective-permute-start | bytes 393224 | tf_op jit(solution)/shard_map/ppermute | solution.py:41
  25.2 12.9 %collective-permute-start.2 = (bf16[512,128]{1,0:T(8,128)(2,1)S(1)}, bf16[512,128]{1,0:T(8,128)(2,1)S(1)}, u32[]{:S(2)}, u32[]{:S(2)}) collective-permute-start(bf16[512,128]{1,0:T(8,128)(2,1)S(1)} %collective-permute-done.1.refs_1_), channel_id=1, source_target_pairs={{0,128},{1,129},{2,130},{3,131},{4,132},{5,133},{6,134},{7,135},{8... | collective-permute-start | bytes 393224 | tf_op jit(solution)/shard_map/ppermute | solution.py:41
  38.3 20.1 %copy-start = (bf16[2560,256]{1,0:T(8,128)(2,1)S(1)}, bf16[2560,256]{1,0:T(8,128)(2,1)}, u32[]{:S(2)}) copy-start(bf16[2560,256]{1,0:T(8,128)(2,1)} %shard_map.120.own_ref.facts_ref) | copy-start | bytes 3932164
  79.4 25.4 %copy-start.1 = (bf16[128,128]{1,0:T(8,128)(2,1)S(1)}, bf16[128,128]{1,0:T(8,128)(2,1)}, u32[]{:S(2)}) copy-start(bf16[128,128]{1,0:T(8,128)(2,1)} %weight_ref.3) | copy-start | bytes 98308
  79.4 25.4 %copy-start.2 = (f32[128]{0:T(128)S(1)}, f32[128]{0:T(128)}, u32[]{:S(2)}) copy-start(f32[128]{0:T(128)} %param.11) | copy-start | bytes 1540
  79.6 10.4 %collective-permute-start.4 = (bf16[512,128]{1,0:T(8,128)(2,1)S(1)}, bf16[512,128]{1,0:T(8,128)(2,1)S(1)}, u32[]{:S(2)}, u32[]{:S(2)}) collective-permute-start(bf16[512,128]{1,0:T(8,128)(2,1)S(1)} %get-tuple-element.47), channel_id=1, source_target_pairs={{0,1},{1,2},{2,3},{3,0},{4,5},{5,6},{6,7},{7,4},{8,9},{9,10},{10,1... | collective-permute-start | bytes 393224 | tf_op jit(solution)/shard_map/ppermute | solution.py:41
  88.0 8.0 %collective-permute-start.6 = (bf16[512,128]{1,0:T(8,128)(2,1)S(1)}, bf16[512,128]{1,0:T(8,128)(2,1)S(1)}, u32[]{:S(2)}, u32[]{:S(2)}) collective-permute-start(bf16[512,128]{1,0:T(8,128)(2,1)S(1)} %get-tuple-element.48), channel_id=1, source_target_pairs={{0,3},{1,0},{2,1},{3,2},{4,7},{5,4},{6,5},{7,6},{8,11},{9,8},{10,9... | collective-permute-start | bytes 393224 | tf_op jit(solution)/shard_map/ppermute | solution.py:41
  90.1 9.4 %collective-permute-start.5 = (bf16[512,128]{1,0:T(8,128)(2,1)S(1)}, bf16[512,128]{1,0:T(8,128)(2,1)S(1)}, u32[]{:S(2)}, u32[]{:S(2)}) collective-permute-start(bf16[512,128]{1,0:T(8,128)(2,1)S(1)} %shard_map.124), channel_id=1, source_target_pairs={{0,1},{1,2},{2,3},{3,0},{4,5},{5,6},{6,7},{7,4},{8,9},{9,10},{10,1... | collective-permute-start | bytes 393224 | tf_op jit(solution)/shard_map/ppermute | solution.py:41
  99.6 5.2 %collective-permute-start.7 = (bf16[512,128]{1,0:T(8,128)(2,1)S(1)}, bf16[512,128]{1,0:T(8,128)(2,1)S(1)}, u32[]{:S(2)}, u32[]{:S(2)}) collective-permute-start(bf16[512,128]{1,0:T(8,128)(2,1)S(1)} %get-tuple-element.50), channel_id=1, source_target_pairs={{0,16},{1,17},{2,18},{3,19},{4,20},{5,21},{6,22},{7,23},{8,24},{9,... | collective-permute-start | bytes 393224 | tf_op jit(solution)/shard_map/ppermute | solution.py:32
  105.7 14.1 %collective-permute-start.8 = (bf16[592,128]{1,0:T(8,128)(2,1)S(1)}, bf16[592,128]{1,0:T(8,128)(2,1)S(1)}, u32[]{:S(2)}, u32[]{:S(2)}) collective-permute-start(bf16[592,128]{1,0:T(8,128)(2,1)S(1)} %get-tuple-element.53.refs_0_.both_ref), channel_id=1, source_target_pairs={{0,128},{1,129},{2,130},{3,131},{4,132},{5,133},{6,134},{7,135},{8... | collective-permute-start | bytes 454664 | tf_op jit(solution)/shard_map/ppermute | solution.py:41
  113.2 12.8 %collective-permute-start.10 = (bf16[592,128]{1,0:T(8,128)(2,1)S(1)}, bf16[592,128]{1,0:T(8,128)(2,1)S(1)}, u32[]{:S(2)}, u32[]{:S(2)}) collective-permute-start(bf16[592,128]{1,0:T(8,128)(2,1)S(1)} %get-tuple-element.53.refs_0_.both_ref), channel_id=1, source_target_pairs={{0,384},{1,385},{2,386},{3,387},{4,388},{5,389},{6,390},{7,391},{8... | collective-permute-start | bytes 454664 | tf_op jit(solution)/shard_map/ppermute | solution.py:41
  119.8 13.0 %collective-permute-start.9 = (bf16[592,128]{1,0:T(8,128)(2,1)S(1)}, bf16[592,128]{1,0:T(8,128)(2,1)S(1)}, u32[]{:S(2)}, u32[]{:S(2)}) collective-permute-start(bf16[592,128]{1,0:T(8,128)(2,1)S(1)} %collective-permute-done.8.refs_1_), channel_id=1, source_target_pairs={{0,128},{1,129},{2,130},{3,131},{4,132},{5,133},{6,134},{7,135},{8... | collective-permute-start | bytes 454664 | tf_op jit(solution)/shard_map/ppermute | solution.py:41
  171.7 8.8 %collective-permute-start.11 = (bf16[592,128]{1,0:T(8,128)(2,1)S(1)}, bf16[592,128]{1,0:T(8,128)(2,1)S(1)}, u32[]{:S(2)}, u32[]{:S(2)}) collective-permute-start(bf16[592,128]{1,0:T(8,128)(2,1)S(1)} %get-tuple-element.63), channel_id=1, source_target_pairs={{0,1},{1,2},{2,3},{3,0},{4,5},{5,6},{6,7},{7,4},{8,9},{9,10},{10,1... | collective-permute-start | bytes 454664 | tf_op jit(solution)/shard_map/ppermute | solution.py:41
  173.6 10.7 %collective-permute-start.13 = (bf16[592,128]{1,0:T(8,128)(2,1)S(1)}, bf16[592,128]{1,0:T(8,128)(2,1)S(1)}, u32[]{:S(2)}, u32[]{:S(2)}) collective-permute-start(bf16[592,128]{1,0:T(8,128)(2,1)S(1)} %get-tuple-element.64), channel_id=1, source_target_pairs={{0,3},{1,0},{2,1},{3,2},{4,7},{5,4},{6,5},{7,6},{8,11},{9,8},{10,9... | collective-permute-start | bytes 454664 | tf_op jit(solution)/shard_map/ppermute | solution.py:41
  180.5 12.0 %collective-permute-start.12 = (bf16[592,128]{1,0:T(8,128)(2,1)S(1)}, bf16[592,128]{1,0:T(8,128)(2,1)S(1)}, u32[]{:S(2)}, u32[]{:S(2)}) collective-permute-start(bf16[592,128]{1,0:T(8,128)(2,1)S(1)} %shard_map.130), channel_id=1, source_target_pairs={{0,1},{1,2},{2,3},{3,0},{4,5},{5,6},{6,7},{7,4},{8,9},{9,10},{10,1... | collective-permute-start | bytes 454664 | tf_op jit(solution)/shard_map/ppermute | solution.py:41
  192.5 4.8 %collective-permute-start.14 = (bf16[416,128]{1,0:T(8,128)(2,1)S(1)}, bf16[416,128]{1,0:T(8,128)(2,1)S(1)}, u32[]{:S(2)}, u32[]{:S(2)}) collective-permute-start(bf16[416,128]{1,0:T(8,128)(2,1)S(1)} %get-tuple-element.66.sent_ref), channel_id=1, source_target_pairs={{0,16},{1,17},{2,18},{3,19},{4,20},{5,21},{6,22},{7,23},{8,24},{9,... | collective-permute-start | bytes 319496 | tf_op jit(solution)/shard_map/ppermute | solution.py:32
